TPU v7x, 32 devices: a whole 2x2x4 slice. The times are simulated.
32 devices in a mesh: lon: 4 (over x, core), lat: 4 (over z), dp: 2 (over y).
Axes of the slice: x: 2, y: 2, z: 4, core: 2. Of those that a mesh axis runs over, the one named last changes fastest.
Arguments:
- tokens: bfloat16 [2, 2, 32, 64, 1024], P('dp', None, 'lat', 'lon'), may hold values from -6 to 6
- norm_gain: float32 [1024], replicated, may hold values from 0.1 to 1.9
- w_qkv: bfloat16 [1024, 3072], replicated, may hold values from -8 to 8
- w_out: bfloat16 [1024, 1024], replicated, may hold values from -0.1875 to 0.1875
- obs_vectors: bfloat16 [2048, 1024], P(('lon', 'lat', 'dp')), may hold values from -6 to 6
- obs_lat: int32 [2048, 1], P(('lon', 'lat', 'dp')), may hold values from 0 to 3; in each aligned block of 64 rows (0 to 63, 64 to 127, ...) at most 24 rows name the same one
- obs_cell: int32 [2048], P(('lon', 'lat', 'dp')), may hold values from 0 to 255
- obs_count: int32 [32], P(('lon', 'lat', 'dp')), may hold values from 1 to 64, 1536 in all
- shift_offsets: int32 [2, 2], P('dp'), may hold values from 1 to 7, as said below
- cotangent: bfloat16 [2, 2, 32, 64, 1024], P('dp', None, 'lat', 'lon'), may hold values from -0.09375 to 0.09375
Outputs:
- block_out: bfloat16 [2, 2, 32, 64, 1024], P('dp', None, 'lat', 'lon')
- gradient: float32 [1024, 1024], P('lon', ('lat', 'dp'))
Inputs may be any that keep to these rules, and one draw needn't show every extreme that they name: `obs_lat`: among the 64 rows of one device at most 24 name the same latitude index; some device has exactly 24 for some index. `obs_count`: some device has exactly 64 live rows. `shift_offsets`: each column takes the value 8 - 1 for some sample.
All inputs are finite; a program needn't handle non-finite values.
Results may differ from a plain program's by a relative error of at most 0.0086.
Values may be sent and summed in bfloat16 or wider, within the bound.
No kernel may reach another device: no remote copies, remote signals or barrier semaphores. Data moves between devices by JAX's collectives and lax.ppermute only.
A program may use at most 64 MiB of HBM per device.

v0:
```python
import jax
import jax.numpy as jnp
from jax import lax
from jax.sharding import PartitionSpec as P

HEADS = 16
WIN = 8


def from_behind(array, axis, by):
    devices = lax.axis_size(axis)
    pairs = [(i, i + by) for i in range(devices) if 0 <= i + by < devices]
    return lax.ppermute(array, axis, pairs)


def shifted(array, axis, by):
    devices = lax.axis_size(axis)
    return lax.ppermute(array, axis, [(i, (i + by) % devices) for i in range(devices)])


def to_windows(field_in):
    levels_n, rows_n, cols_n, feat_width = field_in.shape
    blocks = field_in.reshape(levels_n, rows_n // WIN, WIN, cols_n // WIN, WIN, feat_width)
    return blocks.transpose(1, 3, 0, 2, 4, 5).reshape(-1, levels_n * WIN * WIN, feat_width)


def from_windows(windows, levels_n, rows_n, cols_n):
    feat_width = windows.shape[-1]
    blocks = windows.reshape(rows_n // WIN, cols_n // WIN, levels_n, WIN, WIN, feat_width)
    return blocks.transpose(2, 0, 3, 1, 4, 5).reshape(levels_n, rows_n, cols_n, feat_width)


def window_block(win_tokens, win_valid, norm_gain, w_qkv, w_out):
    n_win, n_tok, d_model = win_tokens.shape
    head_dim = d_model // HEADS
    as_float = win_tokens.astype(jnp.float32)
    average = jnp.mean(as_float, axis=-1, keepdims=True)
    centred = as_float - average
    variance = jnp.mean(centred * centred, axis=-1, keepdims=True)
    normed = (centred * lax.rsqrt(variance + 1e-05) * norm_gain).astype(jnp.bfloat16)
    projected = jnp.dot(
        normed.reshape(-1, d_model), w_qkv, preferred_element_type=jnp.float32
    ).astype(jnp.bfloat16)
    projected = projected.reshape(n_win, n_tok, 3, HEADS, head_dim)
    queries = projected[:, :, 0]
    key_rows = projected[:, :, 1]
    values = projected[:, :, 2]
    scores = jnp.einsum(
        "wqhd,wkhd->whqk", queries, key_rows, preferred_element_type=jnp.float32
    ) * head_dim ** (-0.5)
    scores = jnp.where(win_valid[:, None, None, :], scores, -1e30)
    highest = jnp.max(scores, axis=-1, keepdims=True)
    powers = jnp.exp(scores - highest)
    weights = (powers / jnp.sum(powers, axis=-1, keepdims=True)).astype(jnp.bfloat16)
    context = jnp.einsum(
        "whqk,wkhd->wqhd", weights, values, preferred_element_type=jnp.float32
    ).astype(jnp.bfloat16)
    context = context.reshape(n_win, n_tok, d_model)
    result = jnp.dot(context.reshape(-1, d_model), w_out, preferred_element_type=jnp.float32)
    return ((as_float + result.reshape(n_win, n_tok, d_model)).astype(jnp.bfloat16), context)


def on_device(
    tokens,
    norm_gain,
    w_qkv,
    w_out,
    obs_vectors,
    obs_lat,
    obs_cell,
    obs_count,
    shift_offsets,
    cotangent,
):
    n_batch, levels, lat_dev, lon_dev, d_model = tokens.shape
    n_lat = lax.axis_size("lat")
    obs_rows = obs_vectors.shape[0]
    capacity = obs_rows * 3 // (2 * n_lat)
    n_slots = n_lat * capacity
    destination = obs_lat[:, 0]
    one_hot = (destination[:, None] == jnp.arange(n_lat, dtype=jnp.int32)[None, :]).astype(
        jnp.int32
    )
    earlier = jnp.cumsum(one_hot, axis=0) - one_hot
    rank_in = jnp.sum(earlier * one_hot, axis=1)
    slot_of = destination * capacity + rank_in
    is_live = jnp.arange(obs_rows, dtype=jnp.int32) < obs_count[0]
    cell_tag = jnp.where(is_live, obs_cell, -1)
    chooser = slot_of[None, :] == jnp.arange(n_slots, dtype=jnp.int32)[:, None]
    sent_rows = (
        jnp.dot(chooser.astype(jnp.bfloat16), obs_vectors, preferred_element_type=jnp.float32)
        .astype(jnp.bfloat16)
        .reshape(n_lat, capacity, d_model)
    )
    sent_tags = (jnp.sum(chooser.astype(jnp.int32) * (cell_tag[None, :] + 1), axis=1) - 1).reshape(
        n_lat, capacity
    )
    got_rows, got_tags = (
        lax.all_to_all(sent_rows, "lat", split_axis=0, concat_axis=0, tiled=True),
        lax.all_to_all(sent_tags, "lat", split_axis=0, concat_axis=0, tiled=True),
    )
    flat_tokens = tokens.reshape(-1, d_model)
    placer = (
        got_tags.reshape(-1)[None, :] == jnp.arange(flat_tokens.shape[0], dtype=jnp.int32)[:, None]
    ).astype(jnp.bfloat16)
    added = jnp.dot(placer, got_rows.reshape(-1, d_model), preferred_element_type=jnp.float32)
    enriched = (flat_tokens.astype(jnp.float32) + added).astype(jnp.bfloat16).reshape(tokens.shape)
    margin = WIN - 1
    north_part = from_behind(enriched[:, :, :margin], "lat", -1)
    heightened = jnp.concatenate([enriched, north_part], axis=2)
    east_cols = shifted(heightened[:, :, :, :margin], "lon", -1)
    extended = jnp.concatenate([heightened, east_cols], axis=3)
    lat_shift = shift_offsets[0, 0]
    lon_shift = shift_offsets[0, 1]
    anchor = jnp.zeros((), jnp.int32)
    region = lax.dynamic_slice(
        extended, (anchor, anchor, lat_shift, lon_shift, anchor), tokens.shape
    )[0]
    source_rows = lax.axis_index("lat") * lat_dev + lat_shift + jnp.arange(lat_dev, dtype=jnp.int32)
    is_valid = jnp.broadcast_to(
        (source_rows < lat_dev * n_lat)[None, :, None, None], (levels, lat_dev, lon_dev, 1)
    )
    mixed, context = window_block(
        to_windows(region), to_windows(is_valid)[..., 0], norm_gain, w_qkv, w_out
    )
    block_out = from_windows(mixed, levels, lat_dev, lon_dev)[None]
    cot_rows = to_windows(cotangent[0]).reshape(-1, d_model)
    context_rows = context.reshape(-1, d_model)
    contract = (((0,), (0,)), ((), ()))
    partial_rows = lax.psum_scatter(
        lax.dot_general(cot_rows, context_rows, contract, preferred_element_type=jnp.float32),
        "lon",
        scatter_dimension=0,
        tiled=True,
    )
    gradient = lax.psum_scatter(partial_rows, ("lat", "dp"), scatter_dimension=1, tiled=True)
    return (block_out, gradient)


def solution(mesh):
    placed = (
        P("dp", None, "lat", "lon", None),
        P(),
        P(),
        P(),
        P(("lon", "lat", "dp"), None),
        P(("lon", "lat", "dp"), None),
        P(("lon", "lat", "dp")),
        P(("lon", "lat", "dp")),
        P("dp", None),
        P("dp", None, "lat", "lon", None),
    )
    return jax.shard_map(
        on_device,
        mesh=mesh,
        in_specs=placed,
        out_specs=(P("dp", None, "lat", "lon", None), P("lon", ("lat", "dp"))),
        check_vma=False,
    )
```

profile of v0, /device:TPU:0, one launch (start us, length us, event | category | flops | bytes accessed | tf_op | source)
XLA Modules:
  0.0 211.7 jit_solution(11889364723042357289)
XLA Ops:
  11.1 6.3 %all-to-all-start = ((s32[4,1,24]{2,1,0:T(1,128)}), s32[4,1,24]{2,1,0:T(1,128)S(1)}, u32[]{:S(2)}, u32[]{:S(2)}) async-start(s32[4,1,24]{2,1,0:T(1,128)} %bitcast.3), calls=%async_computation | async-start | bytes 4096 | tf_op jit(solution)/shard_map/all_to_all | solution.py:100
  17.4 1.9 convolution_convert_fusion.2
  19.3 3.6 %all-to-all-done = s32[4,1,24]{2,1,0:T(1,128)S(1)} async-done(((s32[4,1,24]{2,1,0:T(1,128)}), s32[4,1,24]{2,1,0:T(1,128)S(1)}, u32[]{:S(2)}, u32[]{:S(2)}) %all-to-all-start) | async-done | bytes 416 | tf_op jit(solution)/shard_map/all_to_all | solution.py:100
  22.9 3.4 %all-to-all-start.1 = ((bf16[4,24,1024]{2,1,0:T(8,128)(2,1)}), bf16[4,24,1024]{2,1,0:T(8,128)(2,1)S(1)}, u32[]{:S(2)}, u32[]{:S(2)}) async-start(bf16[4,24,1024]{2,1,0:T(8,128)(2,1)} %bitcast.4), calls=%async_computation.1 | async-start | bytes 393216 | tf_op jit(solution)/shard_map/all_to_all | solution.py:99
  27.6 4.9 %all-to-all-done.1 = bf16[4,24,1024]{2,1,0:T(8,128)(2,1)S(1)} async-done(((bf16[4,24,1024]{2,1,0:T(8,128)(2,1)}), bf16[4,24,1024]{2,1,0:T(8,128)(2,1)S(1)}, u32[]{:S(2)}, u32[]{:S(2)}) %all-to-all-start.1) | async-done | bytes 196640 | tf_op jit(solution)/shard_map/all_to_all | solution.py:99
  32.5 1.3 fusion.7
  35.2 10.3 %collective-permute-done = bf16[1,2,7,16,1024]{4,3,2,1,0:T(8,128)(2,1)S(1)} collective-permute-done((bf16[1,2,7,16,1024]{4,3,2,1,0:T(8,128)(2,1)S(1)}, bf16[1,2,7,16,1024]{4,3,2,1,0:T(8,128)(2,1)S(1)}, u32[]{:S(2)}, u32[]{:S(2)}) %collective-permute-start) | collective-permute-done | bytes 458784 | tf_op jit(solution)/shard_map/ppermute | solution.py:13
  50.2 1.9 copy.63
  53.4 1.6 bitcast_reduce_fusion
  55.1 1.7 fusion.15
  57.0 1.6 fusion.22
  58.9 5.7 %convolution_convert_fusion = bf16[256,3072]{1,0:T(8,128)(2,1)} fusion(bf16[256,1024]{1,0:T(8,128)(2,1)S(1)} %fusion.13, bf16[1024,3072]{1,0:T(8,128)(2,1)} %param.12), kind=kOutput, calls=%fused_computation.1 | convolution fusion | flops 1611399168 | bytes 8388608 | tf_op jit(solution)/shard_map/dot_general | solution.py:41
  64.6 4.9 %reshape.123 = bf16[2,128,3,16,64]{4,3,2,1,0:T(8,128)(2,1)} reshape(bf16[256,3072]{1,0:T(8,128)(2,1)} %convolution_convert_fusion) | data formatting | bytes 3145728 | tf_op jit(solution)/shard_map/reshape | solution.py:44
  69.5 3.8 %fusion.47 = (bf16[2,128,1,16,64]{4,3,2,1,0:T(8,128)(2,1)}, bf16[2,128,1,16,64]{4,3,2,1,0:T(8,128)(2,1)}, bf16[2,128,1,16,64]{4,3,2,1,0:T(8,128)(2,1)}) fusion(bf16[2,128,3,16,64]{4,3,2,1,0:T(8,128)(2,1)} %reshape.123), kind=kLoop, calls=%fused_computation.58 | loop fusion | bytes 3145728 | tf_op jit(solution)/shard_map/slice | solution.py:47
  73.3 2.8 %copy.70 = bf16[2,128,1,16,64]{1,4,3,0,2:T(8,128)(2,1)} copy(bf16[2,128,1,16,64]{4,3,2,1,0:T(8,128)(2,1)} %get-tuple-element.13) | data formatting | bytes 1048576
  76.1 2.8 %copy.71 = bf16[2,128,1,16,64]{1,4,3,0,2:T(8,128)(2,1)} copy(bf16[2,128,1,16,64]{4,3,2,1,0:T(8,128)(2,1)} %get-tuple-element.14) | data formatting | bytes 1048576
  78.8 2.8 %copy.69 = bf16[2,128,1,16,64]{1,4,3,0,2:T(8,128)(2,1)} copy(bf16[2,128,1,16,64]{4,3,2,1,0:T(8,128)(2,1)} %get-tuple-element.12) | data formatting | bytes 1048576
  81.6 3.4 %fusion.49 = (f32[2,16,128]{2,1,0:T(8,128)S(1)}, f32[2,16,128,128]{2,3,1,0:T(8,128)}) fusion(pred[128]{0:T(512)(128)(4,1)S(1)} %transpose.44, bf16[2,128,1,16,64]{1,4,3,0,2:T(8,128)(2,1)} %copy.71, bf16[2,128,1,16,64]{1,4,3,0,2:T(8,128)(2,1)} %copy.70), kind=kOutput, calls=%fused_computation.60 | convolution fusion | flops 69206144 | bytes 3162240 | tf_op jit(solution)/shard_map/sub | solution.py:53
  85.0 2.2 %convolution_convert_fusion.1 = bf16[2,16,64,128]{3,2,1,0:T(8,128)(2,1)S(1)} fusion(f32[2,16,128,128]{2,3,1,0:T(8,128)} %get-tuple-element.18, f32[2,16,128]{2,1,0:T(8,128)S(1)} %get-tuple-element.17, bf16[2,128,1,16,64]{1,4,3,0,2:T(8,128)(2,1)} %copy.69), kind=kOutput, calls=%fused_computation.15 | convolution fusion | flops 68419584 | bytes 3162112 | tf_op jit(solution)/shard_map/whqk,wkhd->wqhd/dot_general | solution.py:55
  88.6 2.6 %convolution_bitcast_fusion = f32[1024,1024]{0,1:T(8,128)} fusion(bf16[256,1024]{1,0:T(8,128)(2,1)S(1)} %bitcast.107, bf16[128,8,2,128]{3,2,1,0:T(2,128)(2,1)S(1)} %bitcast.108), kind=kOutput, calls=%fused_computation.2 | convolution fusion | flops 536870912 | bytes 5242880 | tf_op jit(solution)/shard_map/dot_general | solution.py:131
  91.3 43.9 %reduce-scatter.3.cloned.1.call-done = f32[256,1024]{0,1:T(8,128)} async-done(((f32[1024,1024]{0,1:T(8,128)}), f32[256,1024]{0,1:T(8,128)}) %reduce-scatter.3.cloned.1.call-update) | async-done | bytes 1048592 | tf_op jit(solution)/shard_map/reduce_scatter | solution.py:130
  135.3 1.8 fusion.8
  137.9 65.3 %reduce-scatter.5.cloned.1.call-done = f32[256,128]{0,1:T(8,128)} async-done(((f32[256,1024]{0,1:T(8,128)}), f32[256,128]{0,1:T(8,128)}) %reduce-scatter.5.cloned.1.call-update) | async-done | bytes 131088 | tf_op jit(solution)/shard_map/reduce_scatter | solution.py:136
  203.2 1.7 copy.64
  (41 shorter events, 10.2 us)
Async XLA Ops:
  7.2 128.1 %copy-start = (bf16[1024,1024]{1,0:T(8,128)(2,1)S(1)}, bf16[1024,1024]{1,0:T(8,128)(2,1)}, u32[]{:S(2)}) copy-start(bf16[1024,1024]{1,0:T(8,128)(2,1)} %param.13) | copy-start | bytes 6291460
  11.1 11.8 %all-to-all-start = ((s32[4,1,24]{2,1,0:T(1,128)}), s32[4,1,24]{2,1,0:T(1,128)S(1)}, u32[]{:S(2)}, u32[]{:S(2)}) async-start(s32[4,1,24]{2,1,0:T(1,128)} %bitcast.3), calls=%async_computation | async-start | bytes 4096 | tf_op jit(solution)/shard_map/all_to_all | solution.py:100
  19.3 26.9 %copy-start.4 = (s32[1,2]{1,0:T(1,128)S(1)}, s32[1,2]{1,0:T(1,128)}, u32[]{:S(2)}) copy-start(s32[1,2]{1,0:T(1,128)} %param.18) | copy-start | bytes 28
  22.9 9.6 %all-to-all-start.1 = ((bf16[4,24,1024]{2,1,0:T(8,128)(2,1)}), bf16[4,24,1024]{2,1,0:T(8,128)(2,1)S(1)}, u32[]{:S(2)}, u32[]{:S(2)}) async-start(bf16[4,24,1024]{2,1,0:T(8,128)(2,1)} %bitcast.4), calls=%async_computation.1 | async-start | bytes 393216 | tf_op jit(solution)/shard_map/all_to_all | solution.py:99
  26.3 108.9 %reduce-scatter.3.cloned.1.call-start = ((), (), s32[]{:S(2)}) async-start(), calls=%async_computation.4 | async-start | bytes 5242880 | tf_op jit(solution)/shard_map/reduce_scatter | solution.py:130
  33.9 11.6 %collective-permute-start = (bf16[1,2,7,16,1024]{4,3,2,1,0:T(8,128)(2,1)S(1)}, bf16[1,2,7,16,1024]{4,3,2,1,0:T(8,128)(2,1)S(1)}, u32[]{:S(2)}, u32[]{:S(2)}) collective-permute-start(bf16[1,2,7,16,1024]{4,3,2,1,0:T(8,128)(2,1)S(1)} %slice.28), channel_id=1, source_target_pairs={{2,0},{4,2},{6,4},{3,1},{5,3},{7,5},{10,8},{12,10},{14,12},{11,9},... | collective-permute-start | bytes 1376264 | tf_op jit(solution)/shard_map/ppermute | solution.py:13
  46.2 7.2 %collective-permute-start.1 = (bf16[1,2,15,7,1024]{4,3,2,1,0:T(8,128)(2,1)}, bf16[1,2,15,7,1024]{4,3,2,1,0:T(8,128)(2,1)}, u32[]{:S(2)}, u32[]{:S(2)}) collective-permute-start(bf16[1,2,15,7,1024]{4,3,2,1,0:T(8,128)(2,1)} %pad_maximum_fusion), channel_id=1, source_target_pairs={{0,24},{8,0},{16,8},{24,16},{1,25},{9,1},{17,9},{25,17},{2,26},{10... | collective-permute-start | bytes 1290248 | tf_op jit(solution)/shard_map/ppermute | solution.py:18
  57.0 1.7 copy-start.3
  85.0 3.6 %copy-start.1 = (bf16[1,2,2,8,8,1024]{5,4,3,2,1,0:T(8,128)(2,1)S(1)}, bf16[1,2,2,8,8,1024]{5,4,3,2,1,0:T(8,128)(2,1)}, u32[]{:S(2)}) copy-start(bf16[1,2,2,8,8,1024]{5,4,3,2,1,0:T(8,128)(2,1)} %copy.63) | copy-start | bytes 1572868
  87.3 0.8 copy-start.2
  91.3 111.9 %reduce-scatter.5.cloned.1.call-start = ((), (), s32[]{:S(2)}) async-start(), calls=%async_computation.5 | async-start | bytes 1179648 | tf_op jit(solution)/shard_map/reduce_scatter | solution.py:136
Sparse Core Ops, SparseCore 0:
  91.4 43.7 reduce-scatter.2
  139.0 64.1 reduce-scatter.4
where the time goes:
time: 213 us; the launch traced here: 212 us
  waiting for transfers between devices  128 us (60%)
  local copies, waits for them, and re-layouts  25 us (12%)
  between operations  19.3 us (9%)
  matrix products  19 us (9%)
  starting transfers between devices  11.1 us (5%)
  other arithmetic  9.26 us (4%)
    reduce_scatter x1, waiting for transfers between devices, on_device(): lax.psum_scatter(partial_rows, ('lat', 'dp'), scatter_dimension=1, tiled=...  65.3 us
    reduce_scatter x1, waiting for transfers between devices, on_device(): lax.psum_scatter(lax.dot_general(cot_rows, context_rows, contract, prefer...  43.9 us
    unnamed x14, local copies, waits for them, and re-layouts  10.8 us
    ppermute x1, waiting for transfers between devices, from_behind(): return lax.ppermute(array, axis, pairs)  10.3 us
    all_to_all x1, starting transfers between devices, on_device(): lax.all_to_all(sent_tags, 'lat', split_axis=0, concat_axis=0, tiled=True)  6.32 us
    dot_general x1, matrix products, window_block(): jnp.dot(normed.reshape(-1, d_model), w_qkv, preferred_element_type=jnp.fl...  5.73 us
    all_to_all x1, waiting for transfers between devices, on_device(): lax.all_to_all(sent_rows, 'lat', split_axis=0, concat_axis=0, tiled=True)  4.9 us
    reshape x1, local copies, waits for them, and re-layouts, window_block(): projected = projected.reshape(n_win, n_tok, 3, HEADS, head_dim)  4.86 us
  transfers between devices with their start and end apart: 6, of which 5 were waited for; matrix products, arithmetic and copies ran while one was open for 4% of the time, Pallas kernels for 0%

commit v1 on v0

--- a/solution.py
+++ b/solution.py
@@ -1,10 +1,18 @@
+import functools
+
 import jax
 import jax.numpy as jnp
 from jax import lax
+from jax.experimental import pallas as pl
+from jax.experimental.pallas import tpu as pltpu
 from jax.sharding import PartitionSpec as P
 
 HEADS = 16
 WIN = 8
+BF16 = jnp.bfloat16
+F32 = jnp.float32
+LANES = 128
+VMEM_LIMIT = 48 * 1024 * 1024
 
 
 def from_behind(array, axis, by):
@@ -18,6 +26,11 @@
     return lax.ppermute(array, axis, [(i, (i + by) % devices) for i in range(devices)])
 
 
+def swapped(array, axis, bit):
+    devices = lax.axis_size(axis)
+    return lax.ppermute(array, axis, [(i, i ^ bit) for i in range(devices)])
+
+
 def to_windows(field_in):
     levels_n, rows_n, cols_n, feat_width = field_in.shape
     blocks = field_in.reshape(levels_n, rows_n // WIN, WIN, cols_n // WIN, WIN, feat_width)
@@ -33,44 +46,35 @@
 def window_block(win_tokens, win_valid, norm_gain, w_qkv, w_out):
     n_win, n_tok, d_model = win_tokens.shape
     head_dim = d_model // HEADS
-    as_float = win_tokens.astype(jnp.float32)
+    as_float = win_tokens.astype(F32)
     average = jnp.mean(as_float, axis=-1, keepdims=True)
     centred = as_float - average
     variance = jnp.mean(centred * centred, axis=-1, keepdims=True)
-    normed = (centred * lax.rsqrt(variance + 1e-05) * norm_gain).astype(jnp.bfloat16)
+    normed = (centred * lax.rsqrt(variance + 1e-05) * norm_gain).astype(BF16)
     projected = jnp.dot(
-        normed.reshape(-1, d_model), w_qkv, preferred_element_type=jnp.float32
-    ).astype(jnp.bfloat16)
+        normed.reshape(-1, d_model), w_qkv, preferred_element_type=F32
+    ).astype(BF16)
     projected = projected.reshape(n_win, n_tok, 3, HEADS, head_dim)
     queries = projected[:, :, 0]
     key_rows = projected[:, :, 1]
     values = projected[:, :, 2]
     scores = jnp.einsum(
-        "wqhd,wkhd->whqk", queries, key_rows, preferred_element_type=jnp.float32
+        "wqhd,wkhd->whqk", queries, key_rows, preferred_element_type=F32
     ) * head_dim ** (-0.5)
     scores = jnp.where(win_valid[:, None, None, :], scores, -1e30)
     highest = jnp.max(scores, axis=-1, keepdims=True)
     powers = jnp.exp(scores - highest)
-    weights = (powers / jnp.sum(powers, axis=-1, keepdims=True)).astype(jnp.bfloat16)
+    weights = (powers / jnp.sum(powers, axis=-1, keepdims=True)).astype(BF16)
     context = jnp.einsum(
-        "whqk,wkhd->wqhd", weights, values, preferred_element_type=jnp.float32
-    ).astype(jnp.bfloat16)
+        "whqk,wkhd->wqhd", weights, values, preferred_element_type=F32
+    ).astype(BF16)
     context = context.reshape(n_win, n_tok, d_model)
-    result = jnp.dot(context.reshape(-1, d_model), w_out, preferred_element_type=jnp.float32)
-    return ((as_float + result.reshape(n_win, n_tok, d_model)).astype(jnp.bfloat16), context)
-
-
-def on_device(
-    tokens,
-    norm_gain,
-    w_qkv,
-    w_out,
-    obs_vectors,
-    obs_lat,
-    obs_cell,
-    obs_count,
-    shift_offsets,
-    cotangent,
+    result = jnp.dot(context.reshape(-1, d_model), w_out, preferred_element_type=F32)
+    return ((as_float + result.reshape(n_win, n_tok, d_model)).astype(BF16), context)
+
+
+def general_program(
+    tokens, norm_gain, w_qkv, w_out, obs_vectors, obs_lat, obs_cell, obs_count, shift_offsets, cotangent
 ):
     n_batch, levels, lat_dev, lon_dev, d_model = tokens.shape
     n_lat = lax.axis_size("lat")
@@ -78,9 +82,7 @@
     capacity = obs_rows * 3 // (2 * n_lat)
     n_slots = n_lat * capacity
     destination = obs_lat[:, 0]
-    one_hot = (destination[:, None] == jnp.arange(n_lat, dtype=jnp.int32)[None, :]).astype(
-        jnp.int32
-    )
+    one_hot = (destination[:, None] == jnp.arange(n_lat, dtype=jnp.int32)[None, :]).astype(jnp.int32)
     earlier = jnp.cumsum(one_hot, axis=0) - one_hot
     rank_in = jnp.sum(earlier * one_hot, axis=1)
     slot_of = destination * capacity + rank_in
@@ -88,8 +90,8 @@
     cell_tag = jnp.where(is_live, obs_cell, -1)
     chooser = slot_of[None, :] == jnp.arange(n_slots, dtype=jnp.int32)[:, None]
     sent_rows = (
-        jnp.dot(chooser.astype(jnp.bfloat16), obs_vectors, preferred_element_type=jnp.float32)
-        .astype(jnp.bfloat16)
+        jnp.dot(chooser.astype(BF16), obs_vectors, preferred_element_type=F32)
+        .astype(BF16)
         .reshape(n_lat, capacity, d_model)
     )
     sent_tags = (jnp.sum(chooser.astype(jnp.int32) * (cell_tag[None, :] + 1), axis=1) - 1).reshape(
@@ -102,9 +104,9 @@
     flat_tokens = tokens.reshape(-1, d_model)
     placer = (
         got_tags.reshape(-1)[None, :] == jnp.arange(flat_tokens.shape[0], dtype=jnp.int32)[:, None]
-    ).astype(jnp.bfloat16)
-    added = jnp.dot(placer, got_rows.reshape(-1, d_model), preferred_element_type=jnp.float32)
-    enriched = (flat_tokens.astype(jnp.float32) + added).astype(jnp.bfloat16).reshape(tokens.shape)
+    ).astype(BF16)
+    added = jnp.dot(placer, got_rows.reshape(-1, d_model), preferred_element_type=F32)
+    enriched = (flat_tokens.astype(F32) + added).astype(BF16).reshape(tokens.shape)
     margin = WIN - 1
     north_part = from_behind(enriched[:, :, :margin], "lat", -1)
     heightened = jnp.concatenate([enriched, north_part], axis=2)
@@ -128,13 +130,325 @@
     context_rows = context.reshape(-1, d_model)
     contract = (((0,), (0,)), ((), ()))
     partial_rows = lax.psum_scatter(
-        lax.dot_general(cot_rows, context_rows, contract, preferred_element_type=jnp.float32),
+        lax.dot_general(cot_rows, context_rows, contract, preferred_element_type=F32),
         "lon",
         scatter_dimension=0,
         tiled=True,
     )
     gradient = lax.psum_scatter(partial_rows, ("lat", "dp"), scatter_dimension=1, tiled=True)
     return (block_out, gradient)
+
+
+def call(body, out_shape, args, specs, name, scratch=(), flops=0, moved=0):
+    return pl.pallas_call(
+        body,
+        out_shape=out_shape,
+        in_specs=specs,
+        out_specs=jax.tree.map(lambda _: pl.BlockSpec(memory_space=pltpu.VMEM), out_shape),
+        scratch_shapes=list(scratch),
+        compiler_params=pltpu.CompilerParams(vmem_limit_bytes=VMEM_LIMIT),
+        cost_estimate=pl.CostEstimate(flops=flops, bytes_accessed=moved, transcendentals=0),
+        name=name,
+    )(*args)
+
+
+VMEM_SPEC = pl.BlockSpec(memory_space=pltpu.VMEM)
+SMEM_SPEC = pl.BlockSpec(memory_space=pltpu.SMEM)
+
+
+def iota(shape, dim):
+    return lax.broadcasted_iota(jnp.int32, shape, dim)
+
+
+def over_rows(lhs, rhs):
+    return lax.dot_general(lhs, rhs, (((0,), (0,)), ((), ())), preferred_element_type=F32)
+
+
+def matmul(lhs, rhs):
+    return jnp.dot(lhs, rhs, preferred_element_type=F32)
+
+
+def route_body(n_lat, cap, slots, count_ref, lat_ref, cell_ref, vec_ref, *out_refs):
+    rows = vec_ref.shape[0]
+    here = lax.axis_index("lat")
+    lane = iota((rows, LANES), 1)
+    lat = lat_ref[...]
+    named = (lat == lane).astype(BF16)
+    below = (iota((rows, rows), 0) > iota((rows, rows), 1)).astype(BF16)
+    rank = jnp.sum(matmul(below, named) * named.astype(F32), axis=1, keepdims=True)
+    turn = jnp.where(lat < here, lat - here + n_lat, lat - here)
+    base = turn * slots
+    chooser = (base + rank.astype(jnp.int32) == lane).astype(BF16)
+    live = iota((1, rows), 1) < count_ref[0]
+    tag_row = jnp.where(live, cell_ref[...] + 1, 0).astype(F32)
+    same = iota((rows, rows), 0) == iota((rows, rows), 1)
+    tag = jnp.sum(jnp.where(same, tag_row, 0.0), axis=1, keepdims=True)
+    tag_at = jnp.where(lane == base + cap, tag, 0.0).astype(BF16)
+    picked = over_rows(chooser, vec_ref[...])
+    tags = over_rows(tag_at, chooser)
+    for k, out_ref in enumerate(out_refs):
+        piece = slice(k * slots, (k + 1) * slots)
+        out_ref[:, :LANES] = (picked[piece, :LANES] + tags[piece]).astype(BF16)
+        out_ref[:, LANES:] = picked[piece, LANES:].astype(BF16)
+
+
+def enrich_body(n_lat, cap, tok_ref, *refs):
+    parts, (own_ref, north_ref, east_ref) = refs[:n_lat], refs[n_lat:]
+    _, levels, rows, cols, width = tok_ref.shape
+    tags = parts[0][cap : cap + 1, :LANES].astype(F32)
+    for part in parts[1:]:
+        tags = tags + part[cap : cap + 1, :LANES].astype(F32)
+    n_tok = levels * rows * cols
+    place = (tags.astype(jnp.int32) == iota((n_tok, LANES), 0) + 1).astype(BF16)
+    added = matmul(place, jnp.concatenate([part[...] for part in parts], axis=0))
+    total = tok_ref[...].reshape(n_tok, width).astype(F32) + added
+    own_ref[...] = total.astype(BF16)
+    margin = (rows - 1) * cols
+    for level in range(levels):
+        start = level * rows * cols
+        north_ref[level * margin : (level + 1) * margin] = total[start : start + margin].astype(BF16)
+    east_ref[...] = (
+        total.reshape(levels * rows, cols, width)[:, :WIN].reshape(-1, width).astype(BF16)
+    )
+
+
+def corner_body(north_ref, out_ref):
+    rows, width = north_ref.shape
+    grid = north_ref[...].astype(F32).reshape(rows // (2 * WIN), 2 * WIN, width)
+    out_ref[...] = grid[:, :WIN].reshape(-1, width).astype(BF16)
+
+
+def window_body(which, n_lat, n_dp, n_src, shift_ref, *refs):
+    sources = refs[:n_src]
+    gain_ref, wqkv_ref, region_ref, ctx_ref, send_ref, keep_ref, qkv_ref = refs[n_src:]
+    width = gain_ref.shape[1]
+    n_tok = region_ref.shape[0]
+    half = width // n_dp
+    d_blk = half // n_lat
+    lat_shift, lon_shift = shift_ref[0, 0], shift_ref[0, 1]
+    row = iota((n_tok, 1), 0)
+    level = row // (WIN * WIN)
+    at_lat = row // WIN % WIN + lat_shift
+    at_lon = row % WIN + which * WIN + lon_shift
+    cols = 2 * WIN
+    inside, over = at_lat < WIN, at_lat >= WIN
+    near, far = at_lon < cols, at_lon >= cols
+    margin = WIN - 1
+    wanted = [
+        (inside & near, (level * WIN + at_lat) * cols + at_lon),
+        (over & near, (level * margin + at_lat - WIN) * cols + at_lon),
+        (inside & far, (level * WIN + at_lat) * WIN + at_lon - cols),
+        (over & far, (level * margin + at_lat - WIN) * WIN + at_lon - cols),
+    ]
+    region = None
+    for source, (here, index) in zip(sources, wanted):
+        index = jnp.where(here, index, -1)
+        pick = (index == iota((n_tok, source.shape[0]), 1)).astype(BF16)
+        part = matmul(pick, source[...])
+        region = part if region is None else region + part
+    region_ref[...] = region.astype(BF16)
+    centred = region - jnp.mean(region, axis=-1, keepdims=True)
+    variance = jnp.mean(centred * centred, axis=-1, keepdims=True)
+    normed = (centred * lax.rsqrt(variance + 1e-05) * gain_ref[...]).astype(BF16)
+    for third in range(3):
+        piece = slice(third * width, (third + 1) * width)
+        qkv_ref[:, piece] = matmul(normed, wqkv_ref[:, piece]).astype(BF16)
+    key = iota((1, n_tok), 1)
+    n_rows = WIN * n_lat
+    valid = lax.axis_index("lat") * WIN + key // WIN % WIN + lat_shift < n_rows
+    first = iota((n_tok, d_blk), 1) < d_blk // 2
+    scale = (d_blk // 2) ** (-0.5)
+    ones = jnp.ones((n_tok, d_blk), BF16)
+    lat_at, dp_at = lax.axis_index("lat"), lax.axis_index("dp")
+    for part, out_ref in ((1 - dp_at, send_ref), (dp_at, keep_ref)):
+        for k in range(n_lat):
+            lat = lat_at + k
+            lat = jnp.where(lat >= n_lat, lat - n_lat, lat)
+            at = pl.multiple_of((lat * n_dp + part) * d_blk, d_blk)
+            query = qkv_ref[:, pl.ds(at, d_blk)].astype(F32) * scale
+            both = jnp.concatenate(
+                [jnp.where(first, query, 0.0), jnp.where(first, 0.0, query)], axis=0
+            ).astype(BF16)
+            keys = qkv_ref[:, pl.ds(width + at, d_blk)]
+            scores = lax.dot_general(
+                both, keys, (((1,), (1,)), ((), ())), preferred_element_type=F32
+            )
+            scores = jnp.where(valid, scores, -1e30)
+            powers = jnp.exp(scores - jnp.max(scores, axis=-1, keepdims=True)).astype(BF16)
+            values = jnp.concatenate([qkv_ref[:, pl.ds(2 * width + at, d_blk)], ones], axis=1)
+            mixed = matmul(powers, values)
+            mixed = mixed[:, :d_blk] / mixed[:, d_blk:]
+            context = jnp.where(first, mixed[:n_tok], mixed[n_tok:]).astype(BF16)
+            out_ref[:, k * d_blk : (k + 1) * d_blk] = context
+            ctx_ref[:, pl.ds(at, d_blk)] = context
+
+
+def turn_body(n_lon, cot_ref, other_ref, out_ref, flat_ref):
+    _, levels, rows, cols, width = cot_ref.shape
+    e_blk = width // n_lon
+    n_tok = levels * rows * WIN
+    here = lax.axis_index("lon")
+    at = 0
+    for ref in (cot_ref, other_ref):
+        grid = ref[...].astype(F32).reshape(levels * rows, cols, width)
+        for which in range(cols // WIN):
+            flat_ref[...] = grid[:, which * WIN : (which + 1) * WIN].reshape(n_tok, width)
+            for place, block in enumerate(reversed_order(n_lon)):
+                lon = here ^ block
+                piece = flat_ref[:, pl.ds(pl.multiple_of(lon * e_blk, e_blk), e_blk)]
+                out_ref[place, :, at : at + n_tok] = piece.T.astype(BF16)
+            at += n_tok
+
+
+def reversed_order(count):
+    bits = count.bit_length() - 1
+    return [int(format(i, f"0{bits}b")[::-1], 2) if bits else 0 for i in range(count)]
+
+
+def project_body(reg0_ref, reg1_ref, ctx0_ref, ctx1_ref, wout_ref, out_ref):
+    _, levels, rows, cols, width = out_ref.shape
+    halves = []
+    for reg_ref, ctx_ref in ((reg0_ref, ctx0_ref), (reg1_ref, ctx1_ref)):
+        mixed = reg_ref[...].astype(F32) + matmul(ctx_ref[...], wout_ref[...])
+        halves.append(mixed.reshape(levels * rows, WIN, width))
+    whole = jnp.concatenate(halves, axis=1).astype(BF16)
+    out_ref[...] = whole.reshape(out_ref.shape)
+
+
+def gradient_body(cot_ref, *refs):
+    ctx_refs, (keep_ref, send_ref) = refs[:-2], refs[-2:]
+    context = jnp.concatenate([ref[...] for ref in ctx_refs], axis=0)
+    count = cot_ref.shape[0] // 2
+    for place in range(count):
+        keep_ref[place] = matmul(cot_ref[place], context)
+        send_ref[place] = matmul(cot_ref[count + place], context).astype(BF16)
+
+
+def fast_program(
+    tokens, norm_gain, w_qkv, w_out, obs_vectors, obs_lat, obs_cell, obs_count, shift_offsets, cotangent
+):
+    _, levels, lat_dev, lon_dev, d_model = tokens.shape
+    n_lat, n_lon, n_dp = (lax.axis_size(axis) for axis in ("lat", "lon", "dp"))
+    obs_rows = obs_vectors.shape[0]
+    cap = obs_rows * 3 // (2 * n_lat)
+    slots = LANES // n_lat
+    shape = jax.ShapeDtypeStruct
+    n_tok = levels * WIN * WIN
+    margin = WIN - 1
+    half = d_model // n_dp
+    e_blk = d_model // n_lon
+    d_blk = half // n_lat
+
+    payload = call(
+        functools.partial(route_body, n_lat, cap, slots),
+        [shape((slots, d_model), BF16)] * n_lat,
+        (obs_count, obs_lat, obs_cell.reshape(1, -1), obs_vectors),
+        [SMEM_SPEC, VMEM_SPEC, VMEM_SPEC, VMEM_SPEC],
+        "route",
+    )
+    arrived = [payload[0]] + [shifted(payload[k], "lat", k) for k in range(1, n_lat)]
+    own, north, east = call(
+        functools.partial(enrich_body, n_lat, cap),
+        [
+            shape((levels * lat_dev * lon_dev, d_model), BF16),
+            shape((levels * margin * lon_dev, d_model), BF16),
+            shape((levels * lat_dev * WIN, d_model), BF16),
+        ],
+        (tokens, *arrived),
+        [VMEM_SPEC] * (1 + n_lat),
+        "enrich",
+    )
+    north = from_behind(north, "lat", -1)
+    east = shifted(east, "lon", -1)
+    cot_other = swapped(cotangent, "dp", 1)
+    corner = call(
+        corner_body,
+        shape((levels * margin * WIN, d_model), BF16),
+        (north,),
+        [VMEM_SPEC],
+        "corner",
+    )
+    corner = shifted(corner, "lon", -1)
+    cot_turned = call(
+        functools.partial(turn_body, n_lon),
+        shape((n_lon, e_blk, n_dp * lon_dev // WIN * n_tok), BF16),
+        (cotangent, cot_other),
+        [VMEM_SPEC] * 2,
+        "turn",
+        [pltpu.VMEM((n_tok, d_model), F32)],
+    )
+    gain = norm_gain.reshape(1, -1)
+    windows = []
+    for which, sources in enumerate(((own, north), (own, north, east, corner))):
+        windows.append(
+            call(
+                functools.partial(window_body, which, n_lat, n_dp, len(sources)),
+                [
+                    shape((n_tok, d_model), BF16),
+                    shape((n_tok, d_model), BF16),
+                    shape((n_tok, half), BF16),
+                    shape((n_tok, half), BF16),
+                ],
+                (shift_offsets, *sources, gain, w_qkv),
+                [SMEM_SPEC] + [VMEM_SPEC] * (len(sources) + 2),
+                f"window{which}",
+                [pltpu.VMEM((n_tok, 3 * d_model), BF16)],
+                flops=2 * n_tok * d_model * 3 * d_model,
+            )
+        )
+    (region0, ctx0, send0, keep0), (region1, ctx1, send1, keep1) = windows
+    got0 = swapped(send0, "dp", 1)
+    got1 = swapped(send1, "dp", 1)
+    block_out = call(
+        project_body,
+        shape(tokens.shape, BF16),
+        (region0, region1, ctx0, ctx1, w_out),
+        [VMEM_SPEC] * 5,
+        "project",
+        flops=4 * n_tok * d_model * d_model,
+    )
+    kept, sent = call(
+        gradient_body,
+        [shape((n_lon // 2, e_blk, half), F32), shape((n_lon // 2, e_blk, half), BF16)],
+        (cot_turned, keep0, keep1, got0, got1),
+        [VMEM_SPEC] * 5,
+        "gradient",
+        flops=4 * n_tok * d_model * d_model,
+    )
+    bit = 1
+    while True:
+        total = kept + swapped(sent, "lon", bit).astype(F32)
+        bit *= 2
+        if bit == n_lon:
+            break
+        middle = total.shape[0] // 2
+        kept, sent = total[:middle], total[middle:].astype(BF16)
+    total = total[0]
+    blocks = [total[:, k * d_blk : (k + 1) * d_blk] for k in range(n_lat)]
+    gradient = blocks[0]
+    for k in range(1, n_lat):
+        gradient = gradient + shifted(blocks[k].astype(BF16), "lat", k).astype(F32)
+    return (block_out, gradient)
+
+
+def on_device(tokens, norm_gain, w_qkv, w_out, obs_vectors, *rest):
+    _, _, lat_dev, lon_dev, d_model = tokens.shape
+    n_lat, n_lon, n_dp = (lax.axis_size(axis) for axis in ("lat", "lon", "dp"))
+    cap = obs_vectors.shape[0] * 3 // (2 * n_lat)
+    fits = (
+        n_dp == 2
+        and n_lon > 1
+        and n_lon & (n_lon - 1) == 0
+        and LANES % n_lat == 0
+        and cap < LANES // n_lat
+        and lat_dev == WIN
+        and lon_dev == 2 * WIN
+        and d_model // n_lon % LANES == 0
+        and d_model // (n_lat * n_dp) == LANES
+        and d_model // HEADS * 2 == LANES
+    )
+    program = fast_program if fits else general_program
+    return program(tokens, norm_gain, w_qkv, w_out, obs_vectors, *rest)
 
 
 def solution(mesh):

time: 213 us -> 71.6 us (0.34)
  waiting for transfers between devices: 128 us -> 31.4 us
  local copies, waits for them, and re-layouts: 25 us -> 4.76 us
  matrix products: 19 us -> 0 us
  between operations: 19.3 us -> 1.42 us
  Pallas kernels: 0 us -> 15.1 us
  other arithmetic: 9.26 us -> 0.94 us
  starting transfers between devices: 11.1 us -> 17.6 us
    reduce_scatter x2 -> x0, waiting for transfers between devices: 109 us -> none  [the longest x1 65.3 us: on_device(): lax.psum_scatter(partial_rows, ('lat', 'dp'), scatter_dimension=1, tiled=...]
    dot_general x6 -> x0, matrix products: 15.6 us -> none  [the longest x1 5.73 us: window_block(): jnp.dot(normed.reshape(-1, d_model), w_qkv, preferred_element_type=jnp.fl...]
    pallas_call x0 -> x8, Pallas kernels: none -> 15.1 us  [call(): pl.pallas_call(body, out_shape=out_shape, in_specs=specs, out_specs=jax.t...]
    ppermute x0 -> x5, waiting for transfers between devices: none -> 13.1 us  [swapped(): return lax.ppermute(array, axis, [(i, i ^ bit) for i in range(devices)])]
    ppermute x1 -> x8, starting transfers between devices: 0.01 us -> 11 us  [shifted(): lax.ppermute(array, axis, [(i, (i + by) % devices) for i in range(devices)])]
    all_to_all x2 -> x0, starting transfers between devices: 9.68 us -> none  [the longest x1 6.32 us: on_device(): lax.all_to_all(sent_tags, 'lat', split_axis=0, concat_axis=0, tiled=True)]
    all_to_all x2 -> x0, waiting for transfers between devices: 8.47 us -> none  [the longest x1 4.9 us: on_device(): lax.all_to_all(sent_rows, 'lat', split_axis=0, concat_axis=0, tiled=True)]
    ppermute x1 -> x8, waiting for transfers between devices: 0.01 us -> 7.09 us  [shifted(): lax.ppermute(array, axis, [(i, (i + by) % devices) for i in range(devices)])]
  transfers between devices with their start and end apart: 6 -> 14, of which waited for: 5 -> 9; matrix products, arithmetic and copies ran while one was open for 4% -> 0% of each run, Pallas kernels for 0% -> 19%
where the time goes in v1:
time: 71.6 us; the launch traced here: 71.3 us
  waiting for transfers between devices  31.4 us (44%)
  starting transfers between devices  17.6 us (25%)
  Pallas kernels  15.1 us (21%)
  local copies, waits for them, and re-layouts  4.76 us (7%)
  between operations  1.42 us (2%)
  other arithmetic  0.94 us (1%)
    pallas_call x8, Pallas kernels, call(): pl.pallas_call(body, out_shape=out_shape, in_specs=specs, out_specs=jax.t...  15.1 us
    ppermute x5, waiting for transfers between devices, swapped(): return lax.ppermute(array, axis, [(i, i ^ bit) for i in range(devices)])  13.1 us
    ppermute x1, waiting for transfers between devices, from_behind(): return lax.ppermute(array, axis, pairs)  11.2 us
    ppermute x8, starting transfers between devices, shifted(): lax.ppermute(array, axis, [(i, (i + by) % devices) for i in range(devices)])  11 us
    ppermute x8, waiting for transfers between devices, shifted(): lax.ppermute(array, axis, [(i, (i + by) % devices) for i in range(devices)])  7.09 us
    ppermute x5, starting transfers between devices, swapped(): return lax.ppermute(array, axis, [(i, i ^ bit) for i in range(devices)])  5.4 us
    unnamed x15, local copies, waits for them, and re-layouts  4.69 us
  transfers between devices with their start and end apart: 14, of which 9 were waited for; matrix products, arithmetic and copies ran while one was open for 0% of the time, Pallas kernels for 19%

profile of v1, /device:TPU:0, one launch (start us, length us, event | category | flops | bytes accessed | tf_op | source)
XLA Modules:
  0.0 71.3 jit_solution(12975906192993821275)
XLA Ops:
  1.3 0.7 %copy.12.lat_ref = s32[64,1]{1,0:T(8,128)S(1)} copy(s32[64,1]{0,1:T(1,128)} %param.15) | data formatting | bytes 512 | tf_op args[5]
  2.0 0.9 %copy-done.3 = bf16[64,1024]{1,0:T(8,128)(2,1)S(1)} copy-done((bf16[64,1024]{1,0:T(8,128)(2,1)S(1)}, bf16[64,1024]{1,0:T(8,128)(2,1)}, u32[]{:S(2)}) %copy-start.3) | copy-done | bytes 131096
  4.2 3.1 %collective-permute-start = (bf16[32,1024]{1,0:T(8,128)(2,1)S(1)}, bf16[32,1024]{1,0:T(8,128)(2,1)S(1)}, u32[]{:S(2)}, u32[]{:S(2)}) collective-permute-start(bf16[32,1024]{1,0:T(8,128)(2,1)S(1)} %get-tuple-element.20), channel_id=1, source_target_pairs={{0,2},{2,4},{4,6},{6,0},{1,3},{3,5},{5,7},{7,1},{8,10},{10,12},{12... | collective-permute-start | bytes 196616 | tf_op jit(solution)/shard_map/ppermute | solution.py:26
  7.3 2.6 %collective-permute-start.1 = (bf16[32,1024]{1,0:T(8,128)(2,1)S(1)}, bf16[32,1024]{1,0:T(8,128)(2,1)S(1)}, u32[]{:S(2)}, u32[]{:S(2)}) collective-permute-start(bf16[32,1024]{1,0:T(8,128)(2,1)S(1)} %get-tuple-element.21), channel_id=1, source_target_pairs={{0,4},{2,6},{4,0},{6,2},{1,5},{3,7},{5,1},{7,3},{8,12},{10,14},{12... | collective-permute-start | bytes 196616 | tf_op jit(solution)/shard_map/ppermute | solution.py:26
  9.9 1.3 %collective-permute-start.2 = (bf16[32,1024]{1,0:T(8,128)(2,1)S(1)}, bf16[32,1024]{1,0:T(8,128)(2,1)S(1)}, u32[]{:S(2)}, u32[]{:S(2)}) collective-permute-start(bf16[32,1024]{1,0:T(8,128)(2,1)S(1)} %get-tuple-element.22), channel_id=1, source_target_pairs={{0,6},{2,0},{4,2},{6,4},{1,7},{3,1},{5,3},{7,5},{8,14},{10,8},{12,... | collective-permute-start | bytes 196616 | tf_op jit(solution)/shard_map/ppermute | solution.py:26
  11.9 2.5 %collective-permute-done.1.refs_2_ = bf16[32,1024]{1,0:T(8,128)(2,1)S(1)} collective-permute-done((bf16[32,1024]{1,0:T(8,128)(2,1)S(1)}, bf16[32,1024]{1,0:T(8,128)(2,1)S(1)}, u32[]{:S(2)}, u32[]{:S(2)}) %collective-permute-start.1) | collective-permute-done | bytes 65568 | tf_op jit(solution)/shard_map/ppermute | solution.py:26
  14.6 1.0 %copy-done.1 = bf16[1,2,8,16,1024]{4,3,2,1,0:T(8,128)(2,1)S(1)} copy-done((bf16[1,2,8,16,1024]{4,3,2,1,0:T(8,128)(2,1)S(1)}, bf16[1,2,8,16,1024]{4,3,2,1,0:T(8,128)(2,1)}, u32[]{:S(2)}) %copy-start.1) | copy-done | bytes 524312
  16.0 1.3 %collective-permute-start.3 = (bf16[224,1024]{1,0:T(8,128)(2,1)S(1)}, bf16[224,1024]{1,0:T(8,128)(2,1)S(1)}, u32[]{:S(2)}, u32[]{:S(2)}) collective-permute-start(bf16[224,1024]{1,0:T(8,128)(2,1)S(1)} %get-tuple-element.24), channel_id=1, source_target_pairs={{2,0},{4,2},{6,4},{3,1},{5,3},{7,5},{10,8},{12,10},{14,12},{11,9},... | collective-permute-start | bytes 1376264 | tf_op jit(solution)/shard_map/ppermute | solution.py:21
  17.3 1.6 %collective-permute-start.6 = (bf16[1,2,8,16,1024]{4,3,2,1,0:T(8,128)(2,1)}, bf16[1,2,8,16,1024]{4,3,2,1,0:T(8,128)(2,1)S(1)}, u32[]{:S(2)}, u32[]{:S(2)}) collective-permute-start(bf16[1,2,8,16,1024]{4,3,2,1,0:T(8,128)(2,1)} %cot_ref.1), channel_id=1, source_target_pairs={{0,1},{1,0},{2,3},{3,2},{4,5},{5,4},{6,7},{7,6},{8,9},{9,8},{10,11... | collective-permute-start | bytes 1572872 | tf_op jit(solution)/shard_map/ppermute | solution.py:31
  18.9 11.2 %collective-permute-done.3.refs_1_.north_ref = bf16[224,1024]{1,0:T(8,128)(2,1)S(1)} collective-permute-done((bf16[224,1024]{1,0:T(8,128)(2,1)S(1)}, bf16[224,1024]{1,0:T(8,128)(2,1)S(1)}, u32[]{:S(2)}, u32[]{:S(2)}) %collective-permute-start.3) | collective-permute-done | bytes 458784 | tf_op jit(solution)/shard_map/ppermute | solution.py:21
  31.5 5.7 %window0.1 = (bf16[128,1024]{1,0:T(8,128)(2,1)S(1)}, bf16[128,1024]{1,0:T(8,128)(2,1)S(1)}, bf16[128,512]{1,0:T(8,128)(2,1)S(1)}, bf16[128,512]{1,0:T(8,128)(2,1)S(1)}) custom-call(s32[1,2]{1,0:T(1,128)S(1)} %copy-done.5, bf16[256,1024]{1,0:T(8,128)(2,1)S(1)} %get-tuple-element.23.refs_0_, bf16[224,1024]{1,0:T(8,128)(2,1)S(1)} %collective-permute-done.3.refs_1_.north_ref, ...), custom_call_target="tpu_custom_call" | custom-call | flops 805306368 | tf_op jit(solution)/shard_map/window0/pallas_call | solution.py:143
  37.2 1.3 %collective-permute-start.7 = (bf16[128,512]{1,0:T(8,128)(2,1)S(1)}, bf16[128,512]{1,0:T(8,128)(2,1)S(1)}, u32[]{:S(2)}, u32[]{:S(2)}) collective-permute-start(bf16[128,512]{1,0:T(8,128)(2,1)S(1)} %get-tuple-element.32), channel_id=1, source_target_pairs={{0,1},{1,0},{2,3},{3,2},{4,5},{5,4},{6,7},{7,6},{8,9},{9,8},{10,11... | collective-permute-start | bytes 393224 | tf_op jit(solution)/shard_map/ppermute | solution.py:31
  38.6 5.8 %window1.1 = (bf16[128,1024]{1,0:T(8,128)(2,1)S(1)}, bf16[128,1024]{1,0:T(8,128)(2,1)S(1)}, bf16[128,512]{1,0:T(8,128)(2,1)S(1)}, bf16[128,512]{1,0:T(8,128)(2,1)S(1)}) custom-call(s32[1,2]{1,0:T(1,128)S(1)} %copy-done.5, bf16[256,1024]{1,0:T(8,128)(2,1)S(1)} %get-tuple-element.23.refs_0_, bf16[224,1024]{1,0:T(8,128)(2,1)S(1)} %collective-permute-done.3.refs_1_.north_ref, ...), custom_call_target="tpu_custom_call" | custom-call | flops 805306368 | tf_op jit(solution)/shard_map/window1/pallas_call | solution.py:143
  44.4 0.8 %collective-permute-start.8 = (bf16[128,512]{1,0:T(8,128)(2,1)S(1)}, bf16[128,512]{1,0:T(8,128)(2,1)S(1)}, u32[]{:S(2)}, u32[]{:S(2)}) collective-permute-start(bf16[128,512]{1,0:T(8,128)(2,1)S(1)} %get-tuple-element.33), channel_id=1, source_target_pairs={{0,1},{1,0},{2,3},{3,2},{4,5},{5,4},{6,7},{7,6},{8,9},{9,8},{10,11... | collective-permute-start | bytes 393224 | tf_op jit(solution)/shard_map/ppermute | solution.py:31
  45.7 4.3 %collective-permute-done.8.refs_3_ = bf16[128,512]{1,0:T(8,128)(2,1)S(1)} collective-permute-done((bf16[128,512]{1,0:T(8,128)(2,1)S(1)}, bf16[128,512]{1,0:T(8,128)(2,1)S(1)}, u32[]{:S(2)}, u32[]{:S(2)}) %collective-permute-start.8) | collective-permute-done | bytes 131104 | tf_op jit(solution)/shard_map/ppermute | solution.py:31
  50.1 0.7 gradient.1
  50.9 1.9 %collective-permute-done.9 = bf16[2,256,512]{2,1,0:T(8,128)(2,1)S(1)} collective-permute-done((bf16[2,256,512]{2,1,0:T(8,128)(2,1)S(1)}, bf16[2,256,512]{2,1,0:T(8,128)(2,1)S(1)}, u32[]{:S(2)}, u32[]{:S(2)}) %collective-permute-start.9) | collective-permute-done | bytes 524320 | tf_op jit(solution)/shard_map/ppermute | solution.py:31
  53.0 1.5 %collective-permute-start.10 = (bf16[1,256,512]{2,1,0:T(8,128)(2,1)S(1)}, bf16[1,256,512]{2,1,0:T(8,128)(2,1)S(1)}, u32[]{:S(2)}, u32[]{:S(2)}) collective-permute-start(bf16[1,256,512]{2,1,0:T(8,128)(2,1)S(1)} %slice.43), channel_id=1, source_target_pairs={{0,16},{8,24},{16,0},{24,8},{1,17},{9,25},{17,1},{25,9},{2,18},{10... | collective-permute-start | bytes 786440 | tf_op jit(solution)/shard_map/ppermute | solution.py:31
  54.5 6.9 %collective-permute-done.10 = bf16[1,256,512]{2,1,0:T(8,128)(2,1)S(1)} collective-permute-done((bf16[1,256,512]{2,1,0:T(8,128)(2,1)S(1)}, bf16[1,256,512]{2,1,0:T(8,128)(2,1)S(1)}, u32[]{:S(2)}, u32[]{:S(2)}) %collective-permute-start.10) | collective-permute-done | bytes 262176 | tf_op jit(solution)/shard_map/ppermute | solution.py:31
  61.5 1.8 %collective-permute-start.11 = (bf16[256,128]{1,0:T(8,128)(2,1)S(1)}, bf16[256,128]{1,0:T(8,128)(2,1)S(1)}, u32[]{:S(2)}, u32[]{:S(2)}) collective-permute-start(bf16[256,128]{1,0:T(8,128)(2,1)S(1)} %get-tuple-element.38), channel_id=1, source_target_pairs={{0,2},{2,4},{4,6},{6,0},{1,3},{3,5},{5,7},{7,1},{8,10},{10,12},{12... | collective-permute-start | bytes 196616 | tf_op jit(solution)/shard_map/ppermute | solution.py:26
  63.3 2.1 %collective-permute-start.13 = (bf16[256,128]{1,0:T(8,128)(2,1)S(1)}, bf16[256,128]{1,0:T(8,128)(2,1)S(1)}, u32[]{:S(2)}, u32[]{:S(2)}) collective-permute-start(bf16[256,128]{1,0:T(8,128)(2,1)S(1)} %get-tuple-element.39), channel_id=1, source_target_pairs={{0,6},{2,0},{4,2},{6,4},{1,7},{3,1},{5,3},{7,5},{8,14},{10,8},{12,... | collective-permute-start | bytes 196616 | tf_op jit(solution)/shard_map/ppermute | solution.py:26
  65.4 1.5 %project.1 = bf16[1,2,8,16,1024]{4,3,2,1,0:T(8,128)(2,1)} custom-call(bf16[128,1024]{1,0:T(8,128)(2,1)S(1)} %get-tuple-element.25.reg0_ref, bf16[128,1024]{1,0:T(8,128)(2,1)S(1)} %get-tuple-element.27.reg1_ref, bf16[128,1024]{1,0:T(8,128)(2,1)S(1)} %get-tuple-element.28.ctx0_ref, bf16[128,1024]{1,0:T(8,128)(2,1)S(1)} %get-tuple-element.29.ctx1_ref, ...), custom_call_target="tpu_custom_call" | custom-call | flops 536870912 | tf_op jit(solution)/shard_map/project/pallas_call | solution.py:143
  66.9 1.4 %collective-permute-done.11 = bf16[256,128]{1,0:T(8,128)(2,1)S(1)} collective-permute-done((bf16[256,128]{1,0:T(8,128)(2,1)S(1)}, bf16[256,128]{1,0:T(8,128)(2,1)S(1)}, u32[]{:S(2)}, u32[]{:S(2)}) %collective-permute-start.11) | collective-permute-done | bytes 65568 | tf_op jit(solution)/shard_map/ppermute | solution.py:26
  68.4 2.3 %collective-permute-done.12 = bf16[256,128]{1,0:T(8,128)(2,1)S(1)} collective-permute-done((bf16[256,128]{1,0:T(8,128)(2,1)S(1)}, bf16[256,128]{1,0:T(8,128)(2,1)S(1)}, u32[]{:S(2)}, u32[]{:S(2)}) %collective-permute-start.12) | collective-permute-done | bytes 65568 | tf_op jit(solution)/shard_map/ppermute | solution.py:26
  (32 shorter events, 5.4 us)
Async XLA Ops:
  2.0 0.9 %copy-start.3 = (bf16[64,1024]{1,0:T(8,128)(2,1)S(1)}, bf16[64,1024]{1,0:T(8,128)(2,1)}, u32[]{:S(2)}) copy-start(bf16[64,1024]{1,0:T(8,128)(2,1)} %vec_ref.1) | copy-start | bytes 393220
  2.9 0.7 copy-start.6
  4.2 7.6 %collective-permute-start = (bf16[32,1024]{1,0:T(8,128)(2,1)S(1)}, bf16[32,1024]{1,0:T(8,128)(2,1)S(1)}, u32[]{:S(2)}, u32[]{:S(2)}) collective-permute-start(bf16[32,1024]{1,0:T(8,128)(2,1)S(1)} %get-tuple-element.20), channel_id=1, source_target_pairs={{0,2},{2,4},{4,6},{6,0},{1,3},{3,5},{5,7},{7,1},{8,10},{10,12},{12... | collective-permute-start | bytes 196616 | tf_op jit(solution)/shard_map/ppermute | solution.py:26
  7.3 7.1 %collective-permute-start.1 = (bf16[32,1024]{1,0:T(8,128)(2,1)S(1)}, bf16[32,1024]{1,0:T(8,128)(2,1)S(1)}, u32[]{:S(2)}, u32[]{:S(2)}) collective-permute-start(bf16[32,1024]{1,0:T(8,128)(2,1)S(1)} %get-tuple-element.21), channel_id=1, source_target_pairs={{0,4},{2,6},{4,0},{6,2},{1,5},{3,7},{5,1},{7,3},{8,12},{10,14},{12... | collective-permute-start | bytes 196616 | tf_op jit(solution)/shard_map/ppermute | solution.py:26
  9.9 4.7 %collective-permute-start.2 = (bf16[32,1024]{1,0:T(8,128)(2,1)S(1)}, bf16[32,1024]{1,0:T(8,128)(2,1)S(1)}, u32[]{:S(2)}, u32[]{:S(2)}) collective-permute-start(bf16[32,1024]{1,0:T(8,128)(2,1)S(1)} %get-tuple-element.22), channel_id=1, source_target_pairs={{0,6},{2,0},{4,2},{6,4},{1,7},{3,1},{5,3},{7,5},{8,14},{10,8},{12,... | collective-permute-start | bytes 196616 | tf_op jit(solution)/shard_map/ppermute | solution.py:26
  14.6 1.0 %copy-start.1 = (bf16[1,2,8,16,1024]{4,3,2,1,0:T(8,128)(2,1)S(1)}, bf16[1,2,8,16,1024]{4,3,2,1,0:T(8,128)(2,1)}, u32[]{:S(2)}) copy-start(bf16[1,2,8,16,1024]{4,3,2,1,0:T(8,128)(2,1)} %tok_ref.1) | copy-start | bytes 1572868
  16.0 14.1 %collective-permute-start.3 = (bf16[224,1024]{1,0:T(8,128)(2,1)S(1)}, bf16[224,1024]{1,0:T(8,128)(2,1)S(1)}, u32[]{:S(2)}, u32[]{:S(2)}) collective-permute-start(bf16[224,1024]{1,0:T(8,128)(2,1)S(1)} %get-tuple-element.24), channel_id=1, source_target_pairs={{2,0},{4,2},{6,4},{3,1},{5,3},{7,5},{10,8},{12,10},{14,12},{11,9},... | collective-permute-start | bytes 1376264 | tf_op jit(solution)/shard_map/ppermute | solution.py:21
  17.3 28.0 %collective-permute-start.6 = (bf16[1,2,8,16,1024]{4,3,2,1,0:T(8,128)(2,1)}, bf16[1,2,8,16,1024]{4,3,2,1,0:T(8,128)(2,1)S(1)}, u32[]{:S(2)}, u32[]{:S(2)}) collective-permute-start(bf16[1,2,8,16,1024]{4,3,2,1,0:T(8,128)(2,1)} %cot_ref.1), channel_id=1, source_target_pairs={{0,1},{1,0},{2,3},{3,2},{4,5},{5,4},{6,7},{7,6},{8,9},{9,8},{10,11... | collective-permute-start | bytes 1572872 | tf_op jit(solution)/shard_map/ppermute | solution.py:31
  18.9 19.7 %collective-permute-start.4 = (bf16[128,1024]{1,0:T(8,128)(2,1)S(1)}, bf16[128,1024]{1,0:T(8,128)(2,1)S(1)}, u32[]{:S(2)}, u32[]{:S(2)}) collective-permute-start(bf16[128,1024]{1,0:T(8,128)(2,1)S(1)} %get-tuple-element.26), channel_id=1, source_target_pairs={{0,24},{8,0},{16,8},{24,16},{1,25},{9,1},{17,9},{25,17},{2,26},{10... | collective-permute-start | bytes 786440 | tf_op jit(solution)/shard_map/ppermute | solution.py:26
  30.1 8.5 %collective-permute-start.5 = (bf16[112,1024]{1,0:T(8,128)(2,1)S(1)}, bf16[112,1024]{1,0:T(8,128)(2,1)S(1)}, u32[]{:S(2)}, u32[]{:S(2)}) collective-permute-start(bf16[112,1024]{1,0:T(8,128)(2,1)S(1)} %corner.1), channel_id=1, source_target_pairs={{0,24},{8,0},{16,8},{24,16},{1,25},{9,1},{17,9},{25,17},{2,26},{10... | collective-permute-start | bytes 688136 | tf_op jit(solution)/shard_map/ppermute | solution.py:26
  30.2 0.7 copy-start.4
  30.9 0.7 copy-start.5
  31.5 13.7 %copy-start.2 = (bf16[1,2,8,16,1024]{4,3,2,1,0:T(8,128)(2,1)S(1)}, bf16[1,2,8,16,1024]{4,3,2,1,0:T(8,128)(2,1)}, u32[]{:S(2)}) copy-start(bf16[1,2,8,16,1024]{4,3,2,1,0:T(8,128)(2,1)} %cot_ref.1) | copy-start | bytes 1572868
  37.2 8.5 %collective-permute-start.7 = (bf16[128,512]{1,0:T(8,128)(2,1)S(1)}, bf16[128,512]{1,0:T(8,128)(2,1)S(1)}, u32[]{:S(2)}, u32[]{:S(2)}) collective-permute-start(bf16[128,512]{1,0:T(8,128)(2,1)S(1)} %get-tuple-element.32), channel_id=1, source_target_pairs={{0,1},{1,0},{2,3},{3,2},{4,5},{5,4},{6,7},{7,6},{8,9},{9,8},{10,11... | collective-permute-start | bytes 393224 | tf_op jit(solution)/shard_map/ppermute | solution.py:31
  44.4 21.0 %copy-start = (bf16[1024,1024]{1,0:T(8,128)(2,1)S(1)}, bf16[1024,1024]{1,0:T(8,128)(2,1)}, u32[]{:S(2)}) copy-start(bf16[1024,1024]{1,0:T(8,128)(2,1)} %wout_ref.1) | copy-start | bytes 6291460
  44.4 5.7 %collective-permute-start.8 = (bf16[128,512]{1,0:T(8,128)(2,1)S(1)}, bf16[128,512]{1,0:T(8,128)(2,1)S(1)}, u32[]{:S(2)}, u32[]{:S(2)}) collective-permute-start(bf16[128,512]{1,0:T(8,128)(2,1)S(1)} %get-tuple-element.33), channel_id=1, source_target_pairs={{0,1},{1,0},{2,3},{3,2},{4,5},{5,4},{6,7},{7,6},{8,9},{9,8},{10,11... | collective-permute-start | bytes 393224 | tf_op jit(solution)/shard_map/ppermute | solution.py:31
  50.8 2.0 %collective-permute-start.9 = (bf16[2,256,512]{2,1,0:T(8,128)(2,1)S(1)}, bf16[2,256,512]{2,1,0:T(8,128)(2,1)S(1)}, u32[]{:S(2)}, u32[]{:S(2)}) collective-permute-start(bf16[2,256,512]{2,1,0:T(8,128)(2,1)S(1)} %get-tuple-element.35), channel_id=1, source_target_pairs={{0,8},{8,0},{16,24},{24,16},{1,9},{9,1},{17,25},{25,17},{2,10},{10... | collective-permute-start | bytes 1572872 | tf_op jit(solution)/shard_map/ppermute | solution.py:31
  53.0 8.4 %collective-permute-start.10 = (bf16[1,256,512]{2,1,0:T(8,128)(2,1)S(1)}, bf16[1,256,512]{2,1,0:T(8,128)(2,1)S(1)}, u32[]{:S(2)}, u32[]{:S(2)}) collective-permute-start(bf16[1,256,512]{2,1,0:T(8,128)(2,1)S(1)} %slice.43), channel_id=1, source_target_pairs={{0,16},{8,24},{16,0},{24,8},{1,17},{9,25},{17,1},{25,9},{2,18},{10... | collective-permute-start | bytes 786440 | tf_op jit(solution)/shard_map/ppermute | solution.py:31
  61.5 6.8 %collective-permute-start.11 = (bf16[256,128]{1,0:T(8,128)(2,1)S(1)}, bf16[256,128]{1,0:T(8,128)(2,1)S(1)}, u32[]{:S(2)}, u32[]{:S(2)}) collective-permute-start(bf16[256,128]{1,0:T(8,128)(2,1)S(1)} %get-tuple-element.38), channel_id=1, source_target_pairs={{0,2},{2,4},{4,6},{6,0},{1,3},{3,5},{5,7},{7,1},{8,10},{10,12},{12... | collective-permute-start | bytes 196616 | tf_op jit(solution)/shard_map/ppermute | solution.py:26
  63.3 5.0 %collective-permute-start.13 = (bf16[256,128]{1,0:T(8,128)(2,1)S(1)}, bf16[256,128]{1,0:T(8,128)(2,1)S(1)}, u32[]{:S(2)}, u32[]{:S(2)}) collective-permute-start(bf16[256,128]{1,0:T(8,128)(2,1)S(1)} %get-tuple-element.39), channel_id=1, source_target_pairs={{0,6},{2,0},{4,2},{6,4},{1,7},{3,1},{5,3},{7,5},{8,14},{10,8},{12,... | collective-permute-start | bytes 196616 | tf_op jit(solution)/shard_map/ppermute | solution.py:26
  65.4 5.2 %collective-permute-start.12 = (bf16[256,128]{1,0:T(8,128)(2,1)S(1)}, bf16[256,128]{1,0:T(8,128)(2,1)S(1)}, u32[]{:S(2)}, u32[]{:S(2)}) collective-permute-start(bf16[256,128]{1,0:T(8,128)(2,1)S(1)} %get-tuple-element.40), channel_id=1, source_target_pairs={{0,4},{2,6},{4,0},{6,2},{1,5},{3,7},{5,1},{7,3},{8,12},{10,14},{12... | collective-permute-start | bytes 196616 | tf_op jit(solution)/shard_map/ppermute | solution.py:26

commit v2 on v0

--- a/solution.py
+++ b/solution.py
@@ -1,10 +1,20 @@
+import functools
+
 import jax
 import jax.numpy as jnp
 from jax import lax
+from jax.experimental import pallas as pl
+from jax.experimental.pallas import tpu as pltpu
 from jax.sharding import PartitionSpec as P
 
 HEADS = 16
 WIN = 8
+BF16 = jnp.bfloat16
+F32 = jnp.float32
+LANES = 128
+TILE = 16
+VMEM_LIMIT = 24 * 1024 * 1024
+SLOW = 10**10
 
 
 def from_behind(array, axis, by):
@@ -18,6 +28,11 @@
     return lax.ppermute(array, axis, [(i, (i + by) % devices) for i in range(devices)])
 
 
+def swapped(array, axis, bit):
+    devices = lax.axis_size(axis)
+    return lax.ppermute(array, axis, [(i, i ^ bit) for i in range(devices)])
+
+
 def to_windows(field_in):
     levels_n, rows_n, cols_n, feat_width = field_in.shape
     blocks = field_in.reshape(levels_n, rows_n // WIN, WIN, cols_n // WIN, WIN, feat_width)
@@ -33,44 +48,35 @@
 def window_block(win_tokens, win_valid, norm_gain, w_qkv, w_out):
     n_win, n_tok, d_model = win_tokens.shape
     head_dim = d_model // HEADS
-    as_float = win_tokens.astype(jnp.float32)
+    as_float = win_tokens.astype(F32)
     average = jnp.mean(as_float, axis=-1, keepdims=True)
     centred = as_float - average
     variance = jnp.mean(centred * centred, axis=-1, keepdims=True)
-    normed = (centred * lax.rsqrt(variance + 1e-05) * norm_gain).astype(jnp.bfloat16)
+    normed = (centred * lax.rsqrt(variance + 1e-05) * norm_gain).astype(BF16)
     projected = jnp.dot(
-        normed.reshape(-1, d_model), w_qkv, preferred_element_type=jnp.float32
-    ).astype(jnp.bfloat16)
+        normed.reshape(-1, d_model), w_qkv, preferred_element_type=F32
+    ).astype(BF16)
     projected = projected.reshape(n_win, n_tok, 3, HEADS, head_dim)
     queries = projected[:, :, 0]
     key_rows = projected[:, :, 1]
     values = projected[:, :, 2]
     scores = jnp.einsum(
-        "wqhd,wkhd->whqk", queries, key_rows, preferred_element_type=jnp.float32
+        "wqhd,wkhd->whqk", queries, key_rows, preferred_element_type=F32
     ) * head_dim ** (-0.5)
     scores = jnp.where(win_valid[:, None, None, :], scores, -1e30)
     highest = jnp.max(scores, axis=-1, keepdims=True)
     powers = jnp.exp(scores - highest)
-    weights = (powers / jnp.sum(powers, axis=-1, keepdims=True)).astype(jnp.bfloat16)
+    weights = (powers / jnp.sum(powers, axis=-1, keepdims=True)).astype(BF16)
     context = jnp.einsum(
-        "whqk,wkhd->wqhd", weights, values, preferred_element_type=jnp.float32
-    ).astype(jnp.bfloat16)
+        "whqk,wkhd->wqhd", weights, values, preferred_element_type=F32
+    ).astype(BF16)
     context = context.reshape(n_win, n_tok, d_model)
-    result = jnp.dot(context.reshape(-1, d_model), w_out, preferred_element_type=jnp.float32)
-    return ((as_float + result.reshape(n_win, n_tok, d_model)).astype(jnp.bfloat16), context)
-
-
-def on_device(
-    tokens,
-    norm_gain,
-    w_qkv,
-    w_out,
-    obs_vectors,
-    obs_lat,
-    obs_cell,
-    obs_count,
-    shift_offsets,
-    cotangent,
+    result = jnp.dot(context.reshape(-1, d_model), w_out, preferred_element_type=F32)
+    return ((as_float + result.reshape(n_win, n_tok, d_model)).astype(BF16), context)
+
+
+def general_program(
+    tokens, norm_gain, w_qkv, w_out, obs_vectors, obs_lat, obs_cell, obs_count, shift_offsets, cotangent
 ):
     n_batch, levels, lat_dev, lon_dev, d_model = tokens.shape
     n_lat = lax.axis_size("lat")
@@ -78,9 +84,7 @@
     capacity = obs_rows * 3 // (2 * n_lat)
     n_slots = n_lat * capacity
     destination = obs_lat[:, 0]
-    one_hot = (destination[:, None] == jnp.arange(n_lat, dtype=jnp.int32)[None, :]).astype(
-        jnp.int32
-    )
+    one_hot = (destination[:, None] == jnp.arange(n_lat, dtype=jnp.int32)[None, :]).astype(jnp.int32)
     earlier = jnp.cumsum(one_hot, axis=0) - one_hot
     rank_in = jnp.sum(earlier * one_hot, axis=1)
     slot_of = destination * capacity + rank_in
@@ -88,8 +92,8 @@
     cell_tag = jnp.where(is_live, obs_cell, -1)
     chooser = slot_of[None, :] == jnp.arange(n_slots, dtype=jnp.int32)[:, None]
     sent_rows = (
-        jnp.dot(chooser.astype(jnp.bfloat16), obs_vectors, preferred_element_type=jnp.float32)
-        .astype(jnp.bfloat16)
+        jnp.dot(chooser.astype(BF16), obs_vectors, preferred_element_type=F32)
+        .astype(BF16)
         .reshape(n_lat, capacity, d_model)
     )
     sent_tags = (jnp.sum(chooser.astype(jnp.int32) * (cell_tag[None, :] + 1), axis=1) - 1).reshape(
@@ -102,9 +106,9 @@
     flat_tokens = tokens.reshape(-1, d_model)
     placer = (
         got_tags.reshape(-1)[None, :] == jnp.arange(flat_tokens.shape[0], dtype=jnp.int32)[:, None]
-    ).astype(jnp.bfloat16)
-    added = jnp.dot(placer, got_rows.reshape(-1, d_model), preferred_element_type=jnp.float32)
-    enriched = (flat_tokens.astype(jnp.float32) + added).astype(jnp.bfloat16).reshape(tokens.shape)
+    ).astype(BF16)
+    added = jnp.dot(placer, got_rows.reshape(-1, d_model), preferred_element_type=F32)
+    enriched = (flat_tokens.astype(F32) + added).astype(BF16).reshape(tokens.shape)
     margin = WIN - 1
     north_part = from_behind(enriched[:, :, :margin], "lat", -1)
     heightened = jnp.concatenate([enriched, north_part], axis=2)
@@ -128,13 +132,410 @@
     context_rows = context.reshape(-1, d_model)
     contract = (((0,), (0,)), ((), ()))
     partial_rows = lax.psum_scatter(
-        lax.dot_general(cot_rows, context_rows, contract, preferred_element_type=jnp.float32),
+        lax.dot_general(cot_rows, context_rows, contract, preferred_element_type=F32),
         "lon",
         scatter_dimension=0,
         tiled=True,
     )
     gradient = lax.psum_scatter(partial_rows, ("lat", "dp"), scatter_dimension=1, tiled=True)
     return (block_out, gradient)
+
+
+def call(body, out_shape, args, specs, name, scratch=(), flops=1, moved=1):
+    return pl.pallas_call(
+        body,
+        out_shape=out_shape,
+        in_specs=specs,
+        out_specs=jax.tree.map(lambda _: pl.BlockSpec(memory_space=pltpu.VMEM), out_shape),
+        scratch_shapes=list(scratch),
+        compiler_params=pltpu.CompilerParams(vmem_limit_bytes=VMEM_LIMIT),
+        cost_estimate=pl.CostEstimate(flops=flops, bytes_accessed=moved, transcendentals=0),
+        name=name,
+    )(*args)
+
+
+VMEM_SPEC = pl.BlockSpec(memory_space=pltpu.VMEM)
+SMEM_SPEC = pl.BlockSpec(memory_space=pltpu.SMEM)
+ANY_SPEC = pl.BlockSpec(memory_space=pl.ANY)
+
+
+def iota(shape, dim):
+    return lax.broadcasted_iota(jnp.int32, shape, dim)
+
+
+def over_rows(lhs, rhs):
+    return lax.dot_general(lhs, rhs, (((0,), (0,)), ((), ())), preferred_element_type=F32)
+
+
+def matmul(lhs, rhs):
+    return jnp.dot(lhs, rhs, preferred_element_type=F32)
+
+
+def copy_all(pairs, sems):
+    copies = [pltpu.make_async_copy(src, dst, sems.at[i]) for i, (src, dst) in enumerate(pairs)]
+    for copy in copies:
+        copy.start()
+    return copies
+
+
+def route_body(n_lat, count_ref, cell_hbm, lat_hbm, vec_hbm, *refs):
+    out_refs, (cell_ref, lat_ref, vec_ref, sems) = refs[:n_lat], refs[n_lat:]
+    copies = copy_all([(cell_hbm, cell_ref), (lat_hbm, lat_ref), (vec_hbm, vec_ref)], sems)
+    rows = vec_ref.shape[0]
+    here = lax.axis_index("lat")
+    lane = iota((rows, LANES), 1)
+    below = (iota((rows, rows), 0) > iota((rows, rows), 1)).astype(BF16)
+    same = iota((rows, rows), 0) == iota((rows, rows), 1)
+    copies[0].wait()
+    copies[1].wait()
+    tag = jnp.where(iota((1, rows), 1) < count_ref[0], cell_ref[...] + 1, 0)
+    tag, lat = (
+        jnp.sum(jnp.where(same, field.astype(F32), 0.0), axis=1, keepdims=True)
+        for field in (tag, lat_ref[...])
+    )
+    lat = lat.astype(jnp.int32)
+    named = (lat == lane).astype(BF16)
+    rank = jnp.sum(matmul(below, named) * named.astype(F32), axis=1, keepdims=True)
+    rank = rank.astype(jnp.int32)
+    base = jnp.where(lat < here, lat - here + n_lat, lat - here) * TILE
+    late = rank >= TILE
+    choosers = [
+        (jnp.where(chosen, base + rank - back, -1) == lane).astype(BF16)
+        for chosen, back in ((rank < TILE, 0), (late, TILE), (late, TILE // 2))
+    ]
+    tags = sum(
+        over_rows(jnp.where(lane == base + i, tag, 0.0).astype(BF16), chooser)
+        for i, chooser in enumerate(choosers)
+    )
+    copies[2].wait()
+    width = vec_ref.shape[1]
+    picked = over_rows(choosers[0], vec_ref[...])
+    extra = over_rows(choosers[1], vec_ref[:, : width // 2])
+    extra = extra + over_rows(choosers[2], vec_ref[:, width // 2 :])
+    for k, out_ref in enumerate(out_refs):
+        piece = slice(k * TILE, (k + 1) * TILE)
+        out_ref[:, :width] = picked[piece].astype(BF16)
+        out_ref[:, width : width + width // 2] = extra[piece].astype(BF16)
+        out_ref[:, width + width // 2 :] = tags[piece].astype(BF16)
+
+
+def load_body(*refs):
+    count = len(refs) // 2
+    for copy in copy_all(list(zip(refs[:count], refs[count:-1])), refs[-1]):
+        copy.wait()
+
+
+def load(arrays, name):
+    return call(
+        load_body,
+        [jax.ShapeDtypeStruct(array.shape, array.dtype) for array in arrays],
+        tuple(in_hbm(array) for array in arrays),
+        [ANY_SPEC] * len(arrays),
+        name,
+        [pltpu.SemaphoreType.DMA((len(arrays),))],
+    )
+
+
+def stage_body(sizes, shift_ref, tok_hbm, tok_ref, pick_ref, sem):
+    copy = pltpu.make_async_copy(tok_hbm, tok_ref, sem)
+    copy.start()
+    lat_shift, lon_shift = shift_ref[:, :1], shift_ref[:, 1:]
+    n_rows, n_cols = pick_ref.shape
+    n_tok = n_rows // 2
+    row = iota((n_rows, 1), 0)
+    level = row // (WIN * WIN) % (n_tok // (WIN * WIN))
+    at_lat = row // WIN % WIN + lat_shift
+    at_lon = row % WIN + row // n_tok * WIN + lon_shift
+    cols, margin = 2 * WIN, WIN - 1
+    starts = [sum(sizes[:i]) for i in range(len(sizes))]
+    inside = (level * WIN + at_lat) * cols + at_lon
+    north = (level * margin + at_lat - WIN) * WIN + at_lon % WIN
+    east = (level * WIN + at_lat) * WIN + at_lon - cols
+    index = jnp.where(
+        at_lat < WIN,
+        jnp.where(at_lon < cols, inside, east + starts[3]),
+        north + jnp.where(at_lon < WIN, starts[1], jnp.where(at_lon < cols, starts[2], starts[4])),
+    )
+    pick_ref[...] = (index == iota((n_rows, n_cols), 1)).astype(BF16)
+    copy.wait()
+
+
+def enrich_body(n_lat, tok_ref, *refs):
+    parts, (own_ref, north0_ref, north1_ref, east_ref) = refs[:n_lat], refs[n_lat:]
+    _, levels, rows, cols, width = tok_ref.shape
+    n_tok = levels * rows * cols
+    half = width // 2
+    tags = sum(part[:, width + half :].astype(F32) for part in parts).astype(jnp.int32)
+    row = iota((n_tok, LANES), 0) + 1
+    places = [(tags[i : i + 1] == row).astype(BF16)[:, : n_lat * TILE] for i in range(3)]
+    got = jnp.concatenate([part[...] for part in parts], axis=0)
+    extra = got[:, width : width + half]
+    total = tok_ref[...].reshape(n_tok, width).astype(F32) + matmul(places[0], got[:, :width])
+    total = total + jnp.concatenate([matmul(place, extra) for place in places[1:]], axis=1)
+    own_ref[...] = total.astype(BF16)
+    grid = total.reshape(levels, rows, cols, width)
+    for out_ref, part in (
+        (north0_ref, grid[:, : rows - 1, :WIN]),
+        (north1_ref, grid[:, : rows - 1, WIN:]),
+        (east_ref, grid[:, :, :WIN]),
+    ):
+        out_ref[...] = part.reshape(out_ref.shape).astype(BF16)
+
+
+def region_body(pick_ref, gain_ref, *refs):
+    sources, (region_ref, normed_ref) = refs[:-2], refs[-2:]
+    region = matmul(pick_ref[...], jnp.concatenate([ref[...] for ref in sources], axis=0))
+    region_ref[...] = region.astype(BF16)
+    centred = region - jnp.mean(region, axis=-1, keepdims=True)
+    variance = jnp.mean(centred * centred, axis=-1, keepdims=True)
+    normed_ref[...] = (centred * lax.rsqrt(variance + 1e-05) * gain_ref[...]).astype(BF16)
+
+
+def block_start(part, k, n_lat, n_dp, d_blk):
+    lat = lax.axis_index("lat") + k
+    lat = jnp.where(lat >= n_lat, lat - n_lat, lat)
+    dp = lax.axis_index("dp")
+    dp = 1 - dp if part else dp
+    return pl.multiple_of((lat * n_dp + dp) * d_blk, d_blk)
+
+
+def attend_body(part, turns, n_lat, n_dp, normed_ref, wqkv_ref, shift_ref, out_ref):
+    n_rows, width = normed_ref.shape
+    n_tok = n_rows // 2
+    d_blk = width // (n_lat * n_dp)
+    starts = [block_start(part, k, n_lat, n_dp, d_blk) for k in turns]
+    normed = normed_ref[...]
+    thirds = []
+    for third in range(3):
+        weights = jnp.concatenate(
+            [wqkv_ref[:, pl.ds(third * width + at, d_blk)] for at in starts], axis=1
+        )
+        thirds.append(matmul(normed, weights))
+    scale = (d_blk // 2) ** (-0.5)
+    queries = thirds[0].astype(BF16).astype(F32) * scale
+    keys, values = thirds[1].astype(BF16), thirds[2].astype(BF16)
+    key = iota((1, n_tok), 1)
+    valid = lax.axis_index("lat") * WIN + key // WIN % WIN + shift_ref[:, :1] < WIN * n_lat
+    first = iota((n_tok, d_blk), 1) < d_blk // 2
+    ones = jnp.ones((n_tok, d_blk), BF16)
+    for which in range(2):
+        rows = slice(which * n_tok, (which + 1) * n_tok)
+        for k in range(len(turns)):
+            cols = slice(k * d_blk, (k + 1) * d_blk)
+            query = queries[rows, cols]
+            both = jnp.concatenate(
+                [jnp.where(first, query, 0.0), jnp.where(first, 0.0, query)], axis=0
+            ).astype(BF16)
+            scores = lax.dot_general(
+                both, keys[rows, cols], (((1,), (1,)), ((), ())), preferred_element_type=F32
+            )
+            scores = jnp.where(valid, scores, -1e30)
+            powers = jnp.exp(scores - jnp.max(scores, axis=-1, keepdims=True)).astype(BF16)
+            mixed = matmul(powers, jnp.concatenate([values[rows, cols], ones], axis=1))
+            mixed = mixed[:, :d_blk] / mixed[:, d_blk:]
+            out_ref[rows, cols] = jnp.where(first, mixed[:n_tok], mixed[n_tok:]).astype(BF16)
+
+
+def turn_body(n_lon, cot_ref, other_ref, out_ref, flat_ref):
+    _, levels, rows, cols, width = cot_ref.shape
+    e_blk = width // n_lon
+    n_tok = levels * rows * WIN
+    here = lax.axis_index("lon")
+    at = 0
+    for ref in (cot_ref, other_ref):
+        grid = ref[...].astype(F32).reshape(levels * rows, cols, width)
+        for which in range(cols // WIN):
+            flat_ref[...] = grid[:, which * WIN : (which + 1) * WIN].reshape(n_tok, width)
+            for place, block in enumerate(reversed_order(n_lon)):
+                lon = here ^ block
+                piece = flat_ref[:, pl.ds(pl.multiple_of(lon * e_blk, e_blk), e_blk)]
+                out_ref[place, :, at : at + n_tok] = piece.T.astype(BF16)
+            at += n_tok
+
+
+def reversed_order(count):
+    bits = count.bit_length() - 1
+    return [int(format(i, f"0{bits}b")[::-1], 2) if bits else 0 for i in range(count)]
+
+
+def project_body(groups, n_lat, n_dp, reg_ref, wout_ref, *refs):
+    ctx_refs, out_ref = refs[:-1], refs[-1]
+    _, levels, rows, cols, width = out_ref.shape
+    d_blk = width // (n_lat * n_dp)
+    mixed = reg_ref[...].astype(F32)
+    for (part, turns), ctx_ref in zip(groups, ctx_refs):
+        starts = [block_start(part, k, n_lat, n_dp, d_blk) for k in turns]
+        weights = jnp.concatenate([wout_ref[pl.ds(at, d_blk), :] for at in starts], axis=0)
+        mixed = mixed + matmul(ctx_ref[...], weights)
+    n_tok = levels * rows * WIN
+    halves = [
+        mixed[i * n_tok : (i + 1) * n_tok].reshape(levels * rows, WIN, width)
+        for i in range(cols // WIN)
+    ]
+    out_ref[...] = jnp.concatenate(halves, axis=1).astype(BF16).reshape(out_ref.shape)
+
+
+def gradient_body(cot_ref, mine_ref, other_ref, keep_ref, send_ref):
+    context = jnp.concatenate([mine_ref[...], other_ref[...]], axis=0)
+    count = cot_ref.shape[0] // 2
+    for place in range(count):
+        send_ref[place] = matmul(cot_ref[count + place], context).astype(BF16)
+    for place in range(count):
+        keep_ref[place] = matmul(cot_ref[place], context)
+
+
+def in_hbm(array):
+    return pltpu.with_memory_space_constraint(array, pltpu.HBM)
+
+
+def fast_program(
+    tokens, norm_gain, w_qkv, w_out, obs_vectors, obs_lat, obs_cell, obs_count, shift_offsets, cotangent
+):
+    _, levels, lat_dev, lon_dev, d_model = tokens.shape
+    n_lat, n_lon, n_dp = (lax.axis_size(axis) for axis in ("lat", "lon", "dp"))
+    shape = jax.ShapeDtypeStruct
+    n_tok = levels * lat_dev * WIN
+    n_rows = levels * lat_dev * lon_dev
+    n_margin = levels * (lat_dev - 1) * WIN
+    e_blk = d_model // n_lon
+    d_blk = d_model // (n_lat * n_dp)
+    dma = pltpu.SemaphoreType.DMA
+
+    fetched = (obs_cell.reshape(1, -1), obs_lat.reshape(1, -1), obs_vectors)
+    payload = call(
+        functools.partial(route_body, n_lat),
+        [shape((TILE, d_model + d_model // 2 + LANES), BF16)] * n_lat,
+        (obs_count, *(in_hbm(array) for array in fetched)),
+        [SMEM_SPEC] + [ANY_SPEC] * 3,
+        "route",
+        [*(pltpu.VMEM(array.shape, array.dtype) for array in fetched), dma((3,))],
+    )
+    arrived = [payload[0]] + [shifted(payload[k], "lat", k) for k in range(1, n_lat)]
+
+    sizes = (n_rows, n_margin, n_margin, n_tok, n_margin)
+    shift_offsets, tokens = lax.optimization_barrier((payload[0], shift_offsets, tokens))[1:]
+    tokens, picks = call(
+        functools.partial(stage_body, sizes),
+        [shape(tokens.shape, BF16), shape((n_rows, sum(sizes)), BF16)],
+        (shift_offsets, in_hbm(tokens)),
+        [VMEM_SPEC, ANY_SPEC],
+        "stage",
+        [dma],
+    )
+    own, north0, north1, east = call(
+        functools.partial(enrich_body, n_lat),
+        [shape((n, d_model), BF16) for n in (n_rows, n_margin, n_margin, n_tok)],
+        (tokens, *arrived),
+        [VMEM_SPEC] * (1 + n_lat),
+        "enrich",
+    )
+    loaded = (w_qkv, norm_gain.reshape(1, -1))
+    loaded = lax.optimization_barrier((own, *loaded))[1:]
+    w_qkv, gain = load(loaded, "weights")
+    north0 = from_behind(north0, "lat", -1)
+    north1 = from_behind(lax.optimization_barrier((north1, gain))[0], "lat", -1)
+    east = shifted(east, "lon", -1)
+    cot_other = swapped(cotangent, "dp", 1)
+    corner = shifted(north0, "lon", -1)
+    region, normed = call(
+        region_body,
+        [shape((n_rows, d_model), BF16)] * 2,
+        (picks, gain, own, north0, north1, east, corner),
+        [VMEM_SPEC] * 7,
+        "region",
+    )
+    first, second = [k for k in range(n_lat) if k % 3], [k for k in range(n_lat) if k % 3 == 0]
+
+    def attend(normed, part, turns):
+        return call(
+            functools.partial(attend_body, part, turns, n_lat, n_dp),
+            shape((n_rows, len(turns) * d_blk), BF16),
+            (normed, w_qkv, shift_offsets),
+            [VMEM_SPEC] * 3,
+            f"attend{part}{turns[0]}",
+        )
+
+    def local_gradient(turns, mine, other, cost):
+        width = len(turns) * d_blk
+        return call(
+            gradient_body,
+            [shape((n_lon // 2, e_blk, width), F32), shape((n_lon // 2, e_blk, width), BF16)],
+            (cot_turned, mine, other),
+            [VMEM_SPEC] * 3,
+            f"gradient{turns[0]}",
+            flops=cost,
+        )
+
+    def fold(kept, sent, bit):
+        total = kept + swapped(sent, "lon", bit).astype(F32)
+        middle = total.shape[0] // 2
+        return (total[:middle], total[middle:].astype(BF16)) if middle else (total, None)
+
+    def over_lon(kept, sent, bit):
+        while bit < n_lon:
+            kept, sent = fold(kept, sent, bit)
+            bit *= 2
+        return kept[0]
+
+    def over_lat(total, turns):
+        blocks = []
+        for i, k in enumerate(turns):
+            block = total[:, i * d_blk : (i + 1) * d_blk]
+            blocks.append(shifted(block.astype(BF16), "lat", k).astype(F32) if k else block)
+        return blocks
+
+    def after(array, *others):
+        return lax.optimization_barrier((array, *others))[0]
+
+    cot_turned = call(
+        functools.partial(turn_body, n_lon),
+        shape((n_lon, e_blk, n_dp * n_rows), BF16),
+        (cotangent, cot_other),
+        [VMEM_SPEC] * 2,
+        "turn",
+        [pltpu.VMEM((n_tok, d_model), F32)],
+    )
+    theirs0 = attend(normed, 1, first)
+    got0 = swapped(theirs0, "dp", 1)
+    theirs1 = attend(after(normed, theirs0), 1, second)
+    got1 = swapped(theirs1, "dp", 1)
+    mine0 = attend(after(normed, theirs1), 0, first)
+    mine1 = attend(after(normed, mine0), 0, second)
+    kept0, sent0 = local_gradient(first, mine0, after(got0, mine1), 1)
+    kept1, sent1 = local_gradient(second, mine1, after(got1, sent0), SLOW)
+    total0 = over_lon(kept0, sent0, 1)
+    total1 = over_lon(kept1, sent1, 1)
+    blocks = over_lat(total0, first) + over_lat(total1, second)
+    gradient = functools.reduce(jnp.add, blocks)
+    groups = [(1, first), (0, first), (1, second), (0, second)]
+    block_out = call(
+        functools.partial(project_body, groups, n_lat, n_dp),
+        shape((1, levels, lat_dev, lon_dev, d_model), BF16),
+        (region, w_out, theirs0, mine0, theirs1, mine1),
+        [VMEM_SPEC] * 6,
+        "project",
+    )
+    return (block_out, gradient)
+
+
+def on_device(tokens, norm_gain, w_qkv, w_out, obs_vectors, *rest):
+    _, _, lat_dev, lon_dev, d_model = tokens.shape
+    n_lat, n_lon, n_dp = (lax.axis_size(axis) for axis in ("lat", "lon", "dp"))
+    cap = obs_vectors.shape[0] * 3 // (2 * n_lat)
+    fits = (
+        n_dp == 2
+        and n_lon > 2
+        and n_lon & (n_lon - 1) == 0
+        and n_lat * TILE <= LANES
+        and cap * 2 == TILE * 3
+        and lat_dev == WIN
+        and lon_dev == 2 * WIN
+        and d_model // n_lon % LANES == 0
+        and d_model // (n_lat * n_dp) == LANES
+        and d_model // HEADS * 2 == LANES
+    )
+    program = fast_program if fits else general_program
+    return program(tokens, norm_gain, w_qkv, w_out, obs_vectors, *rest)
 
 
 def solution(mesh):

time: 213 us -> 56.9 us (0.27)
  waiting for transfers between devices: 128 us -> 16.6 us
  local copies, waits for them, and re-layouts: 25 us -> 0.73 us
  matrix products: 19 us -> 0 us
  between operations: 19.3 us -> 1.53 us
  Pallas kernels: 0 us -> 15.5 us
  starting transfers between devices: 11.1 us -> 21.5 us
  other arithmetic: 9.26 us -> 0.84 us
    reduce_scatter x2 -> x0, waiting for transfers between devices: 109 us -> none  [the longest x1 65.3 us: on_device(): lax.psum_scatter(partial_rows, ('lat', 'dp'), scatter_dimension=1, tiled=...]
    dot_general x6 -> x0, matrix products: 15.6 us -> none  [the longest x1 5.73 us: window_block(): jnp.dot(normed.reshape(-1, d_model), w_qkv, preferred_element_type=jnp.fl...]
    pallas_call x0 -> x13, Pallas kernels: none -> 15.5 us  [call(): pl.pallas_call(body, out_shape=out_shape, in_specs=specs, out_specs=jax.t...]
    ppermute x1 -> x8, starting transfers between devices: 0.01 us -> 12.4 us  [shifted(): lax.ppermute(array, axis, [(i, (i + by) % devices) for i in range(devices)])]
    unnamed x14 -> x8, local copies, waits for them, and re-layouts: 10.8 us -> 0.67 us
    all_to_all x2 -> x0, starting transfers between devices: 9.68 us -> none  [the longest x1 6.32 us: on_device(): lax.all_to_all(sent_tags, 'lat', split_axis=0, concat_axis=0, tiled=True)]
    all_to_all x2 -> x0, waiting for transfers between devices: 8.47 us -> none  [the longest x1 4.9 us: on_device(): lax.all_to_all(sent_rows, 'lat', split_axis=0, concat_axis=0, tiled=True)]
    ppermute x0 -> x7, starting transfers between devices: none -> 6.5 us  [swapped(): return lax.ppermute(array, axis, [(i, i ^ bit) for i in range(devices)])]
  transfers between devices with their start and end apart: 6 -> 17, of which waited for: 5 -> 9; matrix products, arithmetic and copies ran while one was open for 4% -> 0% of each run, Pallas kernels for 0% -> 24%
where the time goes in v2:
time: 56.9 us; the launch traced here: 56.6 us
  starting transfers between devices  21.5 us (38%)
  waiting for transfers between devices  16.6 us (29%)
  Pallas kernels  15.5 us (27%)
  between operations  1.53 us (3%)
  other arithmetic  0.84 us (1%)
  local copies, waits for them, and re-layouts  0.73 us (1%)
    pallas_call x13, Pallas kernels, call(): pl.pallas_call(body, out_shape=out_shape, in_specs=specs, out_specs=jax.t...  15.5 us
    ppermute x8, starting transfers between devices, shifted(): lax.ppermute(array, axis, [(i, (i + by) % devices) for i in range(devices)])  12.4 us
    ppermute x2, waiting for transfers between devices, from_behind(): return lax.ppermute(array, axis, pairs)  9.2 us
    ppermute x7, starting transfers between devices, swapped(): return lax.ppermute(array, axis, [(i, i ^ bit) for i in range(devices)])  6.5 us
    ppermute x7, waiting for transfers between devices, swapped(): return lax.ppermute(array, axis, [(i, i ^ bit) for i in range(devices)])  4.86 us
    ppermute x2, starting transfers between devices, from_behind(): return lax.ppermute(array, axis, pairs)  2.58 us
    ppermute x8, waiting for transfers between devices, shifted(): lax.ppermute(array, axis, [(i, (i + by) % devices) for i in range(devices)])  2.53 us
  transfers between devices with their start and end apart: 17, of which 9 were waited for; matrix products, arithmetic and copies ran while one was open for 0% of the time, Pallas kernels for 24%

profile of v2, /device:TPU:0, one launch (start us, length us, event | category | flops | bytes accessed | tf_op | source)
XLA Modules:
  0.0 56.6 jit_solution(12361802204105957777)
XLA Ops:
  1.3 1.5 %route.1 = (bf16[16,1664]{1,0:T(8,128)(2,1)S(1)}, bf16[16,1664]{1,0:T(8,128)(2,1)S(1)}, bf16[16,1664]{1,0:T(8,128)(2,1)S(1)}, bf16[16,1664]{1,0:T(8,128)(2,1)S(1)}) custom-call(s32[1]{0:T(128)S(6)} %copy.12.count_ref, s32[1,64]{1,0:T(1,128)} %bitcast.8, s32[1,64]{1,0:T(1,128)} %bitcast.9, bf16[64,1024]{1,0:T(8,128)(2,1)} %vec_hbm.1), custom_call_target="tpu_custom_call" | custom-call | flops 1 | bytes 1 | tf_op jit(solution)/shard_map/route/pallas_call | solution.py:145
  2.8 3.1 %collective-permute-start = (bf16[16,1664]{1,0:T(8,128)(2,1)S(1)}, bf16[16,1664]{1,0:T(8,128)(2,1)S(1)}, u32[]{:S(2)}, u32[]{:S(2)}) collective-permute-start(bf16[16,1664]{1,0:T(8,128)(2,1)S(1)} %get-tuple-element.35), channel_id=1, source_target_pairs={{0,2},{2,4},{4,6},{6,0},{1,3},{3,5},{5,7},{7,1},{8,10},{10,12},{12... | collective-permute-start | bytes 159752 | tf_op jit(solution)/shard_map/ppermute | solution.py:28
  5.9 2.6 %collective-permute-start.1 = (bf16[16,1664]{1,0:T(8,128)(2,1)S(1)}, bf16[16,1664]{1,0:T(8,128)(2,1)S(1)}, u32[]{:S(2)}, u32[]{:S(2)}) collective-permute-start(bf16[16,1664]{1,0:T(8,128)(2,1)S(1)} %get-tuple-element.36), channel_id=1, source_target_pairs={{0,4},{2,6},{4,0},{6,2},{1,5},{3,7},{5,1},{7,3},{8,12},{10,14},{12... | collective-permute-start | bytes 159752 | tf_op jit(solution)/shard_map/ppermute | solution.py:28
  8.5 1.3 %collective-permute-start.2 = (bf16[16,1664]{1,0:T(8,128)(2,1)S(1)}, bf16[16,1664]{1,0:T(8,128)(2,1)S(1)}, u32[]{:S(2)}, u32[]{:S(2)}) collective-permute-start(bf16[16,1664]{1,0:T(8,128)(2,1)S(1)} %get-tuple-element.37), channel_id=1, source_target_pairs={{0,6},{2,0},{4,2},{6,4},{1,7},{3,1},{5,3},{7,5},{8,14},{10,8},{12,... | collective-permute-start | bytes 159752 | tf_op jit(solution)/shard_map/ppermute | solution.py:28
  10.5 1.1 %stage.1 = (bf16[1,2,8,16,1024]{4,3,2,1,0:T(8,128)(2,1)S(1)}, bf16[256,720]{1,0:T(8,128)(2,1)S(1)}) custom-call(s32[1,2]{1,0:T(1,128)S(1)} %copy-done.2, bf16[1,2,8,16,1024]{4,3,2,1,0:T(8,128)(2,1)} %tok_hbm), custom_call_target="tpu_custom_call" | custom-call | flops 1 | bytes 1 | tf_op jit(solution)/shard_map/stage/pallas_call | solution.py:145
  13.2 1.3 %collective-permute-start.3 = (bf16[112,1024]{1,0:T(8,128)(2,1)S(1)}, bf16[112,1024]{1,0:T(8,128)(2,1)S(1)}, u32[]{:S(2)}, u32[]{:S(2)}) collective-permute-start(bf16[112,1024]{1,0:T(8,128)(2,1)S(1)} %get-tuple-element.42), channel_id=1, source_target_pairs={{2,0},{4,2},{6,4},{3,1},{5,3},{7,5},{10,8},{12,10},{14,12},{11,9},... | collective-permute-start | bytes 688136 | tf_op jit(solution)/shard_map/ppermute | solution.py:23
  14.5 1.7 %collective-permute-start.7 = (bf16[1,2,8,16,1024]{4,3,2,1,0:T(8,128)(2,1)}, bf16[1,2,8,16,1024]{4,3,2,1,0:T(8,128)(2,1)S(1)}, u32[]{:S(2)}, u32[]{:S(2)}) collective-permute-start(bf16[1,2,8,16,1024]{4,3,2,1,0:T(8,128)(2,1)} %cot_ref.1), channel_id=1, source_target_pairs={{0,1},{1,0},{2,3},{3,2},{4,5},{5,4},{6,7},{7,6},{8,9},{9,8},{10,11... | collective-permute-start | bytes 1572872 | tf_op jit(solution)/shard_map/ppermute | solution.py:33
  16.2 2.8 %weights.1 = (bf16[1024,3072]{1,0:T(8,128)(2,1)S(1)}, f32[1,1024]{1,0:T(1,128)S(1)}) custom-call(bf16[1024,3072]{1,0:T(8,128)(2,1)} %refs_0_, f32[1,1024]{1,0:T(1,128)} %bitcast.7), custom_call_target="tpu_custom_call" | custom-call | flops 1 | bytes 1 | tf_op jit(solution)/shard_map/weights/pallas_call | solution.py:145
  19.0 1.3 %collective-permute-start.4 = (bf16[112,1024]{1,0:T(8,128)(2,1)S(1)}, bf16[112,1024]{1,0:T(8,128)(2,1)S(1)}, u32[]{:S(2)}, u32[]{:S(2)}) collective-permute-start(bf16[112,1024]{1,0:T(8,128)(2,1)S(1)} %get-tuple-element.44), channel_id=1, source_target_pairs={{2,0},{4,2},{6,4},{3,1},{5,3},{7,5},{10,8},{12,10},{14,12},{11,9},... | collective-permute-start | bytes 688136 | tf_op jit(solution)/shard_map/ppermute | solution.py:23
  20.3 1.3 %collective-permute-done.3.refs_1_ = bf16[112,1024]{1,0:T(8,128)(2,1)S(1)} collective-permute-done((bf16[112,1024]{1,0:T(8,128)(2,1)S(1)}, bf16[112,1024]{1,0:T(8,128)(2,1)S(1)}, u32[]{:S(2)}, u32[]{:S(2)}) %collective-permute-start.3) | collective-permute-done | bytes 229408 | tf_op jit(solution)/shard_map/ppermute | solution.py:23
  22.0 7.8 %collective-permute-done.4.refs_2_ = bf16[112,1024]{1,0:T(8,128)(2,1)S(1)} collective-permute-done((bf16[112,1024]{1,0:T(8,128)(2,1)S(1)}, bf16[112,1024]{1,0:T(8,128)(2,1)S(1)}, u32[]{:S(2)}, u32[]{:S(2)}) %collective-permute-start.4) | collective-permute-done | bytes 229408 | tf_op jit(solution)/shard_map/ppermute | solution.py:23
  29.8 0.8 %region.1 = (bf16[256,1024]{1,0:T(8,128)(2,1)S(1)}, bf16[256,1024]{1,0:T(8,128)(2,1)S(1)}) custom-call(bf16[256,720]{1,0:T(8,128)(2,1)S(1)} %get-tuple-element.33.pick_ref, f32[1,1024]{1,0:T(1,128)S(1)} %get-tuple-element.41.gain_ref, bf16[256,1024]{1,0:T(8,128)(2,1)S(1)} %get-tuple-element.38.refs_0_, bf16[112,1024]{1,0:T(8,128)(2,1)S(1)} %collective-permute-done.3.refs_1_, ...), custom_call_target="tpu_custom_call" | custom-call | flops 1 | bytes 1 | tf_op jit(solution)/shard_map/region/pallas_call | solution.py:145
  30.7 1.5 %attend11.1.refs_0_ = bf16[256,256]{1,0:T(8,128)(2,1)S(1)} custom-call(bf16[256,1024]{1,0:T(8,128)(2,1)S(1)} %get-tuple-element.51.normed_ref, bf16[1024,3072]{1,0:T(8,128)(2,1)S(1)} %get-tuple-element.48.wqkv_ref, s32[1,2]{1,0:T(1,128)S(1)} %copy-done.3), custom_call_target="tpu_custom_call" | custom-call | flops 1 | bytes 1 | tf_op jit(solution)/shard_map/attend11/pallas_call | solution.py:145
  32.6 1.5 %attend10.1.refs_2_ = bf16[256,256]{1,0:T(8,128)(2,1)S(1)} custom-call(bf16[256,1024]{1,0:T(8,128)(2,1)S(1)} %get-tuple-element.51.normed_ref, bf16[1024,3072]{1,0:T(8,128)(2,1)S(1)} %get-tuple-element.48.wqkv_ref, s32[1,2]{1,0:T(1,128)S(1)} %copy-done.3), custom_call_target="tpu_custom_call" | custom-call | flops 1 | bytes 1 | tf_op jit(solution)/shard_map/attend10/pallas_call | solution.py:145
  34.1 1.7 %collective-permute-start.13 = (bf16[256,256]{1,0:T(8,128)(2,1)S(1)}, bf16[256,256]{1,0:T(8,128)(2,1)S(1)}, u32[]{:S(2)}, u32[]{:S(2)}) collective-permute-start(bf16[256,256]{1,0:T(8,128)(2,1)S(1)} %attend10.1.refs_2_), channel_id=1, source_target_pairs={{0,1},{1,0},{2,3},{3,2},{4,5},{5,4},{6,7},{7,6},{8,9},{9,8},{10,11... | collective-permute-start | bytes 393224 | tf_op jit(solution)/shard_map/ppermute | solution.py:33
  35.9 1.5 %attend01.1.refs_1_.mine_ref = bf16[256,256]{1,0:T(8,128)(2,1)S(1)} custom-call(bf16[256,1024]{1,0:T(8,128)(2,1)S(1)} %get-tuple-element.51.normed_ref, bf16[1024,3072]{1,0:T(8,128)(2,1)S(1)} %get-tuple-element.48.wqkv_ref, s32[1,2]{1,0:T(1,128)S(1)} %copy-done.3), custom_call_target="tpu_custom_call" | custom-call | flops 1 | bytes 1 | tf_op jit(solution)/shard_map/attend01/pallas_call | solution.py:145
  37.4 1.5 %attend00.1.refs_3_.mine_ref = bf16[256,256]{1,0:T(8,128)(2,1)S(1)} custom-call(bf16[256,1024]{1,0:T(8,128)(2,1)S(1)} %get-tuple-element.51.normed_ref, bf16[1024,3072]{1,0:T(8,128)(2,1)S(1)} %get-tuple-element.48.wqkv_ref, s32[1,2]{1,0:T(1,128)S(1)} %copy-done.3), custom_call_target="tpu_custom_call" | custom-call | flops 1 | bytes 1 | tf_op jit(solution)/shard_map/attend00/pallas_call | solution.py:145
  41.6 1.6 %collective-permute-start.10 = (bf16[1,256,256]{2,1,0:T(8,128)(2,1)S(1)}, bf16[1,256,256]{2,1,0:T(8,128)(2,1)S(1)}, u32[]{:S(2)}, u32[]{:S(2)}) collective-permute-start(bf16[1,256,256]{2,1,0:T(8,128)(2,1)S(1)} %slice.60), channel_id=1, source_target_pairs={{0,16},{8,24},{16,0},{24,8},{1,17},{9,25},{17,1},{25,9},{2,18},{10... | collective-permute-start | bytes 393224 | tf_op jit(solution)/shard_map/ppermute | solution.py:33
  43.2 0.9 %collective-permute-start.15 = (bf16[1,256,256]{2,1,0:T(8,128)(2,1)S(1)}, bf16[1,256,256]{2,1,0:T(8,128)(2,1)S(1)}, u32[]{:S(2)}, u32[]{:S(2)}) collective-permute-start(bf16[1,256,256]{2,1,0:T(8,128)(2,1)S(1)} %slice.59), channel_id=1, source_target_pairs={{0,16},{8,24},{16,0},{24,8},{1,17},{9,25},{17,1},{25,9},{2,18},{10... | collective-permute-start | bytes 393224 | tf_op jit(solution)/shard_map/ppermute | solution.py:33
  44.1 3.9 %collective-permute-done.10 = bf16[1,256,256]{2,1,0:T(8,128)(2,1)S(1)} collective-permute-done((bf16[1,256,256]{2,1,0:T(8,128)(2,1)S(1)}, bf16[1,256,256]{2,1,0:T(8,128)(2,1)S(1)}, u32[]{:S(2)}, u32[]{:S(2)}) %collective-permute-start.10) | collective-permute-done | bytes 131104 | tf_op jit(solution)/shard_map/ppermute | solution.py:33
  48.0 1.8 %collective-permute-start.11 = (bf16[256,128]{1,0:T(8,128)(2,1)S(1)}, bf16[256,128]{1,0:T(8,128)(2,1)S(1)}, u32[]{:S(2)}, u32[]{:S(2)}) collective-permute-start(bf16[256,128]{1,0:T(8,128)(2,1)S(1)} %get-tuple-element.58), channel_id=1, source_target_pairs={{0,2},{2,4},{4,6},{6,0},{1,3},{3,5},{5,7},{7,1},{8,10},{10,12},{12... | collective-permute-start | bytes 196616 | tf_op jit(solution)/shard_map/ppermute | solution.py:28
  50.2 2.9 %collective-permute-start.16 = (bf16[256,128]{1,0:T(8,128)(2,1)S(1)}, bf16[256,128]{1,0:T(8,128)(2,1)S(1)}, u32[]{:S(2)}, u32[]{:S(2)}) collective-permute-start(bf16[256,128]{1,0:T(8,128)(2,1)S(1)} %slice.61), channel_id=1, source_target_pairs={{0,6},{2,0},{4,2},{6,4},{1,7},{3,1},{5,3},{7,5},{8,14},{10,8},{12,... | collective-permute-start | bytes 196616 | tf_op jit(solution)/shard_map/ppermute | solution.py:28
  53.1 1.5 %project.1 = bf16[1,2,8,16,1024]{4,3,2,1,0:T(8,128)(2,1)} custom-call(bf16[256,1024]{1,0:T(8,128)(2,1)S(1)} %get-tuple-element.46.reg_ref, bf16[1024,1024]{1,0:T(8,128)(2,1)S(1)} %copy-done, bf16[256,256]{1,0:T(8,128)(2,1)S(1)} %attend11.1.refs_0_, bf16[256,256]{1,0:T(8,128)(2,1)S(1)} %attend01.1.refs_1_.mine_ref, bf16[256,256]{1,0:T(8,128)(2,1)S(1)} %attend10.1.refs_2_, ...), custom_call_target="tpu_custom_call" | custom-call | flops 1 | bytes 1 | tf_op jit(solution)/shard_map/project/pallas_call | solution.py:145
  54.9 1.1 %collective-permute-done.12 = bf16[256,128]{1,0:T(8,128)(2,1)S(1)} collective-permute-done((bf16[256,128]{1,0:T(8,128)(2,1)S(1)}, bf16[256,128]{1,0:T(8,128)(2,1)S(1)}, u32[]{:S(2)}, u32[]{:S(2)}) %collective-permute-start.12) | collective-permute-done | bytes 65568 | tf_op jit(solution)/shard_map/ppermute | solution.py:28
  (40 shorter events, 7.1 us)
Async XLA Ops:
  0.6 30.0 %copy-start.3 = (s32[1,2]{1,0:T(1,128)S(1)}, s32[1,2]{1,0:T(1,128)}, u32[]{:S(2)}) copy-start(s32[1,2]{1,0:T(1,128)} %shift_ref.4) | copy-start | bytes 28
  2.8 8.7 %collective-permute-start = (bf16[16,1664]{1,0:T(8,128)(2,1)S(1)}, bf16[16,1664]{1,0:T(8,128)(2,1)S(1)}, u32[]{:S(2)}, u32[]{:S(2)}) collective-permute-start(bf16[16,1664]{1,0:T(8,128)(2,1)S(1)} %get-tuple-element.35), channel_id=1, source_target_pairs={{0,2},{2,4},{4,6},{6,0},{1,3},{3,5},{5,7},{7,1},{8,10},{10,12},{12... | collective-permute-start | bytes 159752 | tf_op jit(solution)/shard_map/ppermute | solution.py:28
  5.9 6.4 %collective-permute-start.1 = (bf16[16,1664]{1,0:T(8,128)(2,1)S(1)}, bf16[16,1664]{1,0:T(8,128)(2,1)S(1)}, u32[]{:S(2)}, u32[]{:S(2)}) collective-permute-start(bf16[16,1664]{1,0:T(8,128)(2,1)S(1)} %get-tuple-element.36), channel_id=1, source_target_pairs={{0,4},{2,6},{4,0},{6,2},{1,5},{3,7},{5,1},{7,3},{8,12},{10,14},{12... | collective-permute-start | bytes 159752 | tf_op jit(solution)/shard_map/ppermute | solution.py:28
  8.5 4.3 %collective-permute-start.2 = (bf16[16,1664]{1,0:T(8,128)(2,1)S(1)}, bf16[16,1664]{1,0:T(8,128)(2,1)S(1)}, u32[]{:S(2)}, u32[]{:S(2)}) collective-permute-start(bf16[16,1664]{1,0:T(8,128)(2,1)S(1)} %get-tuple-element.37), channel_id=1, source_target_pairs={{0,6},{2,0},{4,2},{6,4},{1,7},{3,1},{5,3},{7,5},{8,14},{10,8},{12,... | collective-permute-start | bytes 159752 | tf_op jit(solution)/shard_map/ppermute | solution.py:28
  9.8 0.7 %copy-start.2 = (s32[1,2]{1,0:T(1,128)S(1)}, s32[1,2]{1,0:T(1,128)}, u32[]{:S(2)}) copy-start(s32[1,2]{1,0:T(1,128)} %shift_ref.4) | copy-start | bytes 28
  13.2 8.5 %collective-permute-start.3 = (bf16[112,1024]{1,0:T(8,128)(2,1)S(1)}, bf16[112,1024]{1,0:T(8,128)(2,1)S(1)}, u32[]{:S(2)}, u32[]{:S(2)}) collective-permute-start(bf16[112,1024]{1,0:T(8,128)(2,1)S(1)} %get-tuple-element.42), channel_id=1, source_target_pairs={{2,0},{4,2},{6,4},{3,1},{5,3},{7,5},{10,8},{12,10},{14,12},{11,9},... | collective-permute-start | bytes 688136 | tf_op jit(solution)/shard_map/ppermute | solution.py:23
  14.5 24.4 %collective-permute-start.7 = (bf16[1,2,8,16,1024]{4,3,2,1,0:T(8,128)(2,1)}, bf16[1,2,8,16,1024]{4,3,2,1,0:T(8,128)(2,1)S(1)}, u32[]{:S(2)}, u32[]{:S(2)}) collective-permute-start(bf16[1,2,8,16,1024]{4,3,2,1,0:T(8,128)(2,1)} %cot_ref.1), channel_id=1, source_target_pairs={{0,1},{1,0},{2,3},{3,2},{4,5},{5,4},{6,7},{7,6},{8,9},{9,8},{10,11... | collective-permute-start | bytes 1572872 | tf_op jit(solution)/shard_map/ppermute | solution.py:33
  16.2 13.6 %collective-permute-start.5 = (bf16[128,1024]{1,0:T(8,128)(2,1)S(1)}, bf16[128,1024]{1,0:T(8,128)(2,1)S(1)}, u32[]{:S(2)}, u32[]{:S(2)}) collective-permute-start(bf16[128,1024]{1,0:T(8,128)(2,1)S(1)} %get-tuple-element.45), channel_id=1, source_target_pairs={{0,24},{8,0},{16,8},{24,16},{1,25},{9,1},{17,9},{25,17},{2,26},{10... | collective-permute-start | bytes 786440 | tf_op jit(solution)/shard_map/ppermute | solution.py:28
  19.0 10.8 %collective-permute-start.4 = (bf16[112,1024]{1,0:T(8,128)(2,1)S(1)}, bf16[112,1024]{1,0:T(8,128)(2,1)S(1)}, u32[]{:S(2)}, u32[]{:S(2)}) collective-permute-start(bf16[112,1024]{1,0:T(8,128)(2,1)S(1)} %get-tuple-element.44), channel_id=1, source_target_pairs={{2,0},{4,2},{6,4},{3,1},{5,3},{7,5},{10,8},{12,10},{14,12},{11,9},... | collective-permute-start | bytes 688136 | tf_op jit(solution)/shard_map/ppermute | solution.py:23
  21.6 8.2 %collective-permute-start.6 = (bf16[112,1024]{1,0:T(8,128)(2,1)S(1)}, bf16[112,1024]{1,0:T(8,128)(2,1)S(1)}, u32[]{:S(2)}, u32[]{:S(2)}) collective-permute-start(bf16[112,1024]{1,0:T(8,128)(2,1)S(1)} %collective-permute-done.3.refs_1_), channel_id=1, source_target_pairs={{0,24},{8,0},{16,8},{24,16},{1,25},{9,1},{17,9},{25,17},{2,26},{10... | collective-permute-start | bytes 688136 | tf_op jit(solution)/shard_map/ppermute | solution.py:28
  32.2 7.2 %collective-permute-start.8 = (bf16[256,256]{1,0:T(8,128)(2,1)S(1)}, bf16[256,256]{1,0:T(8,128)(2,1)S(1)}, u32[]{:S(2)}, u32[]{:S(2)}) collective-permute-start(bf16[256,256]{1,0:T(8,128)(2,1)S(1)} %attend11.1.refs_0_), channel_id=1, source_target_pairs={{0,1},{1,0},{2,3},{3,2},{4,5},{5,4},{6,7},{7,6},{8,9},{9,8},{10,11... | collective-permute-start | bytes 393224 | tf_op jit(solution)/shard_map/ppermute | solution.py:33
  34.1 4.8 %copy-start.1 = (bf16[1,2,8,16,1024]{4,3,2,1,0:T(8,128)(2,1)S(1)}, bf16[1,2,8,16,1024]{4,3,2,1,0:T(8,128)(2,1)}, u32[]{:S(2)}) copy-start(bf16[1,2,8,16,1024]{4,3,2,1,0:T(8,128)(2,1)} %cot_ref.1) | copy-start | bytes 1572868
  34.1 6.3 %collective-permute-start.13 = (bf16[256,256]{1,0:T(8,128)(2,1)S(1)}, bf16[256,256]{1,0:T(8,128)(2,1)S(1)}, u32[]{:S(2)}, u32[]{:S(2)}) collective-permute-start(bf16[256,256]{1,0:T(8,128)(2,1)S(1)} %attend10.1.refs_2_), channel_id=1, source_target_pairs={{0,1},{1,0},{2,3},{3,2},{4,5},{5,4},{6,7},{7,6},{8,9},{9,8},{10,11... | collective-permute-start | bytes 393224 | tf_op jit(solution)/shard_map/ppermute | solution.py:33
  39.9 13.3 %copy-start = (bf16[1024,1024]{1,0:T(8,128)(2,1)S(1)}, bf16[1024,1024]{1,0:T(8,128)(2,1)}, u32[]{:S(2)}) copy-start(bf16[1024,1024]{1,0:T(8,128)(2,1)} %wout_ref.1) | copy-start | bytes 6291460
  39.9 1.6 %collective-permute-start.9 = (bf16[2,256,256]{2,1,0:T(8,128)(2,1)S(1)}, bf16[2,256,256]{2,1,0:T(8,128)(2,1)S(1)}, u32[]{:S(2)}, u32[]{:S(2)}) collective-permute-start(bf16[2,256,256]{2,1,0:T(8,128)(2,1)S(1)} %get-tuple-element.54), channel_id=1, source_target_pairs={{0,8},{8,0},{16,24},{24,16},{1,9},{9,1},{17,25},{25,17},{2,10},{10... | collective-permute-start | bytes 786440 | tf_op jit(solution)/shard_map/ppermute | solution.py:33
  40.8 2.3 %collective-permute-start.14 = (bf16[2,256,256]{2,1,0:T(8,128)(2,1)S(1)}, bf16[2,256,256]{2,1,0:T(8,128)(2,1)S(1)}, u32[]{:S(2)}, u32[]{:S(2)}) collective-permute-start(bf16[2,256,256]{2,1,0:T(8,128)(2,1)S(1)} %get-tuple-element.57), channel_id=1, source_target_pairs={{0,8},{8,0},{16,24},{24,16},{1,9},{9,1},{17,25},{25,17},{2,10},{10... | collective-permute-start | bytes 786440 | tf_op jit(solution)/shard_map/ppermute | solution.py:33
  41.6 6.4 %collective-permute-start.10 = (bf16[1,256,256]{2,1,0:T(8,128)(2,1)S(1)}, bf16[1,256,256]{2,1,0:T(8,128)(2,1)S(1)}, u32[]{:S(2)}, u32[]{:S(2)}) collective-permute-start(bf16[1,256,256]{2,1,0:T(8,128)(2,1)S(1)} %slice.60), channel_id=1, source_target_pairs={{0,16},{8,24},{16,0},{24,8},{1,17},{9,25},{17,1},{25,9},{2,18},{10... | collective-permute-start | bytes 393224 | tf_op jit(solution)/shard_map/ppermute | solution.py:33
  43.2 7.0 %collective-permute-start.15 = (bf16[1,256,256]{2,1,0:T(8,128)(2,1)S(1)}, bf16[1,256,256]{2,1,0:T(8,128)(2,1)S(1)}, u32[]{:S(2)}, u32[]{:S(2)}) collective-permute-start(bf16[1,256,256]{2,1,0:T(8,128)(2,1)S(1)} %slice.59), channel_id=1, source_target_pairs={{0,16},{8,24},{16,0},{24,8},{1,17},{9,25},{17,1},{25,9},{2,18},{10... | collective-permute-start | bytes 393224 | tf_op jit(solution)/shard_map/ppermute | solution.py:33
  48.0 6.9 %collective-permute-start.11 = (bf16[256,128]{1,0:T(8,128)(2,1)S(1)}, bf16[256,128]{1,0:T(8,128)(2,1)S(1)}, u32[]{:S(2)}, u32[]{:S(2)}) collective-permute-start(bf16[256,128]{1,0:T(8,128)(2,1)S(1)} %get-tuple-element.58), channel_id=1, source_target_pairs={{0,2},{2,4},{4,6},{6,0},{1,3},{3,5},{5,7},{7,1},{8,10},{10,12},{12... | collective-permute-start | bytes 196616 | tf_op jit(solution)/shard_map/ppermute | solution.py:28
  49.8 6.2 %collective-permute-start.12 = (bf16[256,128]{1,0:T(8,128)(2,1)S(1)}, bf16[256,128]{1,0:T(8,128)(2,1)S(1)}, u32[]{:S(2)}, u32[]{:S(2)}) collective-permute-start(bf16[256,128]{1,0:T(8,128)(2,1)S(1)} %get-tuple-element.59), channel_id=1, source_target_pairs={{0,4},{2,6},{4,0},{6,2},{1,5},{3,7},{5,1},{7,3},{8,12},{10,14},{12... | collective-permute-start | bytes 196616 | tf_op jit(solution)/shard_map/ppermute | solution.py:28
  50.2 5.7 %collective-permute-start.16 = (bf16[256,128]{1,0:T(8,128)(2,1)S(1)}, bf16[256,128]{1,0:T(8,128)(2,1)S(1)}, u32[]{:S(2)}, u32[]{:S(2)}) collective-permute-start(bf16[256,128]{1,0:T(8,128)(2,1)S(1)} %slice.61), channel_id=1, source_target_pairs={{0,6},{2,0},{4,2},{6,4},{1,7},{3,1},{5,3},{7,5},{8,14},{10,8},{12,... | collective-permute-start | bytes 196616 | tf_op jit(solution)/shard_map/ppermute | solution.py:28

commit v3 on v2

--- a/solution.py
+++ b/solution.py
@@ -429,14 +429,14 @@
         [VMEM_SPEC] * (1 + n_lat),
         "enrich",
     )
-    loaded = (w_qkv, norm_gain.reshape(1, -1))
-    loaded = lax.optimization_barrier((own, *loaded))[1:]
-    w_qkv, gain = load(loaded, "weights")
     north0 = from_behind(north0, "lat", -1)
-    north1 = from_behind(lax.optimization_barrier((north1, gain))[0], "lat", -1)
+    north1 = from_behind(north1, "lat", -1)
     east = shifted(east, "lon", -1)
     cot_other = swapped(cotangent, "dp", 1)
     corner = shifted(north0, "lon", -1)
+    loaded = (w_qkv, w_out, norm_gain.reshape(1, -1))
+    loaded = lax.optimization_barrier((north0, *loaded))[1:]
+    w_qkv, w_out, gain = load(loaded, "weights")
     region, normed = call(
         region_body,
         [shape((n_rows, d_model), BF16)] * 2,
@@ -453,6 +453,7 @@
             (normed, w_qkv, shift_offsets),
             [VMEM_SPEC] * 3,
             f"attend{part}{turns[0]}",
+            flops=SLOW if (part, turns) == (0, second) else 1,
         )
 
     def local_gradient(turns, mine, other, cost):
@@ -466,23 +467,25 @@
             flops=cost,
         )
 
+    def halves(total):
+        middle = total.shape[0] // 2
+        return total[:middle], total[middle:].astype(BF16)
+
     def fold(kept, sent, bit):
-        total = kept + swapped(sent, "lon", bit).astype(F32)
-        middle = total.shape[0] // 2
-        return (total[:middle], total[middle:].astype(BF16)) if middle else (total, None)
-
-    def over_lon(kept, sent, bit):
+        return kept + swapped(sent, "lon", bit).astype(F32)
+
+    def over_lon(total, bit):
         while bit < n_lon:
-            kept, sent = fold(kept, sent, bit)
+            total = fold(*halves(total), bit)
             bit *= 2
-        return kept[0]
+        return total
 
     def over_lat(total, turns):
         blocks = []
         for i, k in enumerate(turns):
-            block = total[:, i * d_blk : (i + 1) * d_blk]
+            block = total[..., i * d_blk : (i + 1) * d_blk]
             blocks.append(shifted(block.astype(BF16), "lat", k).astype(F32) if k else block)
-        return blocks
+        return functools.reduce(jnp.add, blocks)
 
     def after(array, *others):
         return lax.optimization_barrier((array, *others))[0]
@@ -500,21 +503,25 @@
     theirs1 = attend(after(normed, theirs0), 1, second)
     got1 = swapped(theirs1, "dp", 1)
     mine0 = attend(after(normed, theirs1), 0, first)
-    mine1 = attend(after(normed, mine0), 0, second)
-    kept0, sent0 = local_gradient(first, mine0, after(got0, mine1), 1)
+    kept0, sent0 = local_gradient(first, mine0, got0, 1)
+    mine1 = attend(after(normed, sent0), 0, second)
+    kept0, sent0 = halves(fold(after(kept0, mine1), sent0, 1))
     kept1, sent1 = local_gradient(second, mine1, after(got1, sent0), SLOW)
-    total0 = over_lon(kept0, sent0, 1)
-    total1 = over_lon(kept1, sent1, 1)
-    blocks = over_lat(total0, first) + over_lat(total1, second)
-    gradient = functools.reduce(jnp.add, blocks)
+    kept1, sent1 = halves(fold(kept1, sent1, 1))
     groups = [(1, first), (0, first), (1, second), (0, second)]
     block_out = call(
         functools.partial(project_body, groups, n_lat, n_dp),
         shape((1, levels, lat_dev, lon_dev, d_model), BF16),
-        (region, w_out, theirs0, mine0, theirs1, mine1),
+        (after(region, sent0), w_out, theirs0, mine0, theirs1, mine1),
         [VMEM_SPEC] * 6,
         "project",
-    )
+        flops=SLOW,
+    )
+    total0 = fold(after(kept0, block_out, sent1), sent0, 2)
+    total1 = fold(kept1, sent1, 2)
+    gradient = over_lat(over_lon(total0, 4), first)
+    gradient, total1 = lax.optimization_barrier((gradient, over_lat(over_lon(total1, 4), second)))
+    gradient = (gradient + total1)[0]
     return (block_out, gradient)
 
 

time: 56.9 us -> 53.5 us (0.940)
  waiting for transfers between devices: 16.6 us -> 13 us
  Pallas kernels: 15.5 us -> 16.1 us
    ppermute x2, waiting for transfers between devices: 9.2 us -> 6.07 us  [from_behind(): return lax.ppermute(array, axis, pairs)]
    ppermute x7, waiting for transfers between devices: 4.86 us -> 2.84 us  [swapped(): return lax.ppermute(array, axis, [(i, i ^ bit) for i in range(devices)])]
    ppermute x8, waiting for transfers between devices: 2.53 us -> 4.08 us  [shifted(): lax.ppermute(array, axis, [(i, (i + by) % devices) for i in range(devices)])]
    ppermute x8, starting transfers between devices: 12.4 us -> 11.7 us  [shifted(): lax.ppermute(array, axis, [(i, (i + by) % devices) for i in range(devices)])]
    squeeze x1, other arithmetic: 0.02 us -> 0.67 us  [fast_program(): gradient = (gradient + total1)[0]]
    pallas_call x13, Pallas kernels: 15.5 us -> 16.1 us  [call(): pl.pallas_call(body, out_shape=out_shape, in_specs=specs, out_specs=jax.t...]
    add x3 -> x5, other arithmetic: 0.79 us -> 0.17 us  [the longest x3 0.14 us: fold(): return kept + swapped(sent, 'lon', bit).astype(F32)]
  transfers between devices with their start and end apart: 17 -> 17, of which waited for: 9 -> 8; matrix products, arithmetic and copies ran while one was open for 0% -> 0% of each run, Pallas kernels for 24% -> 27%
where the time goes in v3:
time: 53.5 us; the launch traced here: 53.3 us
  starting transfers between devices  21 us (39%)
  Pallas kernels  16.1 us (30%)
  waiting for transfers between devices  13 us (24%)
  between operations  1.56 us (3%)
  other arithmetic  0.87 us (2%)
  local copies, waits for them, and re-layouts  0.73 us (1%)
    pallas_call x13, Pallas kernels, call(): pl.pallas_call(body, out_shape=out_shape, in_specs=specs, out_specs=jax.t...  16.1 us
    ppermute x8, starting transfers between devices, shifted(): lax.ppermute(array, axis, [(i, (i + by) % devices) for i in range(devices)])  11.7 us
    ppermute x7, starting transfers between devices, swapped(): return lax.ppermute(array, axis, [(i, i ^ bit) for i in range(devices)])  6.79 us
    ppermute x2, waiting for transfers between devices, from_behind(): return lax.ppermute(array, axis, pairs)  6.07 us
    ppermute x8, waiting for transfers between devices, shifted(): lax.ppermute(array, axis, [(i, (i + by) % devices) for i in range(devices)])  4.08 us
    ppermute x7, waiting for transfers between devices, swapped(): return lax.ppermute(array, axis, [(i, i ^ bit) for i in range(devices)])  2.84 us
    ppermute x2, starting transfers between devices, from_behind(): return lax.ppermute(array, axis, pairs)  2.57 us
  transfers between devices with their start and end apart: 17, of which 8 were waited for; matrix products, arithmetic and copies ran while one was open for 0% of the time, Pallas kernels for 27%

profile of v3, /device:TPU:0, one launch (start us, length us, event | category | flops | bytes accessed | tf_op | source)
XLA Modules:
  0.0 53.3 jit_solution(8109229806887184777)
XLA Ops:
  1.3 1.5 %route.1 = (bf16[16,1664]{1,0:T(8,128)(2,1)S(1)}, bf16[16,1664]{1,0:T(8,128)(2,1)S(1)}, bf16[16,1664]{1,0:T(8,128)(2,1)S(1)}, bf16[16,1664]{1,0:T(8,128)(2,1)S(1)}) custom-call(s32[1]{0:T(128)S(6)} %copy.12.count_ref, s32[1,64]{1,0:T(1,128)} %bitcast.6, s32[1,64]{1,0:T(1,128)} %bitcast.7, bf16[64,1024]{1,0:T(8,128)(2,1)} %vec_hbm.1), custom_call_target="tpu_custom_call" | custom-call | flops 1 | bytes 1 | tf_op jit(solution)/shard_map/route/pallas_call | solution.py:145
  2.8 3.1 %collective-permute-start = (bf16[16,1664]{1,0:T(8,128)(2,1)S(1)}, bf16[16,1664]{1,0:T(8,128)(2,1)S(1)}, u32[]{:S(2)}, u32[]{:S(2)}) collective-permute-start(bf16[16,1664]{1,0:T(8,128)(2,1)S(1)} %get-tuple-element.40), channel_id=1, source_target_pairs={{0,2},{2,4},{4,6},{6,0},{1,3},{3,5},{5,7},{7,1},{8,10},{10,12},{12... | collective-permute-start | bytes 159752 | tf_op jit(solution)/shard_map/ppermute | solution.py:28
  5.9 2.6 %collective-permute-start.1 = (bf16[16,1664]{1,0:T(8,128)(2,1)S(1)}, bf16[16,1664]{1,0:T(8,128)(2,1)S(1)}, u32[]{:S(2)}, u32[]{:S(2)}) collective-permute-start(bf16[16,1664]{1,0:T(8,128)(2,1)S(1)} %get-tuple-element.41), channel_id=1, source_target_pairs={{0,4},{2,6},{4,0},{6,2},{1,5},{3,7},{5,1},{7,3},{8,12},{10,14},{12... | collective-permute-start | bytes 159752 | tf_op jit(solution)/shard_map/ppermute | solution.py:28
  8.5 1.3 %collective-permute-start.2 = (bf16[16,1664]{1,0:T(8,128)(2,1)S(1)}, bf16[16,1664]{1,0:T(8,128)(2,1)S(1)}, u32[]{:S(2)}, u32[]{:S(2)}) collective-permute-start(bf16[16,1664]{1,0:T(8,128)(2,1)S(1)} %get-tuple-element.42), channel_id=1, source_target_pairs={{0,6},{2,0},{4,2},{6,4},{1,7},{3,1},{5,3},{7,5},{8,14},{10,8},{12,... | collective-permute-start | bytes 159752 | tf_op jit(solution)/shard_map/ppermute | solution.py:28
  10.5 1.1 %stage.1 = (bf16[1,2,8,16,1024]{4,3,2,1,0:T(8,128)(2,1)S(1)}, bf16[256,720]{1,0:T(8,128)(2,1)S(1)}) custom-call(s32[1,2]{1,0:T(1,128)S(1)} %copy-done.1, bf16[1,2,8,16,1024]{4,3,2,1,0:T(8,128)(2,1)} %tok_hbm), custom_call_target="tpu_custom_call" | custom-call | flops 1 | bytes 1 | tf_op jit(solution)/shard_map/stage/pallas_call | solution.py:145
  13.2 1.3 %collective-permute-start.3 = (bf16[112,1024]{1,0:T(8,128)(2,1)S(1)}, bf16[112,1024]{1,0:T(8,128)(2,1)S(1)}, u32[]{:S(2)}, u32[]{:S(2)}) collective-permute-start(bf16[112,1024]{1,0:T(8,128)(2,1)S(1)} %get-tuple-element.43), channel_id=1, source_target_pairs={{2,0},{4,2},{6,4},{3,1},{5,3},{7,5},{10,8},{12,10},{14,12},{11,9},... | collective-permute-start | bytes 688136 | tf_op jit(solution)/shard_map/ppermute | solution.py:23
  14.5 1.7 %collective-permute-start.7 = (bf16[1,2,8,16,1024]{4,3,2,1,0:T(8,128)(2,1)}, bf16[1,2,8,16,1024]{4,3,2,1,0:T(8,128)(2,1)S(1)}, u32[]{:S(2)}, u32[]{:S(2)}) collective-permute-start(bf16[1,2,8,16,1024]{4,3,2,1,0:T(8,128)(2,1)} %cot_ref.1), channel_id=1, source_target_pairs={{0,1},{1,0},{2,3},{3,2},{4,5},{5,4},{6,7},{7,6},{8,9},{9,8},{10,11... | collective-permute-start | bytes 1572872 | tf_op jit(solution)/shard_map/ppermute | solution.py:33
  16.2 1.3 %collective-permute-start.4 = (bf16[112,1024]{1,0:T(8,128)(2,1)S(1)}, bf16[112,1024]{1,0:T(8,128)(2,1)S(1)}, u32[]{:S(2)}, u32[]{:S(2)}) collective-permute-start(bf16[112,1024]{1,0:T(8,128)(2,1)S(1)} %get-tuple-element.49), channel_id=1, source_target_pairs={{2,0},{4,2},{6,4},{3,1},{5,3},{7,5},{10,8},{12,10},{14,12},{11,9},... | collective-permute-start | bytes 688136 | tf_op jit(solution)/shard_map/ppermute | solution.py:23
  17.5 4.2 %collective-permute-done.3.refs_1_ = bf16[112,1024]{1,0:T(8,128)(2,1)S(1)} collective-permute-done((bf16[112,1024]{1,0:T(8,128)(2,1)S(1)}, bf16[112,1024]{1,0:T(8,128)(2,1)S(1)}, u32[]{:S(2)}, u32[]{:S(2)}) %collective-permute-start.3) | collective-permute-done | bytes 229408 | tf_op jit(solution)/shard_map/ppermute | solution.py:23
  21.6 3.4 %weights.1 = (bf16[1024,3072]{1,0:T(8,128)(2,1)S(1)}, bf16[1024,1024]{1,0:T(8,128)(2,1)S(1)}, f32[1,1024]{1,0:T(1,128)S(1)}) custom-call(bf16[1024,3072]{1,0:T(8,128)(2,1)} %refs_0_, bf16[1024,1024]{1,0:T(8,128)(2,1)} %refs_1_, f32[1,1024]{1,0:T(1,128)} %bitcast.5), custom_call_target="tpu_custom_call" | custom-call | flops 1 | bytes 1 | tf_op jit(solution)/shard_map/weights/pallas_call | solution.py:145
  25.1 1.9 %collective-permute-done.4.refs_2_ = bf16[112,1024]{1,0:T(8,128)(2,1)S(1)} collective-permute-done((bf16[112,1024]{1,0:T(8,128)(2,1)S(1)}, bf16[112,1024]{1,0:T(8,128)(2,1)S(1)}, u32[]{:S(2)}, u32[]{:S(2)}) %collective-permute-start.4) | collective-permute-done | bytes 229408 | tf_op jit(solution)/shard_map/ppermute | solution.py:23
  27.9 1.5 %attend11.1.refs_0_ = bf16[256,256]{1,0:T(8,128)(2,1)S(1)} custom-call(bf16[256,1024]{1,0:T(8,128)(2,1)S(1)} %get-tuple-element.58.normed_ref, bf16[1024,3072]{1,0:T(8,128)(2,1)S(1)} %get-tuple-element.53.wqkv_ref, s32[1,2]{1,0:T(1,128)S(1)} %copy-done.2), custom_call_target="tpu_custom_call" | custom-call | flops 1 | bytes 1 | tf_op jit(solution)/shard_map/attend11/pallas_call | solution.py:145
  30.1 1.5 %attend10.1.refs_2_ = bf16[256,256]{1,0:T(8,128)(2,1)S(1)} custom-call(bf16[256,1024]{1,0:T(8,128)(2,1)S(1)} %get-tuple-element.58.normed_ref, bf16[1024,3072]{1,0:T(8,128)(2,1)S(1)} %get-tuple-element.53.wqkv_ref, s32[1,2]{1,0:T(1,128)S(1)} %copy-done.2), custom_call_target="tpu_custom_call" | custom-call | flops 1 | bytes 1 | tf_op jit(solution)/shard_map/attend10/pallas_call | solution.py:145
  31.6 1.4 %collective-permute-start.10 = (bf16[256,256]{1,0:T(8,128)(2,1)S(1)}, bf16[256,256]{1,0:T(8,128)(2,1)S(1)}, u32[]{:S(2)}, u32[]{:S(2)}) collective-permute-start(bf16[256,256]{1,0:T(8,128)(2,1)S(1)} %attend10.1.refs_2_), channel_id=1, source_target_pairs={{0,1},{1,0},{2,3},{3,2},{4,5},{5,4},{6,7},{7,6},{8,9},{9,8},{10,11... | collective-permute-start | bytes 393224 | tf_op jit(solution)/shard_map/ppermute | solution.py:33
  33.0 1.5 %attend01.1.mine_ref.refs_1_ = bf16[256,256]{1,0:T(8,128)(2,1)S(1)} custom-call(bf16[256,1024]{1,0:T(8,128)(2,1)S(1)} %get-tuple-element.58.normed_ref, bf16[1024,3072]{1,0:T(8,128)(2,1)S(1)} %get-tuple-element.53.wqkv_ref, s32[1,2]{1,0:T(1,128)S(1)} %copy-done.2), custom_call_target="tpu_custom_call" | custom-call | flops 1 | bytes 1 | tf_op jit(solution)/shard_map/attend01/pallas_call | solution.py:145
  35.6 1.5 %attend00.1.refs_3_.mine_ref = bf16[256,256]{1,0:T(8,128)(2,1)S(1)} custom-call(bf16[256,1024]{1,0:T(8,128)(2,1)S(1)} %get-tuple-element.58.normed_ref, bf16[1024,3072]{1,0:T(8,128)(2,1)S(1)} %get-tuple-element.53.wqkv_ref, s32[1,2]{1,0:T(1,128)S(1)} %copy-done.2), custom_call_target="tpu_custom_call" | custom-call | flops 10000000000 | bytes 1 | tf_op jit(solution)/shard_map/attend00/pallas_call | solution.py:145
  37.2 2.0 %collective-permute-start.12 = (bf16[1,256,256]{2,1,0:T(8,128)(2,1)S(1)}, bf16[1,256,256]{2,1,0:T(8,128)(2,1)S(1)}, u32[]{:S(2)}, u32[]{:S(2)}) collective-permute-start(bf16[1,256,256]{2,1,0:T(8,128)(2,1)S(1)} %slice.51), channel_id=1, source_target_pairs={{0,16},{8,24},{16,0},{24,8},{1,17},{9,25},{17,1},{25,9},{2,18},{10... | collective-permute-start | bytes 393224 | tf_op jit(solution)/shard_map/ppermute | solution.py:33
  40.0 1.5 %project.1 = bf16[1,2,8,16,1024]{4,3,2,1,0:T(8,128)(2,1)} custom-call(bf16[256,1024]{1,0:T(8,128)(2,1)S(1)} %get-tuple-element.60.reg_ref, bf16[1024,1024]{1,0:T(8,128)(2,1)S(1)} %get-tuple-element.61.wout_ref, bf16[256,256]{1,0:T(8,128)(2,1)S(1)} %attend11.1.refs_0_, bf16[256,256]{1,0:T(8,128)(2,1)S(1)} %attend01.1.mine_ref.refs_1_, ...), custom_call_target="tpu_custom_call" | custom-call | flops 10000000000 | bytes 1 | tf_op jit(solution)/shard_map/project/pallas_call | solution.py:145
  42.1 1.3 %collective-permute-done.12 = bf16[1,256,256]{2,1,0:T(8,128)(2,1)S(1)} collective-permute-done((bf16[1,256,256]{2,1,0:T(8,128)(2,1)S(1)}, bf16[1,256,256]{2,1,0:T(8,128)(2,1)S(1)}, u32[]{:S(2)}, u32[]{:S(2)}) %collective-permute-start.12) | collective-permute-done | bytes 131104 | tf_op jit(solution)/shard_map/ppermute | solution.py:33
  43.4 2.3 %collective-permute-start.14 = (bf16[1,256,128]{2,1,0:T(8,128)(2,1)S(1)}, bf16[1,256,128]{2,1,0:T(8,128)(2,1)S(1)}, u32[]{:S(2)}, u32[]{:S(2)}) collective-permute-start(bf16[1,256,128]{2,1,0:T(8,128)(2,1)S(1)} %get-tuple-element.69), channel_id=1, source_target_pairs={{0,4},{2,6},{4,0},{6,2},{1,5},{3,7},{5,1},{7,3},{8,12},{10,14},{12... | collective-permute-start | bytes 196616 | tf_op jit(solution)/shard_map/ppermute | solution.py:28
  45.8 1.6 %collective-permute-done.15 = bf16[1,256,256]{2,1,0:T(8,128)(2,1)S(1)} collective-permute-done((bf16[1,256,256]{2,1,0:T(8,128)(2,1)S(1)}, bf16[1,256,256]{2,1,0:T(8,128)(2,1)S(1)}, u32[]{:S(2)}, u32[]{:S(2)}) %collective-permute-start.15) | collective-permute-done | bytes 131104 | tf_op jit(solution)/shard_map/ppermute | solution.py:33
  47.4 2.3 %collective-permute-start.16 = (bf16[1,256,128]{2,1,0:T(8,128)(2,1)S(1)}, bf16[1,256,128]{2,1,0:T(8,128)(2,1)S(1)}, u32[]{:S(2)}, u32[]{:S(2)}) collective-permute-start(bf16[1,256,128]{2,1,0:T(8,128)(2,1)S(1)} %slice.52), channel_id=1, source_target_pairs={{0,6},{2,0},{4,2},{6,4},{1,7},{3,1},{5,3},{7,5},{8,14},{10,8},{12,... | collective-permute-start | bytes 196616 | tf_op jit(solution)/shard_map/ppermute | solution.py:28
  49.7 1.1 %collective-permute-done.14 = bf16[1,256,128]{2,1,0:T(8,128)(2,1)S(1)} collective-permute-done((bf16[1,256,128]{2,1,0:T(8,128)(2,1)S(1)}, bf16[1,256,128]{2,1,0:T(8,128)(2,1)S(1)}, u32[]{:S(2)}, u32[]{:S(2)}) %collective-permute-start.14) | collective-permute-done | bytes 65568 | tf_op jit(solution)/shard_map/ppermute | solution.py:28
  50.8 1.8 %collective-permute-done.13 = bf16[1,256,128]{2,1,0:T(8,128)(2,1)S(1)} collective-permute-done((bf16[1,256,128]{2,1,0:T(8,128)(2,1)S(1)}, bf16[1,256,128]{2,1,0:T(8,128)(2,1)S(1)}, u32[]{:S(2)}, u32[]{:S(2)}) %collective-permute-start.13) | collective-permute-done | bytes 65568 | tf_op jit(solution)/shard_map/ppermute | solution.py:28
  (44 shorter events, 7.0 us)
Async XLA Ops:
  0.6 27.2 %copy-start.2 = (s32[1,2]{1,0:T(1,128)S(1)}, s32[1,2]{1,0:T(1,128)}, u32[]{:S(2)}) copy-start(s32[1,2]{1,0:T(1,128)} %shift_ref.4) | copy-start | bytes 28
  2.8 8.7 %collective-permute-start = (bf16[16,1664]{1,0:T(8,128)(2,1)S(1)}, bf16[16,1664]{1,0:T(8,128)(2,1)S(1)}, u32[]{:S(2)}, u32[]{:S(2)}) collective-permute-start(bf16[16,1664]{1,0:T(8,128)(2,1)S(1)} %get-tuple-element.40), channel_id=1, source_target_pairs={{0,2},{2,4},{4,6},{6,0},{1,3},{3,5},{5,7},{7,1},{8,10},{10,12},{12... | collective-permute-start | bytes 159752 | tf_op jit(solution)/shard_map/ppermute | solution.py:28
  5.9 6.4 %collective-permute-start.1 = (bf16[16,1664]{1,0:T(8,128)(2,1)S(1)}, bf16[16,1664]{1,0:T(8,128)(2,1)S(1)}, u32[]{:S(2)}, u32[]{:S(2)}) collective-permute-start(bf16[16,1664]{1,0:T(8,128)(2,1)S(1)} %get-tuple-element.41), channel_id=1, source_target_pairs={{0,4},{2,6},{4,0},{6,2},{1,5},{3,7},{5,1},{7,3},{8,12},{10,14},{12... | collective-permute-start | bytes 159752 | tf_op jit(solution)/shard_map/ppermute | solution.py:28
  8.5 4.3 %collective-permute-start.2 = (bf16[16,1664]{1,0:T(8,128)(2,1)S(1)}, bf16[16,1664]{1,0:T(8,128)(2,1)S(1)}, u32[]{:S(2)}, u32[]{:S(2)}) collective-permute-start(bf16[16,1664]{1,0:T(8,128)(2,1)S(1)} %get-tuple-element.42), channel_id=1, source_target_pairs={{0,6},{2,0},{4,2},{6,4},{1,7},{3,1},{5,3},{7,5},{8,14},{10,8},{12,... | collective-permute-start | bytes 159752 | tf_op jit(solution)/shard_map/ppermute | solution.py:28
  9.8 0.7 %copy-start.1 = (s32[1,2]{1,0:T(1,128)S(1)}, s32[1,2]{1,0:T(1,128)}, u32[]{:S(2)}) copy-start(s32[1,2]{1,0:T(1,128)} %shift_ref.4) | copy-start | bytes 28
  13.2 8.5 %collective-permute-start.3 = (bf16[112,1024]{1,0:T(8,128)(2,1)S(1)}, bf16[112,1024]{1,0:T(8,128)(2,1)S(1)}, u32[]{:S(2)}, u32[]{:S(2)}) collective-permute-start(bf16[112,1024]{1,0:T(8,128)(2,1)S(1)} %get-tuple-element.43), channel_id=1, source_target_pairs={{2,0},{4,2},{6,4},{3,1},{5,3},{7,5},{10,8},{12,10},{14,12},{11,9},... | collective-permute-start | bytes 688136 | tf_op jit(solution)/shard_map/ppermute | solution.py:23
  14.5 20.1 %collective-permute-start.7 = (bf16[1,2,8,16,1024]{4,3,2,1,0:T(8,128)(2,1)}, bf16[1,2,8,16,1024]{4,3,2,1,0:T(8,128)(2,1)S(1)}, u32[]{:S(2)}, u32[]{:S(2)}) collective-permute-start(bf16[1,2,8,16,1024]{4,3,2,1,0:T(8,128)(2,1)} %cot_ref.1), channel_id=1, source_target_pairs={{0,1},{1,0},{2,3},{3,2},{4,5},{5,4},{6,7},{7,6},{8,9},{9,8},{10,11... | collective-permute-start | bytes 1572872 | tf_op jit(solution)/shard_map/ppermute | solution.py:33
  16.2 10.8 %collective-permute-start.5 = (bf16[128,1024]{1,0:T(8,128)(2,1)S(1)}, bf16[128,1024]{1,0:T(8,128)(2,1)S(1)}, u32[]{:S(2)}, u32[]{:S(2)}) collective-permute-start(bf16[128,1024]{1,0:T(8,128)(2,1)S(1)} %get-tuple-element.50), channel_id=1, source_target_pairs={{0,24},{8,0},{16,8},{24,16},{1,25},{9,1},{17,9},{25,17},{2,26},{10... | collective-permute-start | bytes 786440 | tf_op jit(solution)/shard_map/ppermute | solution.py:28
  16.2 10.8 %collective-permute-start.4 = (bf16[112,1024]{1,0:T(8,128)(2,1)S(1)}, bf16[112,1024]{1,0:T(8,128)(2,1)S(1)}, u32[]{:S(2)}, u32[]{:S(2)}) collective-permute-start(bf16[112,1024]{1,0:T(8,128)(2,1)S(1)} %get-tuple-element.49), channel_id=1, source_target_pairs={{2,0},{4,2},{6,4},{3,1},{5,3},{7,5},{10,8},{12,10},{14,12},{11,9},... | collective-permute-start | bytes 688136 | tf_op jit(solution)/shard_map/ppermute | solution.py:23
  21.6 5.4 %collective-permute-start.6 = (bf16[112,1024]{1,0:T(8,128)(2,1)S(1)}, bf16[112,1024]{1,0:T(8,128)(2,1)S(1)}, u32[]{:S(2)}, u32[]{:S(2)}) collective-permute-start(bf16[112,1024]{1,0:T(8,128)(2,1)S(1)} %collective-permute-done.3.refs_1_), channel_id=1, source_target_pairs={{0,24},{8,0},{16,8},{24,16},{1,25},{9,1},{17,9},{25,17},{2,26},{10... | collective-permute-start | bytes 688136 | tf_op jit(solution)/shard_map/ppermute | solution.py:28
  29.4 5.2 %copy-start = (bf16[1,2,8,16,1024]{4,3,2,1,0:T(8,128)(2,1)S(1)}, bf16[1,2,8,16,1024]{4,3,2,1,0:T(8,128)(2,1)}, u32[]{:S(2)}) copy-start(bf16[1,2,8,16,1024]{4,3,2,1,0:T(8,128)(2,1)} %cot_ref.1) | copy-start | bytes 1572868
  29.4 5.7 %collective-permute-start.8 = (bf16[256,256]{1,0:T(8,128)(2,1)S(1)}, bf16[256,256]{1,0:T(8,128)(2,1)S(1)}, u32[]{:S(2)}, u32[]{:S(2)}) collective-permute-start(bf16[256,256]{1,0:T(8,128)(2,1)S(1)} %attend11.1.refs_0_), channel_id=1, source_target_pairs={{0,1},{1,0},{2,3},{3,2},{4,5},{5,4},{6,7},{7,6},{8,9},{9,8},{10,11... | collective-permute-start | bytes 393224 | tf_op jit(solution)/shard_map/ppermute | solution.py:33
  31.6 7.6 %collective-permute-start.10 = (bf16[256,256]{1,0:T(8,128)(2,1)S(1)}, bf16[256,256]{1,0:T(8,128)(2,1)S(1)}, u32[]{:S(2)}, u32[]{:S(2)}) collective-permute-start(bf16[256,256]{1,0:T(8,128)(2,1)S(1)} %attend10.1.refs_2_), channel_id=1, source_target_pairs={{0,1},{1,0},{2,3},{3,2},{4,5},{5,4},{6,7},{7,6},{8,9},{9,8},{10,11... | collective-permute-start | bytes 393224 | tf_op jit(solution)/shard_map/ppermute | solution.py:33
  35.5 1.6 %collective-permute-start.9 = (bf16[2,256,256]{2,1,0:T(8,128)(2,1)S(1)}, bf16[2,256,256]{2,1,0:T(8,128)(2,1)S(1)}, u32[]{:S(2)}, u32[]{:S(2)}) collective-permute-start(bf16[2,256,256]{2,1,0:T(8,128)(2,1)S(1)} %get-tuple-element.57), channel_id=1, source_target_pairs={{0,8},{8,0},{16,24},{24,16},{1,9},{9,1},{17,25},{25,17},{2,10},{10... | collective-permute-start | bytes 786440 | tf_op jit(solution)/shard_map/ppermute | solution.py:33
  37.2 2.5 %copy-start.3 = (f32[2,256,256]{2,1,0:T(8,128)}, f32[2,256,256]{2,1,0:T(8,128)S(1)}, u32[]{:S(2)}) copy-start(f32[2,256,256]{2,1,0:T(8,128)S(1)} %convert_add_fusion.1) | copy-start | bytes 1572868
  37.2 6.2 %collective-permute-start.12 = (bf16[1,256,256]{2,1,0:T(8,128)(2,1)S(1)}, bf16[1,256,256]{2,1,0:T(8,128)(2,1)S(1)}, u32[]{:S(2)}, u32[]{:S(2)}) collective-permute-start(bf16[1,256,256]{2,1,0:T(8,128)(2,1)S(1)} %slice.51), channel_id=1, source_target_pairs={{0,16},{8,24},{16,0},{24,8},{1,17},{9,25},{17,1},{25,9},{2,18},{10... | collective-permute-start | bytes 393224 | tf_op jit(solution)/shard_map/ppermute | solution.py:33
  39.7 1.8 %collective-permute-start.11 = (bf16[2,256,256]{2,1,0:T(8,128)(2,1)S(1)}, bf16[2,256,256]{2,1,0:T(8,128)(2,1)S(1)}, u32[]{:S(2)}, u32[]{:S(2)}) collective-permute-start(bf16[2,256,256]{2,1,0:T(8,128)(2,1)S(1)} %get-tuple-element.64), channel_id=1, source_target_pairs={{0,8},{8,0},{16,24},{24,16},{1,9},{9,1},{17,25},{25,17},{2,10},{10... | collective-permute-start | bytes 786440 | tf_op jit(solution)/shard_map/ppermute | solution.py:33
  40.0 3.4 %slice-start = ((f32[2,256,256]{2,1,0:T(8,128)}), f32[1,256,256]{2,1,0:T(8,128)S(1)}, s32[]{:S(2)}) async-start(f32[2,256,256]{2,1,0:T(8,128)} %copy-done.3), calls=%async_computation | async-start | bytes 524288 | tf_op jit(solution)/shard_map/slice | solution.py:472
  41.6 5.8 %collective-permute-start.15 = (bf16[1,256,256]{2,1,0:T(8,128)(2,1)S(1)}, bf16[1,256,256]{2,1,0:T(8,128)(2,1)S(1)}, u32[]{:S(2)}, u32[]{:S(2)}) collective-permute-start(bf16[1,256,256]{2,1,0:T(8,128)(2,1)S(1)} %slice.50), channel_id=1, source_target_pairs={{0,16},{8,24},{16,0},{24,8},{1,17},{9,25},{17,1},{25,9},{2,18},{10... | collective-permute-start | bytes 393224 | tf_op jit(solution)/shard_map/ppermute | solution.py:33
  43.4 7.4 %collective-permute-start.14 = (bf16[1,256,128]{2,1,0:T(8,128)(2,1)S(1)}, bf16[1,256,128]{2,1,0:T(8,128)(2,1)S(1)}, u32[]{:S(2)}, u32[]{:S(2)}) collective-permute-start(bf16[1,256,128]{2,1,0:T(8,128)(2,1)S(1)} %get-tuple-element.69), channel_id=1, source_target_pairs={{0,4},{2,6},{4,0},{6,2},{1,5},{3,7},{5,1},{7,3},{8,12},{10,14},{12... | collective-permute-start | bytes 196616 | tf_op jit(solution)/shard_map/ppermute | solution.py:28
  45.8 6.8 %collective-permute-start.13 = (bf16[1,256,128]{2,1,0:T(8,128)(2,1)S(1)}, bf16[1,256,128]{2,1,0:T(8,128)(2,1)S(1)}, u32[]{:S(2)}, u32[]{:S(2)}) collective-permute-start(bf16[1,256,128]{2,1,0:T(8,128)(2,1)S(1)} %get-tuple-element.68), channel_id=1, source_target_pairs={{0,2},{2,4},{4,6},{6,0},{1,3},{3,5},{5,7},{7,1},{8,10},{10,12},{12... | collective-permute-start | bytes 196616 | tf_op jit(solution)/shard_map/ppermute | solution.py:28
  47.4 5.2 %collective-permute-start.16 = (bf16[1,256,128]{2,1,0:T(8,128)(2,1)S(1)}, bf16[1,256,128]{2,1,0:T(8,128)(2,1)S(1)}, u32[]{:S(2)}, u32[]{:S(2)}) collective-permute-start(bf16[1,256,128]{2,1,0:T(8,128)(2,1)S(1)} %slice.52), channel_id=1, source_target_pairs={{0,6},{2,0},{4,2},{6,4},{1,7},{3,1},{5,3},{7,5},{8,14},{10,8},{12,... | collective-permute-start | bytes 196616 | tf_op jit(solution)/shard_map/ppermute | solution.py:28

commit v4 on v3

--- a/solution.py
+++ b/solution.py
@@ -163,10 +163,6 @@
     return lax.broadcasted_iota(jnp.int32, shape, dim)
 
 
-def over_rows(lhs, rhs):
-    return lax.dot_general(lhs, rhs, (((0,), (0,)), ((), ())), preferred_element_type=F32)
-
-
 def matmul(lhs, rhs):
     return jnp.dot(lhs, rhs, preferred_element_type=F32)
 
@@ -183,35 +179,35 @@
     copies = copy_all([(cell_hbm, cell_ref), (lat_hbm, lat_ref), (vec_hbm, vec_ref)], sems)
     rows = vec_ref.shape[0]
     here = lax.axis_index("lat")
-    lane = iota((rows, LANES), 1)
-    below = (iota((rows, rows), 0) > iota((rows, rows), 1)).astype(BF16)
-    same = iota((rows, rows), 0) == iota((rows, rows), 1)
+    above = (iota((rows, rows), 0) < iota((rows, rows), 1)).astype(BF16)
+    slot = iota((LANES, rows), 0)
     copies[0].wait()
     copies[1].wait()
-    tag = jnp.where(iota((1, rows), 1) < count_ref[0], cell_ref[...] + 1, 0)
-    tag, lat = (
-        jnp.sum(jnp.where(same, field.astype(F32), 0.0), axis=1, keepdims=True)
-        for field in (tag, lat_ref[...])
-    )
-    lat = lat.astype(jnp.int32)
-    named = (lat == lane).astype(BF16)
-    rank = jnp.sum(matmul(below, named) * named.astype(F32), axis=1, keepdims=True)
+    tag = jnp.where(iota((1, rows), 1) < count_ref[0], cell_ref[...] + 1, 0).astype(F32)
+    lat = lat_ref[...]
+    named = (iota((TILE, rows), 0) == lat).astype(BF16)
+    rank = jnp.sum(matmul(named, above) * named.astype(F32), axis=0, keepdims=True)
     rank = rank.astype(jnp.int32)
     base = jnp.where(lat < here, lat - here + n_lat, lat - here) * TILE
     late = rank >= TILE
     choosers = [
-        (jnp.where(chosen, base + rank - back, -1) == lane).astype(BF16)
+        (slot == jnp.where(chosen, base + rank - back, -1)).astype(BF16)
         for chosen, back in ((rank < TILE, 0), (late, TILE), (late, TILE // 2))
     ]
     tags = sum(
-        over_rows(jnp.where(lane == base + i, tag, 0.0).astype(BF16), chooser)
+        lax.dot_general(
+            jnp.where(slot == base + i, tag, 0.0).astype(BF16),
+            chooser,
+            (((1,), (1,)), ((), ())),
+            preferred_element_type=F32,
+        )
         for i, chooser in enumerate(choosers)
     )
     copies[2].wait()
     width = vec_ref.shape[1]
-    picked = over_rows(choosers[0], vec_ref[...])
-    extra = over_rows(choosers[1], vec_ref[:, : width // 2])
-    extra = extra + over_rows(choosers[2], vec_ref[:, width // 2 :])
+    picked = matmul(choosers[0], vec_ref[...])
+    extra = matmul(choosers[1], vec_ref[:, : width // 2])
+    extra = extra + matmul(choosers[2], vec_ref[:, width // 2 :])
     for k, out_ref in enumerate(out_refs):
         piece = slice(k * TILE, (k + 1) * TILE)
         out_ref[:, :width] = picked[piece].astype(BF16)
@@ -312,28 +308,36 @@
         )
         thirds.append(matmul(normed, weights))
     scale = (d_blk // 2) ** (-0.5)
-    queries = thirds[0].astype(BF16).astype(F32) * scale
+    queries = (thirds[0].astype(BF16).astype(F32) * scale).astype(BF16)
     keys, values = thirds[1].astype(BF16), thirds[2].astype(BF16)
     key = iota((1, n_tok), 1)
     valid = lax.axis_index("lat") * WIN + key // WIN % WIN + shift_ref[:, :1] < WIN * n_lat
     first = iota((n_tok, d_blk), 1) < d_blk // 2
-    ones = jnp.ones((n_tok, d_blk), BF16)
-    for which in range(2):
-        rows = slice(which * n_tok, (which + 1) * n_tok)
-        for k in range(len(turns)):
-            cols = slice(k * d_blk, (k + 1) * d_blk)
-            query = queries[rows, cols]
-            both = jnp.concatenate(
-                [jnp.where(first, query, 0.0), jnp.where(first, 0.0, query)], axis=0
-            ).astype(BF16)
-            scores = lax.dot_general(
-                both, keys[rows, cols], (((1,), (1,)), ((), ())), preferred_element_type=F32
-            )
-            scores = jnp.where(valid, scores, -1e30)
-            powers = jnp.exp(scores - jnp.max(scores, axis=-1, keepdims=True)).astype(BF16)
-            mixed = matmul(powers, jnp.concatenate([values[rows, cols], ones], axis=1))
-            mixed = mixed[:, :d_blk] / mixed[:, d_blk:]
-            out_ref[rows, cols] = jnp.where(first, mixed[:n_tok], mixed[n_tok:]).astype(BF16)
+    ones, none = jnp.ones((n_tok, d_blk), BF16), jnp.zeros((n_tok, d_blk), BF16)
+    units = [
+        (slice(which * n_tok, (which + 1) * n_tok), slice(k * d_blk, (k + 1) * d_blk))
+        for which in range(2)
+        for k in range(len(turns))
+    ]
+    scores = []
+    for unit in units:
+        query = queries[unit]
+        both = jnp.concatenate(
+            [jnp.where(first, query, none), jnp.where(first, none, query)], axis=0
+        )
+        scores.append(
+            lax.dot_general(both, keys[unit], (((1,), (1,)), ((), ())), preferred_element_type=F32)
+        )
+    scores = [jnp.where(valid, score, -1e30) for score in scores]
+    highest = [jnp.max(score, axis=-1, keepdims=True) for score in scores]
+    powers = [jnp.exp(score - top).astype(BF16) for score, top in zip(scores, highest)]
+    mixed = [
+        matmul(power, jnp.concatenate([values[unit], ones], axis=1))
+        for power, unit in zip(powers, units)
+    ]
+    for context, unit in zip(mixed, units):
+        context = context[:, :d_blk] / context[:, d_blk:]
+        out_ref[unit] = jnp.where(first, context[:n_tok], context[n_tok:]).astype(BF16)
 
 
 def turn_body(n_lon, cot_ref, other_ref, out_ref, flat_ref):
@@ -500,10 +504,10 @@
     )
     theirs0 = attend(normed, 1, first)
     got0 = swapped(theirs0, "dp", 1)
-    theirs1 = attend(after(normed, theirs0), 1, second)
+    mine0 = attend(after(normed, theirs0), 0, first)
+    theirs1 = attend(after(normed, mine0), 1, second)
     got1 = swapped(theirs1, "dp", 1)
-    mine0 = attend(after(normed, theirs1), 0, first)
-    kept0, sent0 = local_gradient(first, mine0, got0, 1)
+    kept0, sent0 = local_gradient(first, mine0, after(got0, theirs1), 1)
     mine1 = attend(after(normed, sent0), 0, second)
     kept0, sent0 = halves(fold(after(kept0, mine1), sent0, 1))
     kept1, sent1 = local_gradient(second, mine1, after(got1, sent0), SLOW)
@@ -534,6 +538,7 @@
         and n_lon > 2
         and n_lon & (n_lon - 1) == 0
         and n_lat * TILE <= LANES
+        and n_lat <= TILE
         and cap * 2 == TILE * 3
         and lat_dev == WIN
         and lon_dev == 2 * WIN

time: 53.5 us -> 51.8 us (0.968)
  Pallas kernels: 16.1 us -> 14.6 us
  starting transfers between devices: 21 us -> 20.1 us
  waiting for transfers between devices: 13 us -> 13.8 us
    pallas_call x13, Pallas kernels: 16.1 us -> 14.6 us  [call(): pl.pallas_call(body, out_shape=out_shape, in_specs=specs, out_specs=jax.t...]
    ppermute x7, waiting for transfers between devices: 2.84 us -> 3.67 us  [swapped(): return lax.ppermute(array, axis, [(i, i ^ bit) for i in range(devices)])]
  transfers between devices with their start and end apart: 17 -> 17, of which waited for: 8 -> 10; matrix products, arithmetic and copies ran while one was open for 0% -> 0% of each run, Pallas kernels for 27% -> 25%
where the time goes in v4:
time: 51.8 us; the launch traced here: 51.5 us
  starting transfers between devices  20.1 us (39%)
  Pallas kernels  14.6 us (28%)
  waiting for transfers between devices  13.8 us (27%)
  between operations  1.53 us (3%)
  other arithmetic  0.87 us (2%)
  local copies, waits for them, and re-layouts  0.73 us (1%)
    pallas_call x13, Pallas kernels, call(): pl.pallas_call(body, out_shape=out_shape, in_specs=specs, out_specs=jax.t...  14.6 us
    ppermute x8, starting transfers between devices, shifted(): lax.ppermute(array, axis, [(i, (i + by) % devices) for i in range(devices)])  11.2 us
    ppermute x7, starting transfers between devices, swapped(): return lax.ppermute(array, axis, [(i, i ^ bit) for i in range(devices)])  6.27 us
    ppermute x2, waiting for transfers between devices, from_behind(): return lax.ppermute(array, axis, pairs)  6.07 us
    ppermute x8, waiting for transfers between devices, shifted(): lax.ppermute(array, axis, [(i, (i + by) % devices) for i in range(devices)])  4.03 us
    ppermute x7, waiting for transfers between devices, swapped(): return lax.ppermute(array, axis, [(i, i ^ bit) for i in range(devices)])  3.67 us
    ppermute x2, starting transfers between devices, from_behind(): return lax.ppermute(array, axis, pairs)  2.57 us
  transfers between devices with their start and end apart: 17, of which 10 were waited for; matrix products, arithmetic and copies ran while one was open for 0% of the time, Pallas kernels for 25%

profile of v4, /device:TPU:0, one launch (start us, length us, event | category | flops | bytes accessed | tf_op | source)
XLA Modules:
  0.0 51.5 jit_solution(1567520584036569419)
XLA Ops:
  1.3 1.4 %route.1 = (bf16[16,1664]{1,0:T(8,128)(2,1)S(1)}, bf16[16,1664]{1,0:T(8,128)(2,1)S(1)}, bf16[16,1664]{1,0:T(8,128)(2,1)S(1)}, bf16[16,1664]{1,0:T(8,128)(2,1)S(1)}) custom-call(s32[1]{0:T(128)S(6)} %copy.12.count_ref, s32[1,64]{1,0:T(1,128)} %bitcast.6, s32[1,64]{1,0:T(1,128)} %bitcast.7, bf16[64,1024]{1,0:T(8,128)(2,1)} %vec_hbm.1), custom_call_target="tpu_custom_call" | custom-call | flops 1 | bytes 1 | tf_op jit(solution)/shard_map/route/pallas_call | solution.py:145
  2.7 3.1 %collective-permute-start = (bf16[16,1664]{1,0:T(8,128)(2,1)S(1)}, bf16[16,1664]{1,0:T(8,128)(2,1)S(1)}, u32[]{:S(2)}, u32[]{:S(2)}) collective-permute-start(bf16[16,1664]{1,0:T(8,128)(2,1)S(1)} %get-tuple-element.41), channel_id=1, source_target_pairs={{0,2},{2,4},{4,6},{6,0},{1,3},{3,5},{5,7},{7,1},{8,10},{10,12},{12... | collective-permute-start | bytes 159752 | tf_op jit(solution)/shard_map/ppermute | solution.py:28
  5.8 2.6 %collective-permute-start.1 = (bf16[16,1664]{1,0:T(8,128)(2,1)S(1)}, bf16[16,1664]{1,0:T(8,128)(2,1)S(1)}, u32[]{:S(2)}, u32[]{:S(2)}) collective-permute-start(bf16[16,1664]{1,0:T(8,128)(2,1)S(1)} %get-tuple-element.42), channel_id=1, source_target_pairs={{0,4},{2,6},{4,0},{6,2},{1,5},{3,7},{5,1},{7,3},{8,12},{10,14},{12... | collective-permute-start | bytes 159752 | tf_op jit(solution)/shard_map/ppermute | solution.py:28
  8.4 1.3 %collective-permute-start.2 = (bf16[16,1664]{1,0:T(8,128)(2,1)S(1)}, bf16[16,1664]{1,0:T(8,128)(2,1)S(1)}, u32[]{:S(2)}, u32[]{:S(2)}) collective-permute-start(bf16[16,1664]{1,0:T(8,128)(2,1)S(1)} %get-tuple-element.43), channel_id=1, source_target_pairs={{0,6},{2,0},{4,2},{6,4},{1,7},{3,1},{5,3},{7,5},{8,14},{10,8},{12,... | collective-permute-start | bytes 159752 | tf_op jit(solution)/shard_map/ppermute | solution.py:28
  10.4 1.1 %stage.1 = (bf16[1,2,8,16,1024]{4,3,2,1,0:T(8,128)(2,1)S(1)}, bf16[256,720]{1,0:T(8,128)(2,1)S(1)}) custom-call(s32[1,2]{1,0:T(1,128)S(1)} %copy-done.1, bf16[1,2,8,16,1024]{4,3,2,1,0:T(8,128)(2,1)} %tok_hbm), custom_call_target="tpu_custom_call" | custom-call | flops 1 | bytes 1 | tf_op jit(solution)/shard_map/stage/pallas_call | solution.py:145
  13.1 1.3 %collective-permute-start.3 = (bf16[112,1024]{1,0:T(8,128)(2,1)S(1)}, bf16[112,1024]{1,0:T(8,128)(2,1)S(1)}, u32[]{:S(2)}, u32[]{:S(2)}) collective-permute-start(bf16[112,1024]{1,0:T(8,128)(2,1)S(1)} %get-tuple-element.44), channel_id=1, source_target_pairs={{2,0},{4,2},{6,4},{3,1},{5,3},{7,5},{10,8},{12,10},{14,12},{11,9},... | collective-permute-start | bytes 688136 | tf_op jit(solution)/shard_map/ppermute | solution.py:23
  14.4 1.7 %collective-permute-start.7 = (bf16[1,2,8,16,1024]{4,3,2,1,0:T(8,128)(2,1)}, bf16[1,2,8,16,1024]{4,3,2,1,0:T(8,128)(2,1)S(1)}, u32[]{:S(2)}, u32[]{:S(2)}) collective-permute-start(bf16[1,2,8,16,1024]{4,3,2,1,0:T(8,128)(2,1)} %cot_ref.1), channel_id=1, source_target_pairs={{0,1},{1,0},{2,3},{3,2},{4,5},{5,4},{6,7},{7,6},{8,9},{9,8},{10,11... | collective-permute-start | bytes 1572872 | tf_op jit(solution)/shard_map/ppermute | solution.py:33
  16.1 1.3 %collective-permute-start.4 = (bf16[112,1024]{1,0:T(8,128)(2,1)S(1)}, bf16[112,1024]{1,0:T(8,128)(2,1)S(1)}, u32[]{:S(2)}, u32[]{:S(2)}) collective-permute-start(bf16[112,1024]{1,0:T(8,128)(2,1)S(1)} %get-tuple-element.50), channel_id=1, source_target_pairs={{2,0},{4,2},{6,4},{3,1},{5,3},{7,5},{10,8},{12,10},{14,12},{11,9},... | collective-permute-start | bytes 688136 | tf_op jit(solution)/shard_map/ppermute | solution.py:23
  17.4 4.2 %collective-permute-done.3.refs_1_ = bf16[112,1024]{1,0:T(8,128)(2,1)S(1)} collective-permute-done((bf16[112,1024]{1,0:T(8,128)(2,1)S(1)}, bf16[112,1024]{1,0:T(8,128)(2,1)S(1)}, u32[]{:S(2)}, u32[]{:S(2)}) %collective-permute-start.3) | collective-permute-done | bytes 229408 | tf_op jit(solution)/shard_map/ppermute | solution.py:23
  21.5 3.4 %weights.1 = (bf16[1024,3072]{1,0:T(8,128)(2,1)S(1)}, bf16[1024,1024]{1,0:T(8,128)(2,1)S(1)}, f32[1,1024]{1,0:T(1,128)S(1)}) custom-call(bf16[1024,3072]{1,0:T(8,128)(2,1)} %refs_0_, bf16[1024,1024]{1,0:T(8,128)(2,1)} %refs_1_, f32[1,1024]{1,0:T(1,128)} %bitcast.5), custom_call_target="tpu_custom_call" | custom-call | flops 1 | bytes 1 | tf_op jit(solution)/shard_map/weights/pallas_call | solution.py:145
  25.0 1.9 %collective-permute-done.4.refs_2_ = bf16[112,1024]{1,0:T(8,128)(2,1)S(1)} collective-permute-done((bf16[112,1024]{1,0:T(8,128)(2,1)S(1)}, bf16[112,1024]{1,0:T(8,128)(2,1)S(1)}, u32[]{:S(2)}, u32[]{:S(2)}) %collective-permute-start.4) | collective-permute-done | bytes 229408 | tf_op jit(solution)/shard_map/ppermute | solution.py:23
  26.9 0.8 %region.1 = (bf16[256,1024]{1,0:T(8,128)(2,1)S(1)}, bf16[256,1024]{1,0:T(8,128)(2,1)S(1)}) custom-call(bf16[256,720]{1,0:T(8,128)(2,1)S(1)} %get-tuple-element.39.pick_ref, f32[1,1024]{1,0:T(1,128)S(1)} %get-tuple-element.48.gain_ref, bf16[256,1024]{1,0:T(8,128)(2,1)S(1)} %get-tuple-element.49.refs_0_, bf16[112,1024]{1,0:T(8,128)(2,1)S(1)} %collective-permute-done.3.refs_1_, ...), custom_call_target="tpu_custom_call" | custom-call | flops 1 | bytes 1 | tf_op jit(solution)/shard_map/region/pallas_call | solution.py:145
  27.7 1.1 %attend11.1.refs_0_ = bf16[256,256]{1,0:T(8,128)(2,1)S(1)} custom-call(bf16[256,1024]{1,0:T(8,128)(2,1)S(1)} %get-tuple-element.60.normed_ref, bf16[1024,3072]{1,0:T(8,128)(2,1)S(1)} %get-tuple-element.54.wqkv_ref, s32[1,2]{1,0:T(1,128)S(1)} %copy-done.2), custom_call_target="tpu_custom_call" | custom-call | flops 1 | bytes 1 | tf_op jit(solution)/shard_map/attend11/pallas_call | solution.py:145
  29.6 1.1 %attend01.1.mine_ref.refs_1_ = bf16[256,256]{1,0:T(8,128)(2,1)S(1)} custom-call(bf16[256,1024]{1,0:T(8,128)(2,1)S(1)} %get-tuple-element.60.normed_ref, bf16[1024,3072]{1,0:T(8,128)(2,1)S(1)} %get-tuple-element.54.wqkv_ref, s32[1,2]{1,0:T(1,128)S(1)} %copy-done.2), custom_call_target="tpu_custom_call" | custom-call | flops 1 | bytes 1 | tf_op jit(solution)/shard_map/attend01/pallas_call | solution.py:145
  30.8 1.1 %attend10.1.refs_2_ = bf16[256,256]{1,0:T(8,128)(2,1)S(1)} custom-call(bf16[256,1024]{1,0:T(8,128)(2,1)S(1)} %get-tuple-element.60.normed_ref, bf16[1024,3072]{1,0:T(8,128)(2,1)S(1)} %get-tuple-element.54.wqkv_ref, s32[1,2]{1,0:T(1,128)S(1)} %copy-done.2), custom_call_target="tpu_custom_call" | custom-call | flops 1 | bytes 1 | tf_op jit(solution)/shard_map/attend10/pallas_call | solution.py:145
  31.9 1.4 %collective-permute-start.10 = (bf16[256,256]{1,0:T(8,128)(2,1)S(1)}, bf16[256,256]{1,0:T(8,128)(2,1)S(1)}, u32[]{:S(2)}, u32[]{:S(2)}) collective-permute-start(bf16[256,256]{1,0:T(8,128)(2,1)S(1)} %attend10.1.refs_2_), channel_id=1, source_target_pairs={{0,1},{1,0},{2,3},{3,2},{4,5},{5,4},{6,7},{7,6},{8,9},{9,8},{10,11... | collective-permute-start | bytes 393224 | tf_op jit(solution)/shard_map/ppermute | solution.py:33
  34.8 1.1 %attend00.1.refs_3_.mine_ref = bf16[256,256]{1,0:T(8,128)(2,1)S(1)} custom-call(bf16[256,1024]{1,0:T(8,128)(2,1)S(1)} %get-tuple-element.60.normed_ref, bf16[1024,3072]{1,0:T(8,128)(2,1)S(1)} %get-tuple-element.54.wqkv_ref, s32[1,2]{1,0:T(1,128)S(1)} %copy-done.2), custom_call_target="tpu_custom_call" | custom-call | flops 10000000000 | bytes 1 | tf_op jit(solution)/shard_map/attend00/pallas_call | solution.py:145
  36.4 1.6 %collective-permute-start.12 = (bf16[1,256,256]{2,1,0:T(8,128)(2,1)S(1)}, bf16[1,256,256]{2,1,0:T(8,128)(2,1)S(1)}, u32[]{:S(2)}, u32[]{:S(2)}) collective-permute-start(bf16[1,256,256]{2,1,0:T(8,128)(2,1)S(1)} %slice.51), channel_id=1, source_target_pairs={{0,16},{8,24},{16,0},{24,8},{1,17},{9,25},{17,1},{25,9},{2,18},{10... | collective-permute-start | bytes 393224 | tf_op jit(solution)/shard_map/ppermute | solution.py:33
  38.5 1.5 %project.1 = bf16[1,2,8,16,1024]{4,3,2,1,0:T(8,128)(2,1)} custom-call(bf16[256,1024]{1,0:T(8,128)(2,1)S(1)} %get-tuple-element.62.reg_ref, bf16[1024,1024]{1,0:T(8,128)(2,1)S(1)} %get-tuple-element.63.wout_ref, bf16[256,256]{1,0:T(8,128)(2,1)S(1)} %attend11.1.refs_0_, bf16[256,256]{1,0:T(8,128)(2,1)S(1)} %attend01.1.mine_ref.refs_1_, ...), custom_call_target="tpu_custom_call" | custom-call | flops 10000000000 | bytes 1 | tf_op jit(solution)/shard_map/project/pallas_call | solution.py:145
  40.8 1.2 %collective-permute-done.12 = bf16[1,256,256]{2,1,0:T(8,128)(2,1)S(1)} collective-permute-done((bf16[1,256,256]{2,1,0:T(8,128)(2,1)S(1)}, bf16[1,256,256]{2,1,0:T(8,128)(2,1)S(1)}, u32[]{:S(2)}, u32[]{:S(2)}) %collective-permute-start.12) | collective-permute-done | bytes 131104 | tf_op jit(solution)/shard_map/ppermute | solution.py:33
  42.1 1.9 %collective-permute-start.14 = (bf16[1,256,128]{2,1,0:T(8,128)(2,1)S(1)}, bf16[1,256,128]{2,1,0:T(8,128)(2,1)S(1)}, u32[]{:S(2)}, u32[]{:S(2)}) collective-permute-start(bf16[1,256,128]{2,1,0:T(8,128)(2,1)S(1)} %get-tuple-element.71), channel_id=1, source_target_pairs={{0,4},{2,6},{4,0},{6,2},{1,5},{3,7},{5,1},{7,3},{8,12},{10,14},{12... | collective-permute-start | bytes 196616 | tf_op jit(solution)/shard_map/ppermute | solution.py:28
  44.5 1.6 %collective-permute-done.15 = bf16[1,256,256]{2,1,0:T(8,128)(2,1)S(1)} collective-permute-done((bf16[1,256,256]{2,1,0:T(8,128)(2,1)S(1)}, bf16[1,256,256]{2,1,0:T(8,128)(2,1)S(1)}, u32[]{:S(2)}, u32[]{:S(2)}) %collective-permute-start.15) | collective-permute-done | bytes 131104 | tf_op jit(solution)/shard_map/ppermute | solution.py:33
  46.1 1.8 %collective-permute-start.16 = (bf16[1,256,128]{2,1,0:T(8,128)(2,1)S(1)}, bf16[1,256,128]{2,1,0:T(8,128)(2,1)S(1)}, u32[]{:S(2)}, u32[]{:S(2)}) collective-permute-start(bf16[1,256,128]{2,1,0:T(8,128)(2,1)S(1)} %slice.52), channel_id=1, source_target_pairs={{0,6},{2,0},{4,2},{6,4},{1,7},{3,1},{5,3},{7,5},{8,14},{10,8},{12,... | collective-permute-start | bytes 196616 | tf_op jit(solution)/shard_map/ppermute | solution.py:28
  48.0 2.4 %collective-permute-done.13 = bf16[1,256,128]{2,1,0:T(8,128)(2,1)S(1)} collective-permute-done((bf16[1,256,128]{2,1,0:T(8,128)(2,1)S(1)}, bf16[1,256,128]{2,1,0:T(8,128)(2,1)S(1)}, u32[]{:S(2)}, u32[]{:S(2)}) %collective-permute-start.13) | collective-permute-done | bytes 65568 | tf_op jit(solution)/shard_map/ppermute | solution.py:28
  (44 shorter events, 7.8 us)
Async XLA Ops:
  0.6 27.1 %copy-start.2 = (s32[1,2]{1,0:T(1,128)S(1)}, s32[1,2]{1,0:T(1,128)}, u32[]{:S(2)}) copy-start(s32[1,2]{1,0:T(1,128)} %shift_ref.4) | copy-start | bytes 28
  2.7 8.7 %collective-permute-start = (bf16[16,1664]{1,0:T(8,128)(2,1)S(1)}, bf16[16,1664]{1,0:T(8,128)(2,1)S(1)}, u32[]{:S(2)}, u32[]{:S(2)}) collective-permute-start(bf16[16,1664]{1,0:T(8,128)(2,1)S(1)} %get-tuple-element.41), channel_id=1, source_target_pairs={{0,2},{2,4},{4,6},{6,0},{1,3},{3,5},{5,7},{7,1},{8,10},{10,12},{12... | collective-permute-start | bytes 159752 | tf_op jit(solution)/shard_map/ppermute | solution.py:28
  5.8 6.4 %collective-permute-start.1 = (bf16[16,1664]{1,0:T(8,128)(2,1)S(1)}, bf16[16,1664]{1,0:T(8,128)(2,1)S(1)}, u32[]{:S(2)}, u32[]{:S(2)}) collective-permute-start(bf16[16,1664]{1,0:T(8,128)(2,1)S(1)} %get-tuple-element.42), channel_id=1, source_target_pairs={{0,4},{2,6},{4,0},{6,2},{1,5},{3,7},{5,1},{7,3},{8,12},{10,14},{12... | collective-permute-start | bytes 159752 | tf_op jit(solution)/shard_map/ppermute | solution.py:28
  8.4 4.3 %collective-permute-start.2 = (bf16[16,1664]{1,0:T(8,128)(2,1)S(1)}, bf16[16,1664]{1,0:T(8,128)(2,1)S(1)}, u32[]{:S(2)}, u32[]{:S(2)}) collective-permute-start(bf16[16,1664]{1,0:T(8,128)(2,1)S(1)} %get-tuple-element.43), channel_id=1, source_target_pairs={{0,6},{2,0},{4,2},{6,4},{1,7},{3,1},{5,3},{7,5},{8,14},{10,8},{12,... | collective-permute-start | bytes 159752 | tf_op jit(solution)/shard_map/ppermute | solution.py:28
  9.7 0.7 %copy-start.1 = (s32[1,2]{1,0:T(1,128)S(1)}, s32[1,2]{1,0:T(1,128)}, u32[]{:S(2)}) copy-start(s32[1,2]{1,0:T(1,128)} %shift_ref.4) | copy-start | bytes 28
  13.1 8.5 %collective-permute-start.3 = (bf16[112,1024]{1,0:T(8,128)(2,1)S(1)}, bf16[112,1024]{1,0:T(8,128)(2,1)S(1)}, u32[]{:S(2)}, u32[]{:S(2)}) collective-permute-start(bf16[112,1024]{1,0:T(8,128)(2,1)S(1)} %get-tuple-element.44), channel_id=1, source_target_pairs={{2,0},{4,2},{6,4},{3,1},{5,3},{7,5},{10,8},{12,10},{14,12},{11,9},... | collective-permute-start | bytes 688136 | tf_op jit(solution)/shard_map/ppermute | solution.py:23
  14.4 19.0 %collective-permute-start.7 = (bf16[1,2,8,16,1024]{4,3,2,1,0:T(8,128)(2,1)}, bf16[1,2,8,16,1024]{4,3,2,1,0:T(8,128)(2,1)S(1)}, u32[]{:S(2)}, u32[]{:S(2)}) collective-permute-start(bf16[1,2,8,16,1024]{4,3,2,1,0:T(8,128)(2,1)} %cot_ref.1), channel_id=1, source_target_pairs={{0,1},{1,0},{2,3},{3,2},{4,5},{5,4},{6,7},{7,6},{8,9},{9,8},{10,11... | collective-permute-start | bytes 1572872 | tf_op jit(solution)/shard_map/ppermute | solution.py:33
  16.1 10.8 %collective-permute-start.5 = (bf16[128,1024]{1,0:T(8,128)(2,1)S(1)}, bf16[128,1024]{1,0:T(8,128)(2,1)S(1)}, u32[]{:S(2)}, u32[]{:S(2)}) collective-permute-start(bf16[128,1024]{1,0:T(8,128)(2,1)S(1)} %get-tuple-element.51), channel_id=1, source_target_pairs={{0,24},{8,0},{16,8},{24,16},{1,25},{9,1},{17,9},{25,17},{2,26},{10... | collective-permute-start | bytes 786440 | tf_op jit(solution)/shard_map/ppermute | solution.py:28
  16.1 10.8 %collective-permute-start.4 = (bf16[112,1024]{1,0:T(8,128)(2,1)S(1)}, bf16[112,1024]{1,0:T(8,128)(2,1)S(1)}, u32[]{:S(2)}, u32[]{:S(2)}) collective-permute-start(bf16[112,1024]{1,0:T(8,128)(2,1)S(1)} %get-tuple-element.50), channel_id=1, source_target_pairs={{2,0},{4,2},{6,4},{3,1},{5,3},{7,5},{10,8},{12,10},{14,12},{11,9},... | collective-permute-start | bytes 688136 | tf_op jit(solution)/shard_map/ppermute | solution.py:23
  21.5 5.4 %collective-permute-start.6 = (bf16[112,1024]{1,0:T(8,128)(2,1)S(1)}, bf16[112,1024]{1,0:T(8,128)(2,1)S(1)}, u32[]{:S(2)}, u32[]{:S(2)}) collective-permute-start(bf16[112,1024]{1,0:T(8,128)(2,1)S(1)} %collective-permute-done.3.refs_1_), channel_id=1, source_target_pairs={{0,24},{8,0},{16,8},{24,16},{1,25},{9,1},{17,9},{25,17},{2,26},{10... | collective-permute-start | bytes 688136 | tf_op jit(solution)/shard_map/ppermute | solution.py:28
  28.9 4.5 %copy-start = (bf16[1,2,8,16,1024]{4,3,2,1,0:T(8,128)(2,1)S(1)}, bf16[1,2,8,16,1024]{4,3,2,1,0:T(8,128)(2,1)}, u32[]{:S(2)}) copy-start(bf16[1,2,8,16,1024]{4,3,2,1,0:T(8,128)(2,1)} %cot_ref.1) | copy-start | bytes 1572868
  28.9 5.4 %collective-permute-start.8 = (bf16[256,256]{1,0:T(8,128)(2,1)S(1)}, bf16[256,256]{1,0:T(8,128)(2,1)S(1)}, u32[]{:S(2)}, u32[]{:S(2)}) collective-permute-start(bf16[256,256]{1,0:T(8,128)(2,1)S(1)} %attend11.1.refs_0_), channel_id=1, source_target_pairs={{0,1},{1,0},{2,3},{3,2},{4,5},{5,4},{6,7},{7,6},{8,9},{9,8},{10,11... | collective-permute-start | bytes 393224 | tf_op jit(solution)/shard_map/ppermute | solution.py:33
  31.9 6.1 %collective-permute-start.10 = (bf16[256,256]{1,0:T(8,128)(2,1)S(1)}, bf16[256,256]{1,0:T(8,128)(2,1)S(1)}, u32[]{:S(2)}, u32[]{:S(2)}) collective-permute-start(bf16[256,256]{1,0:T(8,128)(2,1)S(1)} %attend10.1.refs_2_), channel_id=1, source_target_pairs={{0,1},{1,0},{2,3},{3,2},{4,5},{5,4},{6,7},{7,6},{8,9},{9,8},{10,11... | collective-permute-start | bytes 393224 | tf_op jit(solution)/shard_map/ppermute | solution.py:33
  34.7 1.6 %collective-permute-start.9 = (bf16[2,256,256]{2,1,0:T(8,128)(2,1)S(1)}, bf16[2,256,256]{2,1,0:T(8,128)(2,1)S(1)}, u32[]{:S(2)}, u32[]{:S(2)}) collective-permute-start(bf16[2,256,256]{2,1,0:T(8,128)(2,1)S(1)} %get-tuple-element.59), channel_id=1, source_target_pairs={{0,8},{8,0},{16,24},{24,16},{1,9},{9,1},{17,25},{25,17},{2,10},{10... | collective-permute-start | bytes 786440 | tf_op jit(solution)/shard_map/ppermute | solution.py:33
  36.4 2.0 %copy-start.3 = (f32[2,256,256]{2,1,0:T(8,128)}, f32[2,256,256]{2,1,0:T(8,128)S(1)}, u32[]{:S(2)}) copy-start(f32[2,256,256]{2,1,0:T(8,128)S(1)} %convert_add_fusion.1) | copy-start | bytes 1572868
  36.4 5.6 %collective-permute-start.12 = (bf16[1,256,256]{2,1,0:T(8,128)(2,1)S(1)}, bf16[1,256,256]{2,1,0:T(8,128)(2,1)S(1)}, u32[]{:S(2)}, u32[]{:S(2)}) collective-permute-start(bf16[1,256,256]{2,1,0:T(8,128)(2,1)S(1)} %slice.51), channel_id=1, source_target_pairs={{0,16},{8,24},{16,0},{24,8},{1,17},{9,25},{17,1},{25,9},{2,18},{10... | collective-permute-start | bytes 393224 | tf_op jit(solution)/shard_map/ppermute | solution.py:33
  38.4 1.6 %collective-permute-start.11 = (bf16[2,256,256]{2,1,0:T(8,128)(2,1)S(1)}, bf16[2,256,256]{2,1,0:T(8,128)(2,1)S(1)}, u32[]{:S(2)}, u32[]{:S(2)}) collective-permute-start(bf16[2,256,256]{2,1,0:T(8,128)(2,1)S(1)} %get-tuple-element.66), channel_id=1, source_target_pairs={{0,8},{8,0},{16,24},{24,16},{1,9},{9,1},{17,25},{25,17},{2,10},{10... | collective-permute-start | bytes 786440 | tf_op jit(solution)/shard_map/ppermute | solution.py:33
  38.5 3.5 %slice-start = ((f32[2,256,256]{2,1,0:T(8,128)}), f32[1,256,256]{2,1,0:T(8,128)S(1)}, s32[]{:S(2)}) async-start(f32[2,256,256]{2,1,0:T(8,128)} %copy-done.3), calls=%async_computation | async-start | bytes 524288 | tf_op jit(solution)/shard_map/slice | solution.py:476
  40.2 5.9 %collective-permute-start.15 = (bf16[1,256,256]{2,1,0:T(8,128)(2,1)S(1)}, bf16[1,256,256]{2,1,0:T(8,128)(2,1)S(1)}, u32[]{:S(2)}, u32[]{:S(2)}) collective-permute-start(bf16[1,256,256]{2,1,0:T(8,128)(2,1)S(1)} %slice.50), channel_id=1, source_target_pairs={{0,16},{8,24},{16,0},{24,8},{1,17},{9,25},{17,1},{25,9},{2,18},{10... | collective-permute-start | bytes 393224 | tf_op jit(solution)/shard_map/ppermute | solution.py:33
  42.1 5.9 %collective-permute-start.14 = (bf16[1,256,128]{2,1,0:T(8,128)(2,1)S(1)}, bf16[1,256,128]{2,1,0:T(8,128)(2,1)S(1)}, u32[]{:S(2)}, u32[]{:S(2)}) collective-permute-start(bf16[1,256,128]{2,1,0:T(8,128)(2,1)S(1)} %get-tuple-element.71), channel_id=1, source_target_pairs={{0,4},{2,6},{4,0},{6,2},{1,5},{3,7},{5,1},{7,3},{8,12},{10,14},{12... | collective-permute-start | bytes 196616 | tf_op jit(solution)/shard_map/ppermute | solution.py:28
  44.0 6.4 %collective-permute-start.13 = (bf16[1,256,128]{2,1,0:T(8,128)(2,1)S(1)}, bf16[1,256,128]{2,1,0:T(8,128)(2,1)S(1)}, u32[]{:S(2)}, u32[]{:S(2)}) collective-permute-start(bf16[1,256,128]{2,1,0:T(8,128)(2,1)S(1)} %get-tuple-element.70), channel_id=1, source_target_pairs={{0,2},{2,4},{4,6},{6,0},{1,3},{3,5},{5,7},{7,1},{8,10},{10,12},{12... | collective-permute-start | bytes 196616 | tf_op jit(solution)/shard_map/ppermute | solution.py:28
  46.1 4.7 %collective-permute-start.16 = (bf16[1,256,128]{2,1,0:T(8,128)(2,1)S(1)}, bf16[1,256,128]{2,1,0:T(8,128)(2,1)S(1)}, u32[]{:S(2)}, u32[]{:S(2)}) collective-permute-start(bf16[1,256,128]{2,1,0:T(8,128)(2,1)S(1)} %slice.52), channel_id=1, source_target_pairs={{0,6},{2,0},{4,2},{6,4},{1,7},{3,1},{5,3},{7,5},{8,14},{10,8},{12,... | collective-permute-start | bytes 196616 | tf_op jit(solution)/shard_map/ppermute | solution.py:28

commit v5 on v4

--- a/solution.py
+++ b/solution.py
@@ -174,19 +174,22 @@
     return copies
 
 
-def route_body(n_lat, count_ref, cell_hbm, lat_hbm, vec_hbm, *refs):
-    out_refs, (cell_ref, lat_ref, vec_ref, sems) = refs[:n_lat], refs[n_lat:]
-    copies = copy_all([(cell_hbm, cell_ref), (lat_hbm, lat_ref), (vec_hbm, vec_ref)], sems)
+def above_body(above_ref):
+    above_ref[...] = (iota(above_ref.shape, 0) < iota(above_ref.shape, 1)).astype(BF16)
+
+
+def live_body(count_ref, live_ref):
+    live_ref[...] = (iota(live_ref.shape, 1) < count_ref[0]).astype(jnp.int32)
+
+
+def route_body(n_lat, above_ref, live_ref, cell_ref, lat_ref, vec_ref, *out_refs):
     rows = vec_ref.shape[0]
     here = lax.axis_index("lat")
-    above = (iota((rows, rows), 0) < iota((rows, rows), 1)).astype(BF16)
     slot = iota((LANES, rows), 0)
-    copies[0].wait()
-    copies[1].wait()
-    tag = jnp.where(iota((1, rows), 1) < count_ref[0], cell_ref[...] + 1, 0).astype(F32)
+    tag = (live_ref[...] * (cell_ref[...] + 1)).astype(F32)
     lat = lat_ref[...]
     named = (iota((TILE, rows), 0) == lat).astype(BF16)
-    rank = jnp.sum(matmul(named, above) * named.astype(F32), axis=0, keepdims=True)
+    rank = jnp.sum(matmul(named, above_ref[...]) * named.astype(F32), axis=0, keepdims=True)
     rank = rank.astype(jnp.int32)
     base = jnp.where(lat < here, lat - here + n_lat, lat - here) * TILE
     late = rank >= TILE
@@ -203,7 +206,6 @@
         )
         for i, chooser in enumerate(choosers)
     )
-    copies[2].wait()
     width = vec_ref.shape[1]
     picked = matmul(choosers[0], vec_ref[...])
     extra = matmul(choosers[1], vec_ref[:, : width // 2])
@@ -406,13 +408,22 @@
     dma = pltpu.SemaphoreType.DMA
 
     fetched = (obs_cell.reshape(1, -1), obs_lat.reshape(1, -1), obs_vectors)
+    obs_rows = obs_vectors.shape[0]
+    above = call(above_body, shape((obs_rows, obs_rows), BF16), (), [], "above", flops=SLOW)
+    above, obs_count = lax.optimization_barrier((above, obs_count))
+    live = call(
+        live_body,
+        shape(fetched[0].shape, jnp.int32),
+        (obs_count,),
+        [SMEM_SPEC],
+        "live",
+    )
     payload = call(
         functools.partial(route_body, n_lat),
         [shape((TILE, d_model + d_model // 2 + LANES), BF16)] * n_lat,
-        (obs_count, *(in_hbm(array) for array in fetched)),
-        [SMEM_SPEC] + [ANY_SPEC] * 3,
+        (above, live, *fetched),
+        [VMEM_SPEC] * 5,
         "route",
-        [*(pltpu.VMEM(array.shape, array.dtype) for array in fetched), dma((3,))],
     )
     arrived = [payload[0]] + [shifted(payload[k], "lat", k) for k in range(1, n_lat)]
 

time: 51.8 us -> 51.1 us (0.986)
  Pallas kernels: 14.6 us -> 13.7 us
  waiting for transfers between devices: 13.8 us -> 14.4 us
  local copies, waits for them, and re-layouts: 0.73 us -> 0.2 us
    pallas_call x13 -> x15, Pallas kernels: 14.6 us -> 13.7 us  [call(): pl.pallas_call(body, out_shape=out_shape, in_specs=specs, out_specs=jax.t...]
    ppermute x8, waiting for transfers between devices: 4.03 us -> 4.69 us  [shifted(): lax.ppermute(array, axis, [(i, (i + by) % devices) for i in range(devices)])]
    unnamed x8 -> x12, local copies, waits for them, and re-layouts: 0.67 us -> 0.15 us
where the time goes in v5:
time: 51.1 us; the launch traced here: 50.9 us
  starting transfers between devices  20.1 us (39%)
  waiting for transfers between devices  14.4 us (28%)
  Pallas kernels  13.7 us (27%)
  between operations  1.65 us (3%)
  other arithmetic  0.86 us (2%)
    pallas_call x15, Pallas kernels, call(): pl.pallas_call(body, out_shape=out_shape, in_specs=specs, out_specs=jax.t...  13.7 us
    ppermute x8, starting transfers between devices, shifted(): lax.ppermute(array, axis, [(i, (i + by) % devices) for i in range(devices)])  11.2 us
    ppermute x7, starting transfers between devices, swapped(): return lax.ppermute(array, axis, [(i, i ^ bit) for i in range(devices)])  6.27 us
    ppermute x2, waiting for transfers between devices, from_behind(): return lax.ppermute(array, axis, pairs)  6.07 us
    ppermute x8, waiting for transfers between devices, shifted(): lax.ppermute(array, axis, [(i, (i + by) % devices) for i in range(devices)])  4.69 us
    ppermute x7, waiting for transfers between devices, swapped(): return lax.ppermute(array, axis, [(i, i ^ bit) for i in range(devices)])  3.65 us
    ppermute x2, starting transfers between devices, from_behind(): return lax.ppermute(array, axis, pairs)  2.57 us
  transfers between devices with their start and end apart: 17, of which 10 were waited for; matrix products, arithmetic and copies ran while one was open for 0% of the time, Pallas kernels for 25%

profile of v5, /device:TPU:0, one launch (start us, length us, event | category | flops | bytes accessed | tf_op | source)
XLA Modules:
  0.0 50.9 jit_solution(2045164645800075995)
XLA Ops:
  2.0 3.1 %collective-permute-start = (bf16[16,1664]{1,0:T(8,128)(2,1)S(1)}, bf16[16,1664]{1,0:T(8,128)(2,1)S(1)}, u32[]{:S(2)}, u32[]{:S(2)}) collective-permute-start(bf16[16,1664]{1,0:T(8,128)(2,1)S(1)} %get-tuple-element.45), channel_id=1, source_target_pairs={{0,2},{2,4},{4,6},{6,0},{1,3},{3,5},{5,7},{7,1},{8,10},{10,12},{12... | collective-permute-start | bytes 159752 | tf_op jit(solution)/shard_map/ppermute | solution.py:28
  5.1 2.6 %collective-permute-start.1 = (bf16[16,1664]{1,0:T(8,128)(2,1)S(1)}, bf16[16,1664]{1,0:T(8,128)(2,1)S(1)}, u32[]{:S(2)}, u32[]{:S(2)}) collective-permute-start(bf16[16,1664]{1,0:T(8,128)(2,1)S(1)} %get-tuple-element.46), channel_id=1, source_target_pairs={{0,4},{2,6},{4,0},{6,2},{1,5},{3,7},{5,1},{7,3},{8,12},{10,14},{12... | collective-permute-start | bytes 159752 | tf_op jit(solution)/shard_map/ppermute | solution.py:28
  7.7 1.3 %collective-permute-start.2 = (bf16[16,1664]{1,0:T(8,128)(2,1)S(1)}, bf16[16,1664]{1,0:T(8,128)(2,1)S(1)}, u32[]{:S(2)}, u32[]{:S(2)}) collective-permute-start(bf16[16,1664]{1,0:T(8,128)(2,1)S(1)} %get-tuple-element.47), channel_id=1, source_target_pairs={{0,6},{2,0},{4,2},{6,4},{1,7},{3,1},{5,3},{7,5},{8,14},{10,8},{12,... | collective-permute-start | bytes 159752 | tf_op jit(solution)/shard_map/ppermute | solution.py:28
  9.1 1.1 %stage.1 = (bf16[1,2,8,16,1024]{4,3,2,1,0:T(8,128)(2,1)S(1)}, bf16[256,720]{1,0:T(8,128)(2,1)S(1)}) custom-call(s32[1,2]{1,0:T(1,128)S(1)} %copy-done.2, bf16[1,2,8,16,1024]{4,3,2,1,0:T(8,128)(2,1)} %tok_hbm), custom_call_target="tpu_custom_call" | custom-call | flops 1 | bytes 1 | tf_op jit(solution)/shard_map/stage/pallas_call | solution.py:145
  10.1 1.4 %collective-permute-done.1.refs_2_ = bf16[16,1664]{1,0:T(8,128)(2,1)S(1)} collective-permute-done((bf16[16,1664]{1,0:T(8,128)(2,1)S(1)}, bf16[16,1664]{1,0:T(8,128)(2,1)S(1)}, u32[]{:S(2)}, u32[]{:S(2)}) %collective-permute-start.1) | collective-permute-done | bytes 53280 | tf_op jit(solution)/shard_map/ppermute | solution.py:28
  12.4 1.3 %collective-permute-start.3 = (bf16[112,1024]{1,0:T(8,128)(2,1)S(1)}, bf16[112,1024]{1,0:T(8,128)(2,1)S(1)}, u32[]{:S(2)}, u32[]{:S(2)}) collective-permute-start(bf16[112,1024]{1,0:T(8,128)(2,1)S(1)} %get-tuple-element.48), channel_id=1, source_target_pairs={{2,0},{4,2},{6,4},{3,1},{5,3},{7,5},{10,8},{12,10},{14,12},{11,9},... | collective-permute-start | bytes 688136 | tf_op jit(solution)/shard_map/ppermute | solution.py:23
  13.7 1.7 %collective-permute-start.7 = (bf16[1,2,8,16,1024]{4,3,2,1,0:T(8,128)(2,1)S(1)}, bf16[1,2,8,16,1024]{4,3,2,1,0:T(8,128)(2,1)S(1)}, u32[]{:S(2)}, u32[]{:S(2)}) collective-permute-start(bf16[1,2,8,16,1024]{4,3,2,1,0:T(8,128)(2,1)S(1)} %copy-done), channel_id=1, source_target_pairs={{0,1},{1,0},{2,3},{3,2},{4,5},{5,4},{6,7},{7,6},{8,9},{9,8},{10,11... | collective-permute-start | bytes 1572872 | tf_op jit(solution)/shard_map/ppermute | solution.py:33
  15.4 1.3 %collective-permute-start.4 = (bf16[112,1024]{1,0:T(8,128)(2,1)S(1)}, bf16[112,1024]{1,0:T(8,128)(2,1)S(1)}, u32[]{:S(2)}, u32[]{:S(2)}) collective-permute-start(bf16[112,1024]{1,0:T(8,128)(2,1)S(1)} %get-tuple-element.54), channel_id=1, source_target_pairs={{2,0},{4,2},{6,4},{3,1},{5,3},{7,5},{10,8},{12,10},{14,12},{11,9},... | collective-permute-start | bytes 688136 | tf_op jit(solution)/shard_map/ppermute | solution.py:23
  16.7 4.2 %collective-permute-done.3.refs_1_ = bf16[112,1024]{1,0:T(8,128)(2,1)S(1)} collective-permute-done((bf16[112,1024]{1,0:T(8,128)(2,1)S(1)}, bf16[112,1024]{1,0:T(8,128)(2,1)S(1)}, u32[]{:S(2)}, u32[]{:S(2)}) %collective-permute-start.3) | collective-permute-done | bytes 229408 | tf_op jit(solution)/shard_map/ppermute | solution.py:23
  20.9 3.4 %weights.1 = (bf16[1024,3072]{1,0:T(8,128)(2,1)S(1)}, bf16[1024,1024]{1,0:T(8,128)(2,1)S(1)}, f32[1,1024]{1,0:T(1,128)S(1)}) custom-call(bf16[1024,3072]{1,0:T(8,128)(2,1)} %refs_0_, bf16[1024,1024]{1,0:T(8,128)(2,1)} %refs_1_, f32[1,1024]{1,0:T(1,128)} %bitcast.7), custom_call_target="tpu_custom_call" | custom-call | flops 1 | bytes 1 | tf_op jit(solution)/shard_map/weights/pallas_call | solution.py:145
  24.3 1.9 %collective-permute-done.4.refs_2_ = bf16[112,1024]{1,0:T(8,128)(2,1)S(1)} collective-permute-done((bf16[112,1024]{1,0:T(8,128)(2,1)S(1)}, bf16[112,1024]{1,0:T(8,128)(2,1)S(1)}, u32[]{:S(2)}, u32[]{:S(2)}) %collective-permute-start.4) | collective-permute-done | bytes 229408 | tf_op jit(solution)/shard_map/ppermute | solution.py:23
  26.2 0.8 %region.1 = (bf16[256,1024]{1,0:T(8,128)(2,1)S(1)}, bf16[256,1024]{1,0:T(8,128)(2,1)S(1)}) custom-call(bf16[256,720]{1,0:T(8,128)(2,1)S(1)} %get-tuple-element.43.pick_ref, f32[1,1024]{1,0:T(1,128)S(1)} %get-tuple-element.52.gain_ref, bf16[256,1024]{1,0:T(8,128)(2,1)S(1)} %get-tuple-element.53.refs_0_, bf16[112,1024]{1,0:T(8,128)(2,1)S(1)} %collective-permute-done.3.refs_1_, ...), custom_call_target="tpu_custom_call" | custom-call | flops 1 | bytes 1 | tf_op jit(solution)/shard_map/region/pallas_call | solution.py:145
  27.1 1.2 %attend11.1.refs_0_ = bf16[256,256]{1,0:T(8,128)(2,1)S(1)} custom-call(bf16[256,1024]{1,0:T(8,128)(2,1)S(1)} %get-tuple-element.64.normed_ref, bf16[1024,3072]{1,0:T(8,128)(2,1)S(1)} %get-tuple-element.58.wqkv_ref, s32[1,2]{1,0:T(1,128)S(1)} %copy-done.2), custom_call_target="tpu_custom_call" | custom-call | flops 1 | bytes 1 | tf_op jit(solution)/shard_map/attend11/pallas_call | solution.py:145
  28.9 1.1 %attend01.1.mine_ref.refs_1_ = bf16[256,256]{1,0:T(8,128)(2,1)S(1)} custom-call(bf16[256,1024]{1,0:T(8,128)(2,1)S(1)} %get-tuple-element.64.normed_ref, bf16[1024,3072]{1,0:T(8,128)(2,1)S(1)} %get-tuple-element.58.wqkv_ref, s32[1,2]{1,0:T(1,128)S(1)} %copy-done.2), custom_call_target="tpu_custom_call" | custom-call | flops 1 | bytes 1 | tf_op jit(solution)/shard_map/attend01/pallas_call | solution.py:145
  30.1 1.1 %attend10.1.refs_2_ = bf16[256,256]{1,0:T(8,128)(2,1)S(1)} custom-call(bf16[256,1024]{1,0:T(8,128)(2,1)S(1)} %get-tuple-element.64.normed_ref, bf16[1024,3072]{1,0:T(8,128)(2,1)S(1)} %get-tuple-element.58.wqkv_ref, s32[1,2]{1,0:T(1,128)S(1)} %copy-done.2), custom_call_target="tpu_custom_call" | custom-call | flops 1 | bytes 1 | tf_op jit(solution)/shard_map/attend10/pallas_call | solution.py:145
  31.2 1.4 %collective-permute-start.10 = (bf16[256,256]{1,0:T(8,128)(2,1)S(1)}, bf16[256,256]{1,0:T(8,128)(2,1)S(1)}, u32[]{:S(2)}, u32[]{:S(2)}) collective-permute-start(bf16[256,256]{1,0:T(8,128)(2,1)S(1)} %attend10.1.refs_2_), channel_id=1, source_target_pairs={{0,1},{1,0},{2,3},{3,2},{4,5},{5,4},{6,7},{7,6},{8,9},{9,8},{10,11... | collective-permute-start | bytes 393224 | tf_op jit(solution)/shard_map/ppermute | solution.py:33
  34.2 1.1 %attend00.1.refs_3_.mine_ref = bf16[256,256]{1,0:T(8,128)(2,1)S(1)} custom-call(bf16[256,1024]{1,0:T(8,128)(2,1)S(1)} %get-tuple-element.64.normed_ref, bf16[1024,3072]{1,0:T(8,128)(2,1)S(1)} %get-tuple-element.58.wqkv_ref, s32[1,2]{1,0:T(1,128)S(1)} %copy-done.2), custom_call_target="tpu_custom_call" | custom-call | flops 10000000000 | bytes 1 | tf_op jit(solution)/shard_map/attend00/pallas_call | solution.py:145
  35.8 1.6 %collective-permute-start.12 = (bf16[1,256,256]{2,1,0:T(8,128)(2,1)S(1)}, bf16[1,256,256]{2,1,0:T(8,128)(2,1)S(1)}, u32[]{:S(2)}, u32[]{:S(2)}) collective-permute-start(bf16[1,256,256]{2,1,0:T(8,128)(2,1)S(1)} %slice.51), channel_id=1, source_target_pairs={{0,16},{8,24},{16,0},{24,8},{1,17},{9,25},{17,1},{25,9},{2,18},{10... | collective-permute-start | bytes 393224 | tf_op jit(solution)/shard_map/ppermute | solution.py:33
  37.9 1.5 %project.1 = bf16[1,2,8,16,1024]{4,3,2,1,0:T(8,128)(2,1)} custom-call(bf16[256,1024]{1,0:T(8,128)(2,1)S(1)} %get-tuple-element.66.reg_ref, bf16[1024,1024]{1,0:T(8,128)(2,1)S(1)} %get-tuple-element.67.wout_ref, bf16[256,256]{1,0:T(8,128)(2,1)S(1)} %attend11.1.refs_0_, bf16[256,256]{1,0:T(8,128)(2,1)S(1)} %attend01.1.mine_ref.refs_1_, ...), custom_call_target="tpu_custom_call" | custom-call | flops 10000000000 | bytes 1 | tf_op jit(solution)/shard_map/project/pallas_call | solution.py:145
  40.2 1.2 %collective-permute-done.12 = bf16[1,256,256]{2,1,0:T(8,128)(2,1)S(1)} collective-permute-done((bf16[1,256,256]{2,1,0:T(8,128)(2,1)S(1)}, bf16[1,256,256]{2,1,0:T(8,128)(2,1)S(1)}, u32[]{:S(2)}, u32[]{:S(2)}) %collective-permute-start.12) | collective-permute-done | bytes 131104 | tf_op jit(solution)/shard_map/ppermute | solution.py:33
  41.4 2.0 %collective-permute-start.14 = (bf16[1,256,128]{2,1,0:T(8,128)(2,1)S(1)}, bf16[1,256,128]{2,1,0:T(8,128)(2,1)S(1)}, u32[]{:S(2)}, u32[]{:S(2)}) collective-permute-start(bf16[1,256,128]{2,1,0:T(8,128)(2,1)S(1)} %get-tuple-element.75), channel_id=1, source_target_pairs={{0,4},{2,6},{4,0},{6,2},{1,5},{3,7},{5,1},{7,3},{8,12},{10,14},{12... | collective-permute-start | bytes 196616 | tf_op jit(solution)/shard_map/ppermute | solution.py:28
  43.8 1.6 %collective-permute-done.15 = bf16[1,256,256]{2,1,0:T(8,128)(2,1)S(1)} collective-permute-done((bf16[1,256,256]{2,1,0:T(8,128)(2,1)S(1)}, bf16[1,256,256]{2,1,0:T(8,128)(2,1)S(1)}, u32[]{:S(2)}, u32[]{:S(2)}) %collective-permute-start.15) | collective-permute-done | bytes 131104 | tf_op jit(solution)/shard_map/ppermute | solution.py:33
  45.5 1.9 %collective-permute-start.16 = (bf16[1,256,128]{2,1,0:T(8,128)(2,1)S(1)}, bf16[1,256,128]{2,1,0:T(8,128)(2,1)S(1)}, u32[]{:S(2)}, u32[]{:S(2)}) collective-permute-start(bf16[1,256,128]{2,1,0:T(8,128)(2,1)S(1)} %slice.52), channel_id=1, source_target_pairs={{0,6},{2,0},{4,2},{6,4},{1,7},{3,1},{5,3},{7,5},{8,14},{10,8},{12,... | collective-permute-start | bytes 196616 | tf_op jit(solution)/shard_map/ppermute | solution.py:28
  47.3 2.4 %collective-permute-done.13 = bf16[1,256,128]{2,1,0:T(8,128)(2,1)S(1)} collective-permute-done((bf16[1,256,128]{2,1,0:T(8,128)(2,1)S(1)}, bf16[1,256,128]{2,1,0:T(8,128)(2,1)S(1)}, u32[]{:S(2)}, u32[]{:S(2)}) %collective-permute-start.13) | collective-permute-done | bytes 65568 | tf_op jit(solution)/shard_map/ppermute | solution.py:28
  (50 shorter events, 6.9 us)
Async XLA Ops:
  0.6 0.8 %copy-start.3 = (s32[64]{0:T(128)S(1)}, s32[64]{0:T(128)}, u32[]{:S(2)}) copy-start(s32[64]{0:T(128)} %param.16) | copy-start | bytes 772
  0.6 0.8 %copy-start.4 = (s32[64,1]{0,1:T(1,128)S(1)}, s32[64,1]{0,1:T(1,128)}, u32[]{:S(2)}) copy-start(s32[64,1]{0,1:T(1,128)} %param.15) | copy-start | bytes 772
  0.7 0.9 %copy-start.1 = (bf16[64,1024]{1,0:T(8,128)(2,1)S(1)}, bf16[64,1024]{1,0:T(8,128)(2,1)}, u32[]{:S(2)}) copy-start(bf16[64,1024]{1,0:T(8,128)(2,1)} %vec_ref.1) | copy-start | bytes 393220
  0.7 8.4 %copy-start.2 = (s32[1,2]{1,0:T(1,128)S(1)}, s32[1,2]{1,0:T(1,128)}, u32[]{:S(2)}) copy-start(s32[1,2]{1,0:T(1,128)} %shift_ref.4) | copy-start | bytes 28
  0.7 13.0 %copy-start = (bf16[1,2,8,16,1024]{4,3,2,1,0:T(8,128)(2,1)S(1)}, bf16[1,2,8,16,1024]{4,3,2,1,0:T(8,128)(2,1)}, u32[]{:S(2)}) copy-start(bf16[1,2,8,16,1024]{4,3,2,1,0:T(8,128)(2,1)} %cot_ref.1) | copy-start | bytes 1572868
  2.0 8.1 %collective-permute-start = (bf16[16,1664]{1,0:T(8,128)(2,1)S(1)}, bf16[16,1664]{1,0:T(8,128)(2,1)S(1)}, u32[]{:S(2)}, u32[]{:S(2)}) collective-permute-start(bf16[16,1664]{1,0:T(8,128)(2,1)S(1)} %get-tuple-element.45), channel_id=1, source_target_pairs={{0,2},{2,4},{4,6},{6,0},{1,3},{3,5},{5,7},{7,1},{8,10},{10,12},{12... | collective-permute-start | bytes 159752 | tf_op jit(solution)/shard_map/ppermute | solution.py:28
  5.1 6.4 %collective-permute-start.1 = (bf16[16,1664]{1,0:T(8,128)(2,1)S(1)}, bf16[16,1664]{1,0:T(8,128)(2,1)S(1)}, u32[]{:S(2)}, u32[]{:S(2)}) collective-permute-start(bf16[16,1664]{1,0:T(8,128)(2,1)S(1)} %get-tuple-element.46), channel_id=1, source_target_pairs={{0,4},{2,6},{4,0},{6,2},{1,5},{3,7},{5,1},{7,3},{8,12},{10,14},{12... | collective-permute-start | bytes 159752 | tf_op jit(solution)/shard_map/ppermute | solution.py:28
  7.7 4.3 %collective-permute-start.2 = (bf16[16,1664]{1,0:T(8,128)(2,1)S(1)}, bf16[16,1664]{1,0:T(8,128)(2,1)S(1)}, u32[]{:S(2)}, u32[]{:S(2)}) collective-permute-start(bf16[16,1664]{1,0:T(8,128)(2,1)S(1)} %get-tuple-element.47), channel_id=1, source_target_pairs={{0,6},{2,0},{4,2},{6,4},{1,7},{3,1},{5,3},{7,5},{8,14},{10,8},{12,... | collective-permute-start | bytes 159752 | tf_op jit(solution)/shard_map/ppermute | solution.py:28
  12.4 8.5 %collective-permute-start.3 = (bf16[112,1024]{1,0:T(8,128)(2,1)S(1)}, bf16[112,1024]{1,0:T(8,128)(2,1)S(1)}, u32[]{:S(2)}, u32[]{:S(2)}) collective-permute-start(bf16[112,1024]{1,0:T(8,128)(2,1)S(1)} %get-tuple-element.48), channel_id=1, source_target_pairs={{2,0},{4,2},{6,4},{3,1},{5,3},{7,5},{10,8},{12,10},{14,12},{11,9},... | collective-permute-start | bytes 688136 | tf_op jit(solution)/shard_map/ppermute | solution.py:23
  13.7 19.0 %collective-permute-start.7 = (bf16[1,2,8,16,1024]{4,3,2,1,0:T(8,128)(2,1)S(1)}, bf16[1,2,8,16,1024]{4,3,2,1,0:T(8,128)(2,1)S(1)}, u32[]{:S(2)}, u32[]{:S(2)}) collective-permute-start(bf16[1,2,8,16,1024]{4,3,2,1,0:T(8,128)(2,1)S(1)} %copy-done), channel_id=1, source_target_pairs={{0,1},{1,0},{2,3},{3,2},{4,5},{5,4},{6,7},{7,6},{8,9},{9,8},{10,11... | collective-permute-start | bytes 1572872 | tf_op jit(solution)/shard_map/ppermute | solution.py:33
  15.4 10.8 %collective-permute-start.5 = (bf16[128,1024]{1,0:T(8,128)(2,1)S(1)}, bf16[128,1024]{1,0:T(8,128)(2,1)S(1)}, u32[]{:S(2)}, u32[]{:S(2)}) collective-permute-start(bf16[128,1024]{1,0:T(8,128)(2,1)S(1)} %get-tuple-element.55), channel_id=1, source_target_pairs={{0,24},{8,0},{16,8},{24,16},{1,25},{9,1},{17,9},{25,17},{2,26},{10... | collective-permute-start | bytes 786440 | tf_op jit(solution)/shard_map/ppermute | solution.py:28
  15.4 10.8 %collective-permute-start.4 = (bf16[112,1024]{1,0:T(8,128)(2,1)S(1)}, bf16[112,1024]{1,0:T(8,128)(2,1)S(1)}, u32[]{:S(2)}, u32[]{:S(2)}) collective-permute-start(bf16[112,1024]{1,0:T(8,128)(2,1)S(1)} %get-tuple-element.54), channel_id=1, source_target_pairs={{2,0},{4,2},{6,4},{3,1},{5,3},{7,5},{10,8},{12,10},{14,12},{11,9},... | collective-permute-start | bytes 688136 | tf_op jit(solution)/shard_map/ppermute | solution.py:23
  20.9 5.4 %collective-permute-start.6 = (bf16[112,1024]{1,0:T(8,128)(2,1)S(1)}, bf16[112,1024]{1,0:T(8,128)(2,1)S(1)}, u32[]{:S(2)}, u32[]{:S(2)}) collective-permute-start(bf16[112,1024]{1,0:T(8,128)(2,1)S(1)} %collective-permute-done.3.refs_1_), channel_id=1, source_target_pairs={{0,24},{8,0},{16,8},{24,16},{1,25},{9,1},{17,9},{25,17},{2,26},{10... | collective-permute-start | bytes 688136 | tf_op jit(solution)/shard_map/ppermute | solution.py:28
  28.2 5.4 %collective-permute-start.8 = (bf16[256,256]{1,0:T(8,128)(2,1)S(1)}, bf16[256,256]{1,0:T(8,128)(2,1)S(1)}, u32[]{:S(2)}, u32[]{:S(2)}) collective-permute-start(bf16[256,256]{1,0:T(8,128)(2,1)S(1)} %attend11.1.refs_0_), channel_id=1, source_target_pairs={{0,1},{1,0},{2,3},{3,2},{4,5},{5,4},{6,7},{7,6},{8,9},{9,8},{10,11... | collective-permute-start | bytes 393224 | tf_op jit(solution)/shard_map/ppermute | solution.py:33
  31.2 6.1 %collective-permute-start.10 = (bf16[256,256]{1,0:T(8,128)(2,1)S(1)}, bf16[256,256]{1,0:T(8,128)(2,1)S(1)}, u32[]{:S(2)}, u32[]{:S(2)}) collective-permute-start(bf16[256,256]{1,0:T(8,128)(2,1)S(1)} %attend10.1.refs_2_), channel_id=1, source_target_pairs={{0,1},{1,0},{2,3},{3,2},{4,5},{5,4},{6,7},{7,6},{8,9},{9,8},{10,11... | collective-permute-start | bytes 393224 | tf_op jit(solution)/shard_map/ppermute | solution.py:33
  34.1 1.6 %collective-permute-start.9 = (bf16[2,256,256]{2,1,0:T(8,128)(2,1)S(1)}, bf16[2,256,256]{2,1,0:T(8,128)(2,1)S(1)}, u32[]{:S(2)}, u32[]{:S(2)}) collective-permute-start(bf16[2,256,256]{2,1,0:T(8,128)(2,1)S(1)} %get-tuple-element.63), channel_id=1, source_target_pairs={{0,8},{8,0},{16,24},{24,16},{1,9},{9,1},{17,25},{25,17},{2,10},{10... | collective-permute-start | bytes 786440 | tf_op jit(solution)/shard_map/ppermute | solution.py:33
  35.7 2.0 %copy-start.5 = (f32[2,256,256]{2,1,0:T(8,128)}, f32[2,256,256]{2,1,0:T(8,128)S(1)}, u32[]{:S(2)}) copy-start(f32[2,256,256]{2,1,0:T(8,128)S(1)} %convert_add_fusion.1) | copy-start | bytes 1572868
  35.8 5.6 %collective-permute-start.12 = (bf16[1,256,256]{2,1,0:T(8,128)(2,1)S(1)}, bf16[1,256,256]{2,1,0:T(8,128)(2,1)S(1)}, u32[]{:S(2)}, u32[]{:S(2)}) collective-permute-start(bf16[1,256,256]{2,1,0:T(8,128)(2,1)S(1)} %slice.51), channel_id=1, source_target_pairs={{0,16},{8,24},{16,0},{24,8},{1,17},{9,25},{17,1},{25,9},{2,18},{10... | collective-permute-start | bytes 393224 | tf_op jit(solution)/shard_map/ppermute | solution.py:33
  37.8 1.6 %collective-permute-start.11 = (bf16[2,256,256]{2,1,0:T(8,128)(2,1)S(1)}, bf16[2,256,256]{2,1,0:T(8,128)(2,1)S(1)}, u32[]{:S(2)}, u32[]{:S(2)}) collective-permute-start(bf16[2,256,256]{2,1,0:T(8,128)(2,1)S(1)} %get-tuple-element.70), channel_id=1, source_target_pairs={{0,8},{8,0},{16,24},{24,16},{1,9},{9,1},{17,25},{25,17},{2,10},{10... | collective-permute-start | bytes 786440 | tf_op jit(solution)/shard_map/ppermute | solution.py:33
  37.8 3.5 %slice-start = ((f32[2,256,256]{2,1,0:T(8,128)}), f32[1,256,256]{2,1,0:T(8,128)S(1)}, s32[]{:S(2)}) async-start(f32[2,256,256]{2,1,0:T(8,128)} %copy-done.5), calls=%async_computation | async-start | bytes 524288 | tf_op jit(solution)/shard_map/slice | solution.py:487
  39.5 5.9 %collective-permute-start.15 = (bf16[1,256,256]{2,1,0:T(8,128)(2,1)S(1)}, bf16[1,256,256]{2,1,0:T(8,128)(2,1)S(1)}, u32[]{:S(2)}, u32[]{:S(2)}) collective-permute-start(bf16[1,256,256]{2,1,0:T(8,128)(2,1)S(1)} %slice.50), channel_id=1, source_target_pairs={{0,16},{8,24},{16,0},{24,8},{1,17},{9,25},{17,1},{25,9},{2,18},{10... | collective-permute-start | bytes 393224 | tf_op jit(solution)/shard_map/ppermute | solution.py:33
  41.4 5.9 %collective-permute-start.14 = (bf16[1,256,128]{2,1,0:T(8,128)(2,1)S(1)}, bf16[1,256,128]{2,1,0:T(8,128)(2,1)S(1)}, u32[]{:S(2)}, u32[]{:S(2)}) collective-permute-start(bf16[1,256,128]{2,1,0:T(8,128)(2,1)S(1)} %get-tuple-element.75), channel_id=1, source_target_pairs={{0,4},{2,6},{4,0},{6,2},{1,5},{3,7},{5,1},{7,3},{8,12},{10,14},{12... | collective-permute-start | bytes 196616 | tf_op jit(solution)/shard_map/ppermute | solution.py:28
  43.4 6.4 %collective-permute-start.13 = (bf16[1,256,128]{2,1,0:T(8,128)(2,1)S(1)}, bf16[1,256,128]{2,1,0:T(8,128)(2,1)S(1)}, u32[]{:S(2)}, u32[]{:S(2)}) collective-permute-start(bf16[1,256,128]{2,1,0:T(8,128)(2,1)S(1)} %get-tuple-element.74), channel_id=1, source_target_pairs={{0,2},{2,4},{4,6},{6,0},{1,3},{3,5},{5,7},{7,1},{8,10},{10,12},{12... | collective-permute-start | bytes 196616 | tf_op jit(solution)/shard_map/ppermute | solution.py:28
  45.5 4.7 %collective-permute-start.16 = (bf16[1,256,128]{2,1,0:T(8,128)(2,1)S(1)}, bf16[1,256,128]{2,1,0:T(8,128)(2,1)S(1)}, u32[]{:S(2)}, u32[]{:S(2)}) collective-permute-start(bf16[1,256,128]{2,1,0:T(8,128)(2,1)S(1)} %slice.52), channel_id=1, source_target_pairs={{0,6},{2,0},{4,2},{6,4},{1,7},{3,1},{5,3},{7,5},{8,14},{10,8},{12,... | collective-permute-start | bytes 196616 | tf_op jit(solution)/shard_map/ppermute | solution.py:28

commit v6 on v5

--- a/solution.py
+++ b/solution.py
@@ -234,6 +234,22 @@
     )
 
 
+def weights_body(groups, n_lat, n_dp, *refs):
+    (wqkv_hbm, wqkv_ref), sems = refs[0::3][:2], refs[-1]
+    width = wqkv_hbm.shape[0]
+    d_blk = width // (n_lat * n_dp)
+    pairs = [(refs[2], refs[5]), (refs[1], refs[4])]
+    to = 0
+    for part, turns in groups:
+        for third in range(3):
+            for k in turns:
+                at = pl.multiple_of(third * width + block_start(part, k, n_lat, n_dp, d_blk), d_blk)
+                pairs.append((wqkv_hbm.at[:, pl.ds(at, d_blk)], wqkv_ref.at[:, to : to + d_blk]))
+                to += d_blk
+    for copy in copy_all(pairs, sems):
+        copy.wait()
+
+
 def stage_body(sizes, shift_ref, tok_hbm, tok_ref, pick_ref, sem):
     copy = pltpu.make_async_copy(tok_hbm, tok_ref, sem)
     copy.start()
@@ -297,18 +313,14 @@
     return pl.multiple_of((lat * n_dp + dp) * d_blk, d_blk)
 
 
-def attend_body(part, turns, n_lat, n_dp, normed_ref, wqkv_ref, shift_ref, out_ref):
+def attend_body(group, turns, n_lat, n_dp, normed_ref, wqkv_ref, shift_ref, out_ref):
     n_rows, width = normed_ref.shape
     n_tok = n_rows // 2
     d_blk = width // (n_lat * n_dp)
-    starts = [block_start(part, k, n_lat, n_dp, d_blk) for k in turns]
-    normed = normed_ref[...]
-    thirds = []
-    for third in range(3):
-        weights = jnp.concatenate(
-            [wqkv_ref[:, pl.ds(third * width + at, d_blk)] for at in starts], axis=1
-        )
-        thirds.append(matmul(normed, weights))
+    part = len(turns) * d_blk
+    at = 3 * group * part
+    every = matmul(normed_ref[...], wqkv_ref[:, at : at + 3 * part])
+    thirds = [every[:, i * part : (i + 1) * part] for i in range(3)]
     scale = (d_blk // 2) ** (-0.5)
     queries = (thirds[0].astype(BF16).astype(F32) * scale).astype(BF16)
     keys, values = thirds[1].astype(BF16), thirds[2].astype(BF16)
@@ -451,7 +463,16 @@
     corner = shifted(north0, "lon", -1)
     loaded = (w_qkv, w_out, norm_gain.reshape(1, -1))
     loaded = lax.optimization_barrier((north0, *loaded))[1:]
-    w_qkv, w_out, gain = load(loaded, "weights")
+    first, second = [k for k in range(n_lat) if k % 3], [k for k in range(n_lat) if k % 3 == 0]
+    groups = [(1, first), (0, first), (1, second), (0, second)]
+    w_qkv, w_out, gain = call(
+        functools.partial(weights_body, groups, n_lat, n_dp),
+        [shape(array.shape, array.dtype) for array in loaded],
+        tuple(in_hbm(array) for array in loaded),
+        [ANY_SPEC] * 3,
+        "weights",
+        [dma((2 + 3 * n_lat * n_dp,))],
+    )
     region, normed = call(
         region_body,
         [shape((n_rows, d_model), BF16)] * 2,
@@ -463,7 +484,7 @@
 
     def attend(normed, part, turns):
         return call(
-            functools.partial(attend_body, part, turns, n_lat, n_dp),
+            functools.partial(attend_body, groups.index((part, turns)), turns, n_lat, n_dp),
             shape((n_rows, len(turns) * d_blk), BF16),
             (normed, w_qkv, shift_offsets),
             [VMEM_SPEC] * 3,

time: 51.1 us -> 51.2 us (level)
  no operation moved by 1% of the time
where the time goes in v6:
time: 51.2 us; the launch traced here: 51 us
  starting transfers between devices  20.4 us (40%)
  waiting for transfers between devices  14.3 us (28%)
  Pallas kernels  13.5 us (26%)
  between operations  1.65 us (3%)
  other arithmetic  0.86 us (2%)
    pallas_call x15, Pallas kernels, call(): pl.pallas_call(body, out_shape=out_shape, in_specs=specs, out_specs=jax.t...  13.5 us
    ppermute x8, starting transfers between devices, shifted(): lax.ppermute(array, axis, [(i, (i + by) % devices) for i in range(devices)])  11.6 us
    ppermute x7, starting transfers between devices, swapped(): return lax.ppermute(array, axis, [(i, i ^ bit) for i in range(devices)])  6.25 us
    ppermute x2, waiting for transfers between devices, from_behind(): return lax.ppermute(array, axis, pairs)  5.72 us
    ppermute x8, waiting for transfers between devices, shifted(): lax.ppermute(array, axis, [(i, (i + by) % devices) for i in range(devices)])  4.67 us
    ppermute x7, waiting for transfers between devices, swapped(): return lax.ppermute(array, axis, [(i, i ^ bit) for i in range(devices)])  3.92 us
    ppermute x2, starting transfers between devices, from_behind(): return lax.ppermute(array, axis, pairs)  2.57 us
  transfers between devices with their start and end apart: 17, of which 10 were waited for; matrix products, arithmetic and copies ran while one was open for 0% of the time, Pallas kernels for 25%

profile of v6, /device:TPU:0, one launch (start us, length us, event | category | flops | bytes accessed | tf_op | source)
XLA Modules:
  0.0 51.0 jit_solution(15998907574375269017)
XLA Ops:
  2.0 3.1 %collective-permute-start = (bf16[16,1664]{1,0:T(8,128)(2,1)S(1)}, bf16[16,1664]{1,0:T(8,128)(2,1)S(1)}, u32[]{:S(2)}, u32[]{:S(2)}) collective-permute-start(bf16[16,1664]{1,0:T(8,128)(2,1)S(1)} %get-tuple-element.45), channel_id=1, source_target_pairs={{0,2},{2,4},{4,6},{6,0},{1,3},{3,5},{5,7},{7,1},{8,10},{10,12},{12... | collective-permute-start | bytes 159752 | tf_op jit(solution)/shard_map/ppermute | solution.py:28
  5.1 2.6 %collective-permute-start.1 = (bf16[16,1664]{1,0:T(8,128)(2,1)S(1)}, bf16[16,1664]{1,0:T(8,128)(2,1)S(1)}, u32[]{:S(2)}, u32[]{:S(2)}) collective-permute-start(bf16[16,1664]{1,0:T(8,128)(2,1)S(1)} %get-tuple-element.46), channel_id=1, source_target_pairs={{0,4},{2,6},{4,0},{6,2},{1,5},{3,7},{5,1},{7,3},{8,12},{10,14},{12... | collective-permute-start | bytes 159752 | tf_op jit(solution)/shard_map/ppermute | solution.py:28
  7.7 1.3 %collective-permute-start.2 = (bf16[16,1664]{1,0:T(8,128)(2,1)S(1)}, bf16[16,1664]{1,0:T(8,128)(2,1)S(1)}, u32[]{:S(2)}, u32[]{:S(2)}) collective-permute-start(bf16[16,1664]{1,0:T(8,128)(2,1)S(1)} %get-tuple-element.47), channel_id=1, source_target_pairs={{0,6},{2,0},{4,2},{6,4},{1,7},{3,1},{5,3},{7,5},{8,14},{10,8},{12,... | collective-permute-start | bytes 159752 | tf_op jit(solution)/shard_map/ppermute | solution.py:28
  9.1 1.1 %stage.1 = (bf16[1,2,8,16,1024]{4,3,2,1,0:T(8,128)(2,1)S(1)}, bf16[256,720]{1,0:T(8,128)(2,1)S(1)}) custom-call(s32[1,2]{1,0:T(1,128)S(1)} %copy-done.2, bf16[1,2,8,16,1024]{4,3,2,1,0:T(8,128)(2,1)} %tok_hbm), custom_call_target="tpu_custom_call" | custom-call | flops 1 | bytes 1 | tf_op jit(solution)/shard_map/stage/pallas_call | solution.py:145
  10.1 1.4 %collective-permute-done.1.refs_2_ = bf16[16,1664]{1,0:T(8,128)(2,1)S(1)} collective-permute-done((bf16[16,1664]{1,0:T(8,128)(2,1)S(1)}, bf16[16,1664]{1,0:T(8,128)(2,1)S(1)}, u32[]{:S(2)}, u32[]{:S(2)}) %collective-permute-start.1) | collective-permute-done | bytes 53280 | tf_op jit(solution)/shard_map/ppermute | solution.py:28
  12.4 1.3 %collective-permute-start.3 = (bf16[112,1024]{1,0:T(8,128)(2,1)S(1)}, bf16[112,1024]{1,0:T(8,128)(2,1)S(1)}, u32[]{:S(2)}, u32[]{:S(2)}) collective-permute-start(bf16[112,1024]{1,0:T(8,128)(2,1)S(1)} %get-tuple-element.48), channel_id=1, source_target_pairs={{2,0},{4,2},{6,4},{3,1},{5,3},{7,5},{10,8},{12,10},{14,12},{11,9},... | collective-permute-start | bytes 688136 | tf_op jit(solution)/shard_map/ppermute | solution.py:23
  13.7 1.7 %collective-permute-start.7 = (bf16[1,2,8,16,1024]{4,3,2,1,0:T(8,128)(2,1)S(1)}, bf16[1,2,8,16,1024]{4,3,2,1,0:T(8,128)(2,1)S(1)}, u32[]{:S(2)}, u32[]{:S(2)}) collective-permute-start(bf16[1,2,8,16,1024]{4,3,2,1,0:T(8,128)(2,1)S(1)} %copy-done), channel_id=1, source_target_pairs={{0,1},{1,0},{2,3},{3,2},{4,5},{5,4},{6,7},{7,6},{8,9},{9,8},{10,11... | collective-permute-start | bytes 1572872 | tf_op jit(solution)/shard_map/ppermute | solution.py:33
  15.4 1.3 %collective-permute-start.4 = (bf16[112,1024]{1,0:T(8,128)(2,1)S(1)}, bf16[112,1024]{1,0:T(8,128)(2,1)S(1)}, u32[]{:S(2)}, u32[]{:S(2)}) collective-permute-start(bf16[112,1024]{1,0:T(8,128)(2,1)S(1)} %get-tuple-element.54), channel_id=1, source_target_pairs={{2,0},{4,2},{6,4},{3,1},{5,3},{7,5},{10,8},{12,10},{14,12},{11,9},... | collective-permute-start | bytes 688136 | tf_op jit(solution)/shard_map/ppermute | solution.py:23
  16.7 4.2 %collective-permute-done.3.refs_1_ = bf16[112,1024]{1,0:T(8,128)(2,1)S(1)} collective-permute-done((bf16[112,1024]{1,0:T(8,128)(2,1)S(1)}, bf16[112,1024]{1,0:T(8,128)(2,1)S(1)}, u32[]{:S(2)}, u32[]{:S(2)}) %collective-permute-start.3) | collective-permute-done | bytes 229408 | tf_op jit(solution)/shard_map/ppermute | solution.py:23
  20.9 3.8 %weights.1 = (bf16[1024,3072]{1,0:T(8,128)(2,1)S(1)}, bf16[1024,1024]{1,0:T(8,128)(2,1)S(1)}, f32[1,1024]{1,0:T(1,128)S(1)}) custom-call(bf16[1024,3072]{1,0:T(8,128)(2,1)} %refs_0_, bf16[1024,1024]{1,0:T(8,128)(2,1)} %refs_1_, f32[1,1024]{1,0:T(1,128)} %bitcast.7), custom_call_target="tpu_custom_call" | custom-call | flops 1 | bytes 1 | tf_op jit(solution)/shard_map/weights/pallas_call | solution.py:145
  24.7 1.6 %collective-permute-done.4.refs_2_ = bf16[112,1024]{1,0:T(8,128)(2,1)S(1)} collective-permute-done((bf16[112,1024]{1,0:T(8,128)(2,1)S(1)}, bf16[112,1024]{1,0:T(8,128)(2,1)S(1)}, u32[]{:S(2)}, u32[]{:S(2)}) %collective-permute-start.4) | collective-permute-done | bytes 229408 | tf_op jit(solution)/shard_map/ppermute | solution.py:23
  26.2 0.8 %region.1 = (bf16[256,1024]{1,0:T(8,128)(2,1)S(1)}, bf16[256,1024]{1,0:T(8,128)(2,1)S(1)}) custom-call(bf16[256,720]{1,0:T(8,128)(2,1)S(1)} %get-tuple-element.43.pick_ref, f32[1,1024]{1,0:T(1,128)S(1)} %get-tuple-element.52.gain_ref, bf16[256,1024]{1,0:T(8,128)(2,1)S(1)} %get-tuple-element.53.refs_0_, bf16[112,1024]{1,0:T(8,128)(2,1)S(1)} %collective-permute-done.3.refs_1_, ...), custom_call_target="tpu_custom_call" | custom-call | flops 1 | bytes 1 | tf_op jit(solution)/shard_map/region/pallas_call | solution.py:145
  27.1 1.0 %attend11.1.refs_0_ = bf16[256,256]{1,0:T(8,128)(2,1)S(1)} custom-call(bf16[256,1024]{1,0:T(8,128)(2,1)S(1)} %get-tuple-element.64.normed_ref, bf16[1024,3072]{1,0:T(8,128)(2,1)S(1)} %get-tuple-element.58.wqkv_ref, s32[1,2]{1,0:T(1,128)S(1)} %copy-done.2), custom_call_target="tpu_custom_call" | custom-call | flops 1 | bytes 1 | tf_op jit(solution)/shard_map/attend11/pallas_call | solution.py:145
  28.8 1.0 %attend01.1.mine_ref.refs_1_ = bf16[256,256]{1,0:T(8,128)(2,1)S(1)} custom-call(bf16[256,1024]{1,0:T(8,128)(2,1)S(1)} %get-tuple-element.64.normed_ref, bf16[1024,3072]{1,0:T(8,128)(2,1)S(1)} %get-tuple-element.58.wqkv_ref, s32[1,2]{1,0:T(1,128)S(1)} %copy-done.2), custom_call_target="tpu_custom_call" | custom-call | flops 1 | bytes 1 | tf_op jit(solution)/shard_map/attend01/pallas_call | solution.py:145
  29.9 1.0 %attend10.1.refs_2_ = bf16[256,256]{1,0:T(8,128)(2,1)S(1)} custom-call(bf16[256,1024]{1,0:T(8,128)(2,1)S(1)} %get-tuple-element.64.normed_ref, bf16[1024,3072]{1,0:T(8,128)(2,1)S(1)} %get-tuple-element.58.wqkv_ref, s32[1,2]{1,0:T(1,128)S(1)} %copy-done.2), custom_call_target="tpu_custom_call" | custom-call | flops 1 | bytes 1 | tf_op jit(solution)/shard_map/attend10/pallas_call | solution.py:145
  30.9 1.4 %collective-permute-start.10 = (bf16[256,256]{1,0:T(8,128)(2,1)S(1)}, bf16[256,256]{1,0:T(8,128)(2,1)S(1)}, u32[]{:S(2)}, u32[]{:S(2)}) collective-permute-start(bf16[256,256]{1,0:T(8,128)(2,1)S(1)} %attend10.1.refs_2_), channel_id=1, source_target_pairs={{0,1},{1,0},{2,3},{3,2},{4,5},{5,4},{6,7},{7,6},{8,9},{9,8},{10,11... | collective-permute-start | bytes 393224 | tf_op jit(solution)/shard_map/ppermute | solution.py:33
  34.0 1.0 %attend00.1.refs_3_.mine_ref = bf16[256,256]{1,0:T(8,128)(2,1)S(1)} custom-call(bf16[256,1024]{1,0:T(8,128)(2,1)S(1)} %get-tuple-element.64.normed_ref, bf16[1024,3072]{1,0:T(8,128)(2,1)S(1)} %get-tuple-element.58.wqkv_ref, s32[1,2]{1,0:T(1,128)S(1)} %copy-done.2), custom_call_target="tpu_custom_call" | custom-call | flops 10000000000 | bytes 1 | tf_op jit(solution)/shard_map/attend00/pallas_call | solution.py:145
  35.6 1.7 %collective-permute-start.12 = (bf16[1,256,256]{2,1,0:T(8,128)(2,1)S(1)}, bf16[1,256,256]{2,1,0:T(8,128)(2,1)S(1)}, u32[]{:S(2)}, u32[]{:S(2)}) collective-permute-start(bf16[1,256,256]{2,1,0:T(8,128)(2,1)S(1)} %slice.51), channel_id=1, source_target_pairs={{0,16},{8,24},{16,0},{24,8},{1,17},{9,25},{17,1},{25,9},{2,18},{10... | collective-permute-start | bytes 393224 | tf_op jit(solution)/shard_map/ppermute | solution.py:33
  37.9 1.5 %project.1 = bf16[1,2,8,16,1024]{4,3,2,1,0:T(8,128)(2,1)} custom-call(bf16[256,1024]{1,0:T(8,128)(2,1)S(1)} %get-tuple-element.66.reg_ref, bf16[1024,1024]{1,0:T(8,128)(2,1)S(1)} %get-tuple-element.67.wout_ref, bf16[256,256]{1,0:T(8,128)(2,1)S(1)} %attend11.1.refs_0_, bf16[256,256]{1,0:T(8,128)(2,1)S(1)} %attend01.1.mine_ref.refs_1_, ...), custom_call_target="tpu_custom_call" | custom-call | flops 10000000000 | bytes 1 | tf_op jit(solution)/shard_map/project/pallas_call | solution.py:145
  40.0 1.2 %collective-permute-done.12 = bf16[1,256,256]{2,1,0:T(8,128)(2,1)S(1)} collective-permute-done((bf16[1,256,256]{2,1,0:T(8,128)(2,1)S(1)}, bf16[1,256,256]{2,1,0:T(8,128)(2,1)S(1)}, u32[]{:S(2)}, u32[]{:S(2)}) %collective-permute-start.12) | collective-permute-done | bytes 131104 | tf_op jit(solution)/shard_map/ppermute | solution.py:33
  41.3 2.2 %collective-permute-start.14 = (bf16[1,256,128]{2,1,0:T(8,128)(2,1)S(1)}, bf16[1,256,128]{2,1,0:T(8,128)(2,1)S(1)}, u32[]{:S(2)}, u32[]{:S(2)}) collective-permute-start(bf16[1,256,128]{2,1,0:T(8,128)(2,1)S(1)} %get-tuple-element.75), channel_id=1, source_target_pairs={{0,4},{2,6},{4,0},{6,2},{1,5},{3,7},{5,1},{7,3},{8,12},{10,14},{12... | collective-permute-start | bytes 196616 | tf_op jit(solution)/shard_map/ppermute | solution.py:28
  43.9 1.5 %collective-permute-done.15 = bf16[1,256,256]{2,1,0:T(8,128)(2,1)S(1)} collective-permute-done((bf16[1,256,256]{2,1,0:T(8,128)(2,1)S(1)}, bf16[1,256,256]{2,1,0:T(8,128)(2,1)S(1)}, u32[]{:S(2)}, u32[]{:S(2)}) %collective-permute-start.15) | collective-permute-done | bytes 131104 | tf_op jit(solution)/shard_map/ppermute | solution.py:33
  45.5 2.0 %collective-permute-start.16 = (bf16[1,256,128]{2,1,0:T(8,128)(2,1)S(1)}, bf16[1,256,128]{2,1,0:T(8,128)(2,1)S(1)}, u32[]{:S(2)}, u32[]{:S(2)}) collective-permute-start(bf16[1,256,128]{2,1,0:T(8,128)(2,1)S(1)} %slice.52), channel_id=1, source_target_pairs={{0,6},{2,0},{4,2},{6,4},{1,7},{3,1},{5,3},{7,5},{8,14},{10,8},{12,... | collective-permute-start | bytes 196616 | tf_op jit(solution)/shard_map/ppermute | solution.py:28
  47.5 2.4 %collective-permute-done.13 = bf16[1,256,128]{2,1,0:T(8,128)(2,1)S(1)} collective-permute-done((bf16[1,256,128]{2,1,0:T(8,128)(2,1)S(1)}, bf16[1,256,128]{2,1,0:T(8,128)(2,1)S(1)}, u32[]{:S(2)}, u32[]{:S(2)}) %collective-permute-start.13) | collective-permute-done | bytes 65568 | tf_op jit(solution)/shard_map/ppermute | solution.py:28
  (50 shorter events, 7.1 us)
Async XLA Ops:
  0.6 0.8 %copy-start.3 = (s32[64]{0:T(128)S(1)}, s32[64]{0:T(128)}, u32[]{:S(2)}) copy-start(s32[64]{0:T(128)} %param.16) | copy-start | bytes 772
  0.6 0.8 %copy-start.4 = (s32[64,1]{0,1:T(1,128)S(1)}, s32[64,1]{0,1:T(1,128)}, u32[]{:S(2)}) copy-start(s32[64,1]{0,1:T(1,128)} %param.15) | copy-start | bytes 772
  0.7 0.9 %copy-start.1 = (bf16[64,1024]{1,0:T(8,128)(2,1)S(1)}, bf16[64,1024]{1,0:T(8,128)(2,1)}, u32[]{:S(2)}) copy-start(bf16[64,1024]{1,0:T(8,128)(2,1)} %vec_ref.1) | copy-start | bytes 393220
  0.7 8.4 %copy-start.2 = (s32[1,2]{1,0:T(1,128)S(1)}, s32[1,2]{1,0:T(1,128)}, u32[]{:S(2)}) copy-start(s32[1,2]{1,0:T(1,128)} %shift_ref.4) | copy-start | bytes 28
  0.7 13.0 %copy-start = (bf16[1,2,8,16,1024]{4,3,2,1,0:T(8,128)(2,1)S(1)}, bf16[1,2,8,16,1024]{4,3,2,1,0:T(8,128)(2,1)}, u32[]{:S(2)}) copy-start(bf16[1,2,8,16,1024]{4,3,2,1,0:T(8,128)(2,1)} %cot_ref.1) | copy-start | bytes 1572868
  2.0 8.1 %collective-permute-start = (bf16[16,1664]{1,0:T(8,128)(2,1)S(1)}, bf16[16,1664]{1,0:T(8,128)(2,1)S(1)}, u32[]{:S(2)}, u32[]{:S(2)}) collective-permute-start(bf16[16,1664]{1,0:T(8,128)(2,1)S(1)} %get-tuple-element.45), channel_id=1, source_target_pairs={{0,2},{2,4},{4,6},{6,0},{1,3},{3,5},{5,7},{7,1},{8,10},{10,12},{12... | collective-permute-start | bytes 159752 | tf_op jit(solution)/shard_map/ppermute | solution.py:28
  5.1 6.4 %collective-permute-start.1 = (bf16[16,1664]{1,0:T(8,128)(2,1)S(1)}, bf16[16,1664]{1,0:T(8,128)(2,1)S(1)}, u32[]{:S(2)}, u32[]{:S(2)}) collective-permute-start(bf16[16,1664]{1,0:T(8,128)(2,1)S(1)} %get-tuple-element.46), channel_id=1, source_target_pairs={{0,4},{2,6},{4,0},{6,2},{1,5},{3,7},{5,1},{7,3},{8,12},{10,14},{12... | collective-permute-start | bytes 159752 | tf_op jit(solution)/shard_map/ppermute | solution.py:28
  7.7 4.3 %collective-permute-start.2 = (bf16[16,1664]{1,0:T(8,128)(2,1)S(1)}, bf16[16,1664]{1,0:T(8,128)(2,1)S(1)}, u32[]{:S(2)}, u32[]{:S(2)}) collective-permute-start(bf16[16,1664]{1,0:T(8,128)(2,1)S(1)} %get-tuple-element.47), channel_id=1, source_target_pairs={{0,6},{2,0},{4,2},{6,4},{1,7},{3,1},{5,3},{7,5},{8,14},{10,8},{12,... | collective-permute-start | bytes 159752 | tf_op jit(solution)/shard_map/ppermute | solution.py:28
  12.4 8.5 %collective-permute-start.3 = (bf16[112,1024]{1,0:T(8,128)(2,1)S(1)}, bf16[112,1024]{1,0:T(8,128)(2,1)S(1)}, u32[]{:S(2)}, u32[]{:S(2)}) collective-permute-start(bf16[112,1024]{1,0:T(8,128)(2,1)S(1)} %get-tuple-element.48), channel_id=1, source_target_pairs={{2,0},{4,2},{6,4},{3,1},{5,3},{7,5},{10,8},{12,10},{14,12},{11,9},... | collective-permute-start | bytes 688136 | tf_op jit(solution)/shard_map/ppermute | solution.py:23
  13.7 18.6 %collective-permute-start.7 = (bf16[1,2,8,16,1024]{4,3,2,1,0:T(8,128)(2,1)S(1)}, bf16[1,2,8,16,1024]{4,3,2,1,0:T(8,128)(2,1)S(1)}, u32[]{:S(2)}, u32[]{:S(2)}) collective-permute-start(bf16[1,2,8,16,1024]{4,3,2,1,0:T(8,128)(2,1)S(1)} %copy-done), channel_id=1, source_target_pairs={{0,1},{1,0},{2,3},{3,2},{4,5},{5,4},{6,7},{7,6},{8,9},{9,8},{10,11... | collective-permute-start | bytes 1572872 | tf_op jit(solution)/shard_map/ppermute | solution.py:33
  15.4 10.8 %collective-permute-start.5 = (bf16[128,1024]{1,0:T(8,128)(2,1)S(1)}, bf16[128,1024]{1,0:T(8,128)(2,1)S(1)}, u32[]{:S(2)}, u32[]{:S(2)}) collective-permute-start(bf16[128,1024]{1,0:T(8,128)(2,1)S(1)} %get-tuple-element.55), channel_id=1, source_target_pairs={{0,24},{8,0},{16,8},{24,16},{1,25},{9,1},{17,9},{25,17},{2,26},{10... | collective-permute-start | bytes 786440 | tf_op jit(solution)/shard_map/ppermute | solution.py:28
  15.4 10.8 %collective-permute-start.4 = (bf16[112,1024]{1,0:T(8,128)(2,1)S(1)}, bf16[112,1024]{1,0:T(8,128)(2,1)S(1)}, u32[]{:S(2)}, u32[]{:S(2)}) collective-permute-start(bf16[112,1024]{1,0:T(8,128)(2,1)S(1)} %get-tuple-element.54), channel_id=1, source_target_pairs={{2,0},{4,2},{6,4},{3,1},{5,3},{7,5},{10,8},{12,10},{14,12},{11,9},... | collective-permute-start | bytes 688136 | tf_op jit(solution)/shard_map/ppermute | solution.py:23
  20.9 5.4 %collective-permute-start.6 = (bf16[112,1024]{1,0:T(8,128)(2,1)S(1)}, bf16[112,1024]{1,0:T(8,128)(2,1)S(1)}, u32[]{:S(2)}, u32[]{:S(2)}) collective-permute-start(bf16[112,1024]{1,0:T(8,128)(2,1)S(1)} %collective-permute-done.3.refs_1_), channel_id=1, source_target_pairs={{0,24},{8,0},{16,8},{24,16},{1,25},{9,1},{17,9},{25,17},{2,26},{10... | collective-permute-start | bytes 688136 | tf_op jit(solution)/shard_map/ppermute | solution.py:28
  28.1 5.4 %collective-permute-start.8 = (bf16[256,256]{1,0:T(8,128)(2,1)S(1)}, bf16[256,256]{1,0:T(8,128)(2,1)S(1)}, u32[]{:S(2)}, u32[]{:S(2)}) collective-permute-start(bf16[256,256]{1,0:T(8,128)(2,1)S(1)} %attend11.1.refs_0_), channel_id=1, source_target_pairs={{0,1},{1,0},{2,3},{3,2},{4,5},{5,4},{6,7},{7,6},{8,9},{9,8},{10,11... | collective-permute-start | bytes 393224 | tf_op jit(solution)/shard_map/ppermute | solution.py:33
  30.9 6.4 %collective-permute-start.10 = (bf16[256,256]{1,0:T(8,128)(2,1)S(1)}, bf16[256,256]{1,0:T(8,128)(2,1)S(1)}, u32[]{:S(2)}, u32[]{:S(2)}) collective-permute-start(bf16[256,256]{1,0:T(8,128)(2,1)S(1)} %attend10.1.refs_2_), channel_id=1, source_target_pairs={{0,1},{1,0},{2,3},{3,2},{4,5},{5,4},{6,7},{7,6},{8,9},{9,8},{10,11... | collective-permute-start | bytes 393224 | tf_op jit(solution)/shard_map/ppermute | solution.py:33
  33.9 1.6 %collective-permute-start.9 = (bf16[2,256,256]{2,1,0:T(8,128)(2,1)S(1)}, bf16[2,256,256]{2,1,0:T(8,128)(2,1)S(1)}, u32[]{:S(2)}, u32[]{:S(2)}) collective-permute-start(bf16[2,256,256]{2,1,0:T(8,128)(2,1)S(1)} %get-tuple-element.63), channel_id=1, source_target_pairs={{0,8},{8,0},{16,24},{24,16},{1,9},{9,1},{17,25},{25,17},{2,10},{10... | collective-permute-start | bytes 786440 | tf_op jit(solution)/shard_map/ppermute | solution.py:33
  35.6 2.2 %copy-start.5 = (f32[2,256,256]{2,1,0:T(8,128)}, f32[2,256,256]{2,1,0:T(8,128)S(1)}, u32[]{:S(2)}) copy-start(f32[2,256,256]{2,1,0:T(8,128)S(1)} %convert_add_fusion.1) | copy-start | bytes 1572868
  35.6 5.6 %collective-permute-start.12 = (bf16[1,256,256]{2,1,0:T(8,128)(2,1)S(1)}, bf16[1,256,256]{2,1,0:T(8,128)(2,1)S(1)}, u32[]{:S(2)}, u32[]{:S(2)}) collective-permute-start(bf16[1,256,256]{2,1,0:T(8,128)(2,1)S(1)} %slice.51), channel_id=1, source_target_pairs={{0,16},{8,24},{16,0},{24,8},{1,17},{9,25},{17,1},{25,9},{2,18},{10... | collective-permute-start | bytes 393224 | tf_op jit(solution)/shard_map/ppermute | solution.py:33
  37.8 1.6 %collective-permute-start.11 = (bf16[2,256,256]{2,1,0:T(8,128)(2,1)S(1)}, bf16[2,256,256]{2,1,0:T(8,128)(2,1)S(1)}, u32[]{:S(2)}, u32[]{:S(2)}) collective-permute-start(bf16[2,256,256]{2,1,0:T(8,128)(2,1)S(1)} %get-tuple-element.70), channel_id=1, source_target_pairs={{0,8},{8,0},{16,24},{24,16},{1,9},{9,1},{17,25},{25,17},{2,10},{10... | collective-permute-start | bytes 786440 | tf_op jit(solution)/shard_map/ppermute | solution.py:33
  37.9 3.4 %slice-start = ((f32[2,256,256]{2,1,0:T(8,128)}), f32[1,256,256]{2,1,0:T(8,128)S(1)}, s32[]{:S(2)}) async-start(f32[2,256,256]{2,1,0:T(8,128)} %copy-done.5), calls=%async_computation | async-start | bytes 524288 | tf_op jit(solution)/shard_map/slice | solution.py:508
  39.5 5.9 %collective-permute-start.15 = (bf16[1,256,256]{2,1,0:T(8,128)(2,1)S(1)}, bf16[1,256,256]{2,1,0:T(8,128)(2,1)S(1)}, u32[]{:S(2)}, u32[]{:S(2)}) collective-permute-start(bf16[1,256,256]{2,1,0:T(8,128)(2,1)S(1)} %slice.50), channel_id=1, source_target_pairs={{0,16},{8,24},{16,0},{24,8},{1,17},{9,25},{17,1},{25,9},{2,18},{10... | collective-permute-start | bytes 393224 | tf_op jit(solution)/shard_map/ppermute | solution.py:33
  41.3 6.2 %collective-permute-start.14 = (bf16[1,256,128]{2,1,0:T(8,128)(2,1)S(1)}, bf16[1,256,128]{2,1,0:T(8,128)(2,1)S(1)}, u32[]{:S(2)}, u32[]{:S(2)}) collective-permute-start(bf16[1,256,128]{2,1,0:T(8,128)(2,1)S(1)} %get-tuple-element.75), channel_id=1, source_target_pairs={{0,4},{2,6},{4,0},{6,2},{1,5},{3,7},{5,1},{7,3},{8,12},{10,14},{12... | collective-permute-start | bytes 196616 | tf_op jit(solution)/shard_map/ppermute | solution.py:28
  43.5 6.4 %collective-permute-start.13 = (bf16[1,256,128]{2,1,0:T(8,128)(2,1)S(1)}, bf16[1,256,128]{2,1,0:T(8,128)(2,1)S(1)}, u32[]{:S(2)}, u32[]{:S(2)}) collective-permute-start(bf16[1,256,128]{2,1,0:T(8,128)(2,1)S(1)} %get-tuple-element.74), channel_id=1, source_target_pairs={{0,2},{2,4},{4,6},{6,0},{1,3},{3,5},{5,7},{7,1},{8,10},{10,12},{12... | collective-permute-start | bytes 196616 | tf_op jit(solution)/shard_map/ppermute | solution.py:28
  45.5 4.8 %collective-permute-start.16 = (bf16[1,256,128]{2,1,0:T(8,128)(2,1)S(1)}, bf16[1,256,128]{2,1,0:T(8,128)(2,1)S(1)}, u32[]{:S(2)}, u32[]{:S(2)}) collective-permute-start(bf16[1,256,128]{2,1,0:T(8,128)(2,1)S(1)} %slice.52), channel_id=1, source_target_pairs={{0,6},{2,0},{4,2},{6,4},{1,7},{3,1},{5,3},{7,5},{8,14},{10,8},{12,... | collective-permute-start | bytes 196616 | tf_op jit(solution)/shard_map/ppermute | solution.py:28

commit v7 on v5

--- a/solution.py
+++ b/solution.py
@@ -459,7 +459,7 @@
         [VMEM_SPEC] * 7,
         "region",
     )
-    first, second = [k for k in range(n_lat) if k % 3], [k for k in range(n_lat) if k % 3 == 0]
+    first, second = [k for k in range(n_lat) if k % 3][::-1], [k for k in range(n_lat) if k % 3 == 0]
 
     def attend(normed, part, turns):
         return call(

time: 51.1 us -> 51 us (level)
  transfers between devices with their start and end apart: 17 -> 17, of which waited for: 10 -> 11; matrix products, arithmetic and copies ran while one was open for 0% -> 0% of each run, Pallas kernels for 25% -> 25%
where the time goes in v7:
time: 51 us; the launch traced here: 50.8 us
  starting transfers between devices  20 us (39%)
  waiting for transfers between devices  14.4 us (28%)
  Pallas kernels  13.6 us (27%)
  between operations  1.65 us (3%)
  other arithmetic  0.86 us (2%)
    pallas_call x15, Pallas kernels, call(): pl.pallas_call(body, out_shape=out_shape, in_specs=specs, out_specs=jax.t...  13.6 us
    ppermute x8, starting transfers between devices, shifted(): lax.ppermute(array, axis, [(i, (i + by) % devices) for i in range(devices)])  11.2 us
    ppermute x7, starting transfers between devices, swapped(): return lax.ppermute(array, axis, [(i, i ^ bit) for i in range(devices)])  6.28 us
    ppermute x2, waiting for transfers between devices, from_behind(): return lax.ppermute(array, axis, pairs)  6.07 us
    ppermute x8, waiting for transfers between devices, shifted(): lax.ppermute(array, axis, [(i, (i + by) % devices) for i in range(devices)])  4.67 us
    ppermute x7, waiting for transfers between devices, swapped(): return lax.ppermute(array, axis, [(i, i ^ bit) for i in range(devices)])  3.66 us
    ppermute x2, starting transfers between devices, from_behind(): return lax.ppermute(array, axis, pairs)  2.57 us
  transfers between devices with their start and end apart: 17, of which 11 were waited for; matrix products, arithmetic and copies ran while one was open for 0% of the time, Pallas kernels for 25%

profile of v7, /device:TPU:0, one launch (start us, length us, event | category | flops | bytes accessed | tf_op | source)
XLA Modules:
  0.0 50.8 jit_solution(12070057959331082313)
XLA Ops:
  2.0 3.1 %collective-permute-start = (bf16[16,1664]{1,0:T(8,128)(2,1)S(1)}, bf16[16,1664]{1,0:T(8,128)(2,1)S(1)}, u32[]{:S(2)}, u32[]{:S(2)}) collective-permute-start(bf16[16,1664]{1,0:T(8,128)(2,1)S(1)} %get-tuple-element.45), channel_id=1, source_target_pairs={{0,2},{2,4},{4,6},{6,0},{1,3},{3,5},{5,7},{7,1},{8,10},{10,12},{12... | collective-permute-start | bytes 159752 | tf_op jit(solution)/shard_map/ppermute | solution.py:28
  5.1 2.6 %collective-permute-start.1 = (bf16[16,1664]{1,0:T(8,128)(2,1)S(1)}, bf16[16,1664]{1,0:T(8,128)(2,1)S(1)}, u32[]{:S(2)}, u32[]{:S(2)}) collective-permute-start(bf16[16,1664]{1,0:T(8,128)(2,1)S(1)} %get-tuple-element.46), channel_id=1, source_target_pairs={{0,4},{2,6},{4,0},{6,2},{1,5},{3,7},{5,1},{7,3},{8,12},{10,14},{12... | collective-permute-start | bytes 159752 | tf_op jit(solution)/shard_map/ppermute | solution.py:28
  7.7 1.3 %collective-permute-start.2 = (bf16[16,1664]{1,0:T(8,128)(2,1)S(1)}, bf16[16,1664]{1,0:T(8,128)(2,1)S(1)}, u32[]{:S(2)}, u32[]{:S(2)}) collective-permute-start(bf16[16,1664]{1,0:T(8,128)(2,1)S(1)} %get-tuple-element.47), channel_id=1, source_target_pairs={{0,6},{2,0},{4,2},{6,4},{1,7},{3,1},{5,3},{7,5},{8,14},{10,8},{12,... | collective-permute-start | bytes 159752 | tf_op jit(solution)/shard_map/ppermute | solution.py:28
  9.1 1.1 %stage.1 = (bf16[1,2,8,16,1024]{4,3,2,1,0:T(8,128)(2,1)S(1)}, bf16[256,720]{1,0:T(8,128)(2,1)S(1)}) custom-call(s32[1,2]{1,0:T(1,128)S(1)} %copy-done.2, bf16[1,2,8,16,1024]{4,3,2,1,0:T(8,128)(2,1)} %tok_hbm), custom_call_target="tpu_custom_call" | custom-call | flops 1 | bytes 1 | tf_op jit(solution)/shard_map/stage/pallas_call | solution.py:145
  10.1 1.4 %collective-permute-done.1.refs_2_ = bf16[16,1664]{1,0:T(8,128)(2,1)S(1)} collective-permute-done((bf16[16,1664]{1,0:T(8,128)(2,1)S(1)}, bf16[16,1664]{1,0:T(8,128)(2,1)S(1)}, u32[]{:S(2)}, u32[]{:S(2)}) %collective-permute-start.1) | collective-permute-done | bytes 53280 | tf_op jit(solution)/shard_map/ppermute | solution.py:28
  12.4 1.3 %collective-permute-start.3 = (bf16[112,1024]{1,0:T(8,128)(2,1)S(1)}, bf16[112,1024]{1,0:T(8,128)(2,1)S(1)}, u32[]{:S(2)}, u32[]{:S(2)}) collective-permute-start(bf16[112,1024]{1,0:T(8,128)(2,1)S(1)} %get-tuple-element.48), channel_id=1, source_target_pairs={{2,0},{4,2},{6,4},{3,1},{5,3},{7,5},{10,8},{12,10},{14,12},{11,9},... | collective-permute-start | bytes 688136 | tf_op jit(solution)/shard_map/ppermute | solution.py:23
  13.7 1.7 %collective-permute-start.7 = (bf16[1,2,8,16,1024]{4,3,2,1,0:T(8,128)(2,1)S(1)}, bf16[1,2,8,16,1024]{4,3,2,1,0:T(8,128)(2,1)S(1)}, u32[]{:S(2)}, u32[]{:S(2)}) collective-permute-start(bf16[1,2,8,16,1024]{4,3,2,1,0:T(8,128)(2,1)S(1)} %copy-done), channel_id=1, source_target_pairs={{0,1},{1,0},{2,3},{3,2},{4,5},{5,4},{6,7},{7,6},{8,9},{9,8},{10,11... | collective-permute-start | bytes 1572872 | tf_op jit(solution)/shard_map/ppermute | solution.py:33
  15.4 1.3 %collective-permute-start.4 = (bf16[112,1024]{1,0:T(8,128)(2,1)S(1)}, bf16[112,1024]{1,0:T(8,128)(2,1)S(1)}, u32[]{:S(2)}, u32[]{:S(2)}) collective-permute-start(bf16[112,1024]{1,0:T(8,128)(2,1)S(1)} %get-tuple-element.54), channel_id=1, source_target_pairs={{2,0},{4,2},{6,4},{3,1},{5,3},{7,5},{10,8},{12,10},{14,12},{11,9},... | collective-permute-start | bytes 688136 | tf_op jit(solution)/shard_map/ppermute | solution.py:23
  16.7 4.2 %collective-permute-done.3.refs_1_ = bf16[112,1024]{1,0:T(8,128)(2,1)S(1)} collective-permute-done((bf16[112,1024]{1,0:T(8,128)(2,1)S(1)}, bf16[112,1024]{1,0:T(8,128)(2,1)S(1)}, u32[]{:S(2)}, u32[]{:S(2)}) %collective-permute-start.3) | collective-permute-done | bytes 229408 | tf_op jit(solution)/shard_map/ppermute | solution.py:23
  20.9 3.4 %weights.1 = (bf16[1024,3072]{1,0:T(8,128)(2,1)S(1)}, bf16[1024,1024]{1,0:T(8,128)(2,1)S(1)}, f32[1,1024]{1,0:T(1,128)S(1)}) custom-call(bf16[1024,3072]{1,0:T(8,128)(2,1)} %refs_0_, bf16[1024,1024]{1,0:T(8,128)(2,1)} %refs_1_, f32[1,1024]{1,0:T(1,128)} %bitcast.7), custom_call_target="tpu_custom_call" | custom-call | flops 1 | bytes 1 | tf_op jit(solution)/shard_map/weights/pallas_call | solution.py:145
  24.3 1.9 %collective-permute-done.4.refs_2_ = bf16[112,1024]{1,0:T(8,128)(2,1)S(1)} collective-permute-done((bf16[112,1024]{1,0:T(8,128)(2,1)S(1)}, bf16[112,1024]{1,0:T(8,128)(2,1)S(1)}, u32[]{:S(2)}, u32[]{:S(2)}) %collective-permute-start.4) | collective-permute-done | bytes 229408 | tf_op jit(solution)/shard_map/ppermute | solution.py:23
  26.2 0.8 %region.1 = (bf16[256,1024]{1,0:T(8,128)(2,1)S(1)}, bf16[256,1024]{1,0:T(8,128)(2,1)S(1)}) custom-call(bf16[256,720]{1,0:T(8,128)(2,1)S(1)} %get-tuple-element.43.pick_ref, f32[1,1024]{1,0:T(1,128)S(1)} %get-tuple-element.52.gain_ref, bf16[256,1024]{1,0:T(8,128)(2,1)S(1)} %get-tuple-element.53.refs_0_, bf16[112,1024]{1,0:T(8,128)(2,1)S(1)} %collective-permute-done.3.refs_1_, ...), custom_call_target="tpu_custom_call" | custom-call | flops 1 | bytes 1 | tf_op jit(solution)/shard_map/region/pallas_call | solution.py:145
  27.1 1.1 %attend12.1.refs_0_ = bf16[256,256]{1,0:T(8,128)(2,1)S(1)} custom-call(bf16[256,1024]{1,0:T(8,128)(2,1)S(1)} %get-tuple-element.64.normed_ref, bf16[1024,3072]{1,0:T(8,128)(2,1)S(1)} %get-tuple-element.58.wqkv_ref, s32[1,2]{1,0:T(1,128)S(1)} %copy-done.2), custom_call_target="tpu_custom_call" | custom-call | flops 1 | bytes 1 | tf_op jit(solution)/shard_map/attend12/pallas_call | solution.py:145
  28.9 1.1 %attend02.1.mine_ref.refs_1_ = bf16[256,256]{1,0:T(8,128)(2,1)S(1)} custom-call(bf16[256,1024]{1,0:T(8,128)(2,1)S(1)} %get-tuple-element.64.normed_ref, bf16[1024,3072]{1,0:T(8,128)(2,1)S(1)} %get-tuple-element.58.wqkv_ref, s32[1,2]{1,0:T(1,128)S(1)} %copy-done.2), custom_call_target="tpu_custom_call" | custom-call | flops 1 | bytes 1 | tf_op jit(solution)/shard_map/attend02/pallas_call | solution.py:145
  30.1 1.1 %attend10.1.refs_2_ = bf16[256,256]{1,0:T(8,128)(2,1)S(1)} custom-call(bf16[256,1024]{1,0:T(8,128)(2,1)S(1)} %get-tuple-element.64.normed_ref, bf16[1024,3072]{1,0:T(8,128)(2,1)S(1)} %get-tuple-element.58.wqkv_ref, s32[1,2]{1,0:T(1,128)S(1)} %copy-done.2), custom_call_target="tpu_custom_call" | custom-call | flops 1 | bytes 1 | tf_op jit(solution)/shard_map/attend10/pallas_call | solution.py:145
  31.2 1.5 %collective-permute-start.10 = (bf16[256,256]{1,0:T(8,128)(2,1)S(1)}, bf16[256,256]{1,0:T(8,128)(2,1)S(1)}, u32[]{:S(2)}, u32[]{:S(2)}) collective-permute-start(bf16[256,256]{1,0:T(8,128)(2,1)S(1)} %attend10.1.refs_2_), channel_id=1, source_target_pairs={{0,1},{1,0},{2,3},{3,2},{4,5},{5,4},{6,7},{7,6},{8,9},{9,8},{10,11... | collective-permute-start | bytes 393224 | tf_op jit(solution)/shard_map/ppermute | solution.py:33
  34.1 1.1 %attend00.1.refs_3_.mine_ref = bf16[256,256]{1,0:T(8,128)(2,1)S(1)} custom-call(bf16[256,1024]{1,0:T(8,128)(2,1)S(1)} %get-tuple-element.64.normed_ref, bf16[1024,3072]{1,0:T(8,128)(2,1)S(1)} %get-tuple-element.58.wqkv_ref, s32[1,2]{1,0:T(1,128)S(1)} %copy-done.2), custom_call_target="tpu_custom_call" | custom-call | flops 10000000000 | bytes 1 | tf_op jit(solution)/shard_map/attend00/pallas_call | solution.py:145
  35.8 1.6 %collective-permute-start.12 = (bf16[1,256,256]{2,1,0:T(8,128)(2,1)S(1)}, bf16[1,256,256]{2,1,0:T(8,128)(2,1)S(1)}, u32[]{:S(2)}, u32[]{:S(2)}) collective-permute-start(bf16[1,256,256]{2,1,0:T(8,128)(2,1)S(1)} %slice.51), channel_id=1, source_target_pairs={{0,16},{8,24},{16,0},{24,8},{1,17},{9,25},{17,1},{25,9},{2,18},{10... | collective-permute-start | bytes 393224 | tf_op jit(solution)/shard_map/ppermute | solution.py:33
  37.9 1.5 %project.1 = bf16[1,2,8,16,1024]{4,3,2,1,0:T(8,128)(2,1)} custom-call(bf16[256,1024]{1,0:T(8,128)(2,1)S(1)} %get-tuple-element.66.reg_ref, bf16[1024,1024]{1,0:T(8,128)(2,1)S(1)} %get-tuple-element.67.wout_ref, bf16[256,256]{1,0:T(8,128)(2,1)S(1)} %attend12.1.refs_0_, bf16[256,256]{1,0:T(8,128)(2,1)S(1)} %attend02.1.mine_ref.refs_1_, ...), custom_call_target="tpu_custom_call" | custom-call | flops 10000000000 | bytes 1 | tf_op jit(solution)/shard_map/project/pallas_call | solution.py:145
  40.2 1.2 %collective-permute-done.12 = bf16[1,256,256]{2,1,0:T(8,128)(2,1)S(1)} collective-permute-done((bf16[1,256,256]{2,1,0:T(8,128)(2,1)S(1)}, bf16[1,256,256]{2,1,0:T(8,128)(2,1)S(1)}, u32[]{:S(2)}, u32[]{:S(2)}) %collective-permute-start.12) | collective-permute-done | bytes 131104 | tf_op jit(solution)/shard_map/ppermute | solution.py:33
  41.4 1.6 %collective-permute-start.14 = (bf16[1,256,128]{2,1,0:T(8,128)(2,1)S(1)}, bf16[1,256,128]{2,1,0:T(8,128)(2,1)S(1)}, u32[]{:S(2)}, u32[]{:S(2)}) collective-permute-start(bf16[1,256,128]{2,1,0:T(8,128)(2,1)S(1)} %get-tuple-element.75), channel_id=1, source_target_pairs={{0,2},{2,4},{4,6},{6,0},{1,3},{3,5},{5,7},{7,1},{8,10},{10,12},{12... | collective-permute-start | bytes 196616 | tf_op jit(solution)/shard_map/ppermute | solution.py:28
  43.8 1.6 %collective-permute-done.15 = bf16[1,256,256]{2,1,0:T(8,128)(2,1)S(1)} collective-permute-done((bf16[1,256,256]{2,1,0:T(8,128)(2,1)S(1)}, bf16[1,256,256]{2,1,0:T(8,128)(2,1)S(1)}, u32[]{:S(2)}, u32[]{:S(2)}) %collective-permute-start.15) | collective-permute-done | bytes 131104 | tf_op jit(solution)/shard_map/ppermute | solution.py:33
  45.4 1.8 %collective-permute-start.16 = (bf16[1,256,128]{2,1,0:T(8,128)(2,1)S(1)}, bf16[1,256,128]{2,1,0:T(8,128)(2,1)S(1)}, u32[]{:S(2)}, u32[]{:S(2)}) collective-permute-start(bf16[1,256,128]{2,1,0:T(8,128)(2,1)S(1)} %slice.52), channel_id=1, source_target_pairs={{0,6},{2,0},{4,2},{6,4},{1,7},{3,1},{5,3},{7,5},{8,14},{10,8},{12,... | collective-permute-start | bytes 196616 | tf_op jit(solution)/shard_map/ppermute | solution.py:28
  47.5 2.1 %collective-permute-done.13 = bf16[1,256,128]{2,1,0:T(8,128)(2,1)S(1)} collective-permute-done((bf16[1,256,128]{2,1,0:T(8,128)(2,1)S(1)}, bf16[1,256,128]{2,1,0:T(8,128)(2,1)S(1)}, u32[]{:S(2)}, u32[]{:S(2)}) %collective-permute-start.13) | collective-permute-done | bytes 65568 | tf_op jit(solution)/shard_map/ppermute | solution.py:28
  (50 shorter events, 7.6 us)
Async XLA Ops:
  0.6 0.8 %copy-start.3 = (s32[64]{0:T(128)S(1)}, s32[64]{0:T(128)}, u32[]{:S(2)}) copy-start(s32[64]{0:T(128)} %param.16) | copy-start | bytes 772
  0.6 0.8 %copy-start.4 = (s32[64,1]{0,1:T(1,128)S(1)}, s32[64,1]{0,1:T(1,128)}, u32[]{:S(2)}) copy-start(s32[64,1]{0,1:T(1,128)} %param.15) | copy-start | bytes 772
  0.7 0.9 %copy-start.1 = (bf16[64,1024]{1,0:T(8,128)(2,1)S(1)}, bf16[64,1024]{1,0:T(8,128)(2,1)}, u32[]{:S(2)}) copy-start(bf16[64,1024]{1,0:T(8,128)(2,1)} %vec_ref.1) | copy-start | bytes 393220
  0.7 8.4 %copy-start.2 = (s32[1,2]{1,0:T(1,128)S(1)}, s32[1,2]{1,0:T(1,128)}, u32[]{:S(2)}) copy-start(s32[1,2]{1,0:T(1,128)} %shift_ref.4) | copy-start | bytes 28
  0.7 13.0 %copy-start = (bf16[1,2,8,16,1024]{4,3,2,1,0:T(8,128)(2,1)S(1)}, bf16[1,2,8,16,1024]{4,3,2,1,0:T(8,128)(2,1)}, u32[]{:S(2)}) copy-start(bf16[1,2,8,16,1024]{4,3,2,1,0:T(8,128)(2,1)} %cot_ref.1) | copy-start | bytes 1572868
  2.0 8.1 %collective-permute-start = (bf16[16,1664]{1,0:T(8,128)(2,1)S(1)}, bf16[16,1664]{1,0:T(8,128)(2,1)S(1)}, u32[]{:S(2)}, u32[]{:S(2)}) collective-permute-start(bf16[16,1664]{1,0:T(8,128)(2,1)S(1)} %get-tuple-element.45), channel_id=1, source_target_pairs={{0,2},{2,4},{4,6},{6,0},{1,3},{3,5},{5,7},{7,1},{8,10},{10,12},{12... | collective-permute-start | bytes 159752 | tf_op jit(solution)/shard_map/ppermute | solution.py:28
  5.1 6.4 %collective-permute-start.1 = (bf16[16,1664]{1,0:T(8,128)(2,1)S(1)}, bf16[16,1664]{1,0:T(8,128)(2,1)S(1)}, u32[]{:S(2)}, u32[]{:S(2)}) collective-permute-start(bf16[16,1664]{1,0:T(8,128)(2,1)S(1)} %get-tuple-element.46), channel_id=1, source_target_pairs={{0,4},{2,6},{4,0},{6,2},{1,5},{3,7},{5,1},{7,3},{8,12},{10,14},{12... | collective-permute-start | bytes 159752 | tf_op jit(solution)/shard_map/ppermute | solution.py:28
  7.7 4.3 %collective-permute-start.2 = (bf16[16,1664]{1,0:T(8,128)(2,1)S(1)}, bf16[16,1664]{1,0:T(8,128)(2,1)S(1)}, u32[]{:S(2)}, u32[]{:S(2)}) collective-permute-start(bf16[16,1664]{1,0:T(8,128)(2,1)S(1)} %get-tuple-element.47), channel_id=1, source_target_pairs={{0,6},{2,0},{4,2},{6,4},{1,7},{3,1},{5,3},{7,5},{8,14},{10,8},{12,... | collective-permute-start | bytes 159752 | tf_op jit(solution)/shard_map/ppermute | solution.py:28
  12.4 8.5 %collective-permute-start.3 = (bf16[112,1024]{1,0:T(8,128)(2,1)S(1)}, bf16[112,1024]{1,0:T(8,128)(2,1)S(1)}, u32[]{:S(2)}, u32[]{:S(2)}) collective-permute-start(bf16[112,1024]{1,0:T(8,128)(2,1)S(1)} %get-tuple-element.48), channel_id=1, source_target_pairs={{2,0},{4,2},{6,4},{3,1},{5,3},{7,5},{10,8},{12,10},{14,12},{11,9},... | collective-permute-start | bytes 688136 | tf_op jit(solution)/shard_map/ppermute | solution.py:23
  13.7 19.0 %collective-permute-start.7 = (bf16[1,2,8,16,1024]{4,3,2,1,0:T(8,128)(2,1)S(1)}, bf16[1,2,8,16,1024]{4,3,2,1,0:T(8,128)(2,1)S(1)}, u32[]{:S(2)}, u32[]{:S(2)}) collective-permute-start(bf16[1,2,8,16,1024]{4,3,2,1,0:T(8,128)(2,1)S(1)} %copy-done), channel_id=1, source_target_pairs={{0,1},{1,0},{2,3},{3,2},{4,5},{5,4},{6,7},{7,6},{8,9},{9,8},{10,11... | collective-permute-start | bytes 1572872 | tf_op jit(solution)/shard_map/ppermute | solution.py:33
  15.4 10.8 %collective-permute-start.5 = (bf16[128,1024]{1,0:T(8,128)(2,1)S(1)}, bf16[128,1024]{1,0:T(8,128)(2,1)S(1)}, u32[]{:S(2)}, u32[]{:S(2)}) collective-permute-start(bf16[128,1024]{1,0:T(8,128)(2,1)S(1)} %get-tuple-element.55), channel_id=1, source_target_pairs={{0,24},{8,0},{16,8},{24,16},{1,25},{9,1},{17,9},{25,17},{2,26},{10... | collective-permute-start | bytes 786440 | tf_op jit(solution)/shard_map/ppermute | solution.py:28
  15.4 10.8 %collective-permute-start.4 = (bf16[112,1024]{1,0:T(8,128)(2,1)S(1)}, bf16[112,1024]{1,0:T(8,128)(2,1)S(1)}, u32[]{:S(2)}, u32[]{:S(2)}) collective-permute-start(bf16[112,1024]{1,0:T(8,128)(2,1)S(1)} %get-tuple-element.54), channel_id=1, source_target_pairs={{2,0},{4,2},{6,4},{3,1},{5,3},{7,5},{10,8},{12,10},{14,12},{11,9},... | collective-permute-start | bytes 688136 | tf_op jit(solution)/shard_map/ppermute | solution.py:23
  20.9 5.4 %collective-permute-start.6 = (bf16[112,1024]{1,0:T(8,128)(2,1)S(1)}, bf16[112,1024]{1,0:T(8,128)(2,1)S(1)}, u32[]{:S(2)}, u32[]{:S(2)}) collective-permute-start(bf16[112,1024]{1,0:T(8,128)(2,1)S(1)} %collective-permute-done.3.refs_1_), channel_id=1, source_target_pairs={{0,24},{8,0},{16,8},{24,16},{1,25},{9,1},{17,9},{25,17},{2,26},{10... | collective-permute-start | bytes 688136 | tf_op jit(solution)/shard_map/ppermute | solution.py:28
  28.2 5.4 %collective-permute-start.8 = (bf16[256,256]{1,0:T(8,128)(2,1)S(1)}, bf16[256,256]{1,0:T(8,128)(2,1)S(1)}, u32[]{:S(2)}, u32[]{:S(2)}) collective-permute-start(bf16[256,256]{1,0:T(8,128)(2,1)S(1)} %attend12.1.refs_0_), channel_id=1, source_target_pairs={{0,1},{1,0},{2,3},{3,2},{4,5},{5,4},{6,7},{7,6},{8,9},{9,8},{10,11... | collective-permute-start | bytes 393224 | tf_op jit(solution)/shard_map/ppermute | solution.py:33
  31.2 6.1 %collective-permute-start.10 = (bf16[256,256]{1,0:T(8,128)(2,1)S(1)}, bf16[256,256]{1,0:T(8,128)(2,1)S(1)}, u32[]{:S(2)}, u32[]{:S(2)}) collective-permute-start(bf16[256,256]{1,0:T(8,128)(2,1)S(1)} %attend10.1.refs_2_), channel_id=1, source_target_pairs={{0,1},{1,0},{2,3},{3,2},{4,5},{5,4},{6,7},{7,6},{8,9},{9,8},{10,11... | collective-permute-start | bytes 393224 | tf_op jit(solution)/shard_map/ppermute | solution.py:33
  34.1 1.6 %collective-permute-start.9 = (bf16[2,256,256]{2,1,0:T(8,128)(2,1)S(1)}, bf16[2,256,256]{2,1,0:T(8,128)(2,1)S(1)}, u32[]{:S(2)}, u32[]{:S(2)}) collective-permute-start(bf16[2,256,256]{2,1,0:T(8,128)(2,1)S(1)} %get-tuple-element.63), channel_id=1, source_target_pairs={{0,8},{8,0},{16,24},{24,16},{1,9},{9,1},{17,25},{25,17},{2,10},{10... | collective-permute-start | bytes 786440 | tf_op jit(solution)/shard_map/ppermute | solution.py:33
  35.7 2.0 %copy-start.5 = (f32[2,256,256]{2,1,0:T(8,128)}, f32[2,256,256]{2,1,0:T(8,128)S(1)}, u32[]{:S(2)}) copy-start(f32[2,256,256]{2,1,0:T(8,128)S(1)} %convert_add_fusion.1) | copy-start | bytes 1572868
  35.8 5.6 %collective-permute-start.12 = (bf16[1,256,256]{2,1,0:T(8,128)(2,1)S(1)}, bf16[1,256,256]{2,1,0:T(8,128)(2,1)S(1)}, u32[]{:S(2)}, u32[]{:S(2)}) collective-permute-start(bf16[1,256,256]{2,1,0:T(8,128)(2,1)S(1)} %slice.51), channel_id=1, source_target_pairs={{0,16},{8,24},{16,0},{24,8},{1,17},{9,25},{17,1},{25,9},{2,18},{10... | collective-permute-start | bytes 393224 | tf_op jit(solution)/shard_map/ppermute | solution.py:33
  37.8 1.6 %collective-permute-start.11 = (bf16[2,256,256]{2,1,0:T(8,128)(2,1)S(1)}, bf16[2,256,256]{2,1,0:T(8,128)(2,1)S(1)}, u32[]{:S(2)}, u32[]{:S(2)}) collective-permute-start(bf16[2,256,256]{2,1,0:T(8,128)(2,1)S(1)} %get-tuple-element.70), channel_id=1, source_target_pairs={{0,8},{8,0},{16,24},{24,16},{1,9},{9,1},{17,25},{25,17},{2,10},{10... | collective-permute-start | bytes 786440 | tf_op jit(solution)/shard_map/ppermute | solution.py:33
  37.8 3.5 %slice-start = ((f32[2,256,256]{2,1,0:T(8,128)}), f32[1,256,256]{2,1,0:T(8,128)S(1)}, s32[]{:S(2)}) async-start(f32[2,256,256]{2,1,0:T(8,128)} %copy-done.5), calls=%async_computation | async-start | bytes 524288 | tf_op jit(solution)/shard_map/slice | solution.py:487
  39.5 5.9 %collective-permute-start.15 = (bf16[1,256,256]{2,1,0:T(8,128)(2,1)S(1)}, bf16[1,256,256]{2,1,0:T(8,128)(2,1)S(1)}, u32[]{:S(2)}, u32[]{:S(2)}) collective-permute-start(bf16[1,256,256]{2,1,0:T(8,128)(2,1)S(1)} %slice.50), channel_id=1, source_target_pairs={{0,16},{8,24},{16,0},{24,8},{1,17},{9,25},{17,1},{25,9},{2,18},{10... | collective-permute-start | bytes 393224 | tf_op jit(solution)/shard_map/ppermute | solution.py:33
  41.4 6.1 %collective-permute-start.14 = (bf16[1,256,128]{2,1,0:T(8,128)(2,1)S(1)}, bf16[1,256,128]{2,1,0:T(8,128)(2,1)S(1)}, u32[]{:S(2)}, u32[]{:S(2)}) collective-permute-start(bf16[1,256,128]{2,1,0:T(8,128)(2,1)S(1)} %get-tuple-element.75), channel_id=1, source_target_pairs={{0,2},{2,4},{4,6},{6,0},{1,3},{3,5},{5,7},{7,1},{8,10},{10,12},{12... | collective-permute-start | bytes 196616 | tf_op jit(solution)/shard_map/ppermute | solution.py:28
  43.0 6.6 %collective-permute-start.13 = (bf16[1,256,128]{2,1,0:T(8,128)(2,1)S(1)}, bf16[1,256,128]{2,1,0:T(8,128)(2,1)S(1)}, u32[]{:S(2)}, u32[]{:S(2)}) collective-permute-start(bf16[1,256,128]{2,1,0:T(8,128)(2,1)S(1)} %get-tuple-element.74), channel_id=1, source_target_pairs={{0,4},{2,6},{4,0},{6,2},{1,5},{3,7},{5,1},{7,3},{8,12},{10,14},{12... | collective-permute-start | bytes 196616 | tf_op jit(solution)/shard_map/ppermute | solution.py:28
  45.4 4.6 %collective-permute-start.16 = (bf16[1,256,128]{2,1,0:T(8,128)(2,1)S(1)}, bf16[1,256,128]{2,1,0:T(8,128)(2,1)S(1)}, u32[]{:S(2)}, u32[]{:S(2)}) collective-permute-start(bf16[1,256,128]{2,1,0:T(8,128)(2,1)S(1)} %slice.52), channel_id=1, source_target_pairs={{0,6},{2,0},{4,2},{6,4},{1,7},{3,1},{5,3},{7,5},{8,14},{10,8},{12,... | collective-permute-start | bytes 196616 | tf_op jit(solution)/shard_map/ppermute | solution.py:28
